TPU v7x, 32 devices: a whole 2x2x4 slice. The times are simulated.
32 devices in a mesh: section: 2 (over x), dp: 8 (over z, y), mp: 2 (over core).
Axes of the slice: x: 2, y: 2, z: 4, core: 2. Of those that a mesh axis runs over, the one named last changes fastest.
Arguments:
- inputs: bfloat16 [2, 2048, 1024], P(None, ('dp', 'mp')), may hold values from -6 to 6
- target_inputs: bfloat16 [2, 2048, 1024], P(None, ('dp', 'mp')), may hold values from -6 to 6
- cotangent: bfloat16 [2, 2048, 1024], P(None, ('dp', 'mp')), may hold values from -6 to 6
- slot_counts: int32 [2, 2], replicated, may hold values from 2 to 4
- w_qkv: bfloat16 [2, 3, 1024, 1024], P('section', None, None, 'mp'), may hold values from -0.1875 to 0.1875
- w_out: bfloat16 [2, 1024, 1024], P('section', None, 'mp'), may hold values from -0.75 to 0.75
- norm1_gain: float32 [2, 1024], P('section'), may hold values from 0.5 to 1.5
- norm1_bias: float32 [2, 1024], P('section'), may hold values from -1.2 to 1.2
- w_up: bfloat16 [2, 1024, 4096], P('section', None, 'mp'), may hold values from -0.1875 to 0.1875
- w_down: bfloat16 [2, 1024, 4096], P('section', None, 'mp'), may hold values from -0.125 to 0.125
- norm2_gain: float32 [2, 1024], P('section'), may hold values from 0.5 to 1.5
- norm2_bias: float32 [2, 1024], P('section'), may hold values from -1.2 to 1.2
- cross_qkv: bfloat16 [3, 1024, 1024], P(None, None, 'mp'), may hold values from -0.1875 to 0.1875
- cross_out: bfloat16 [1024, 1024], P(None, 'mp'), may hold values from -0.75 to 0.75
- norm3_gain: float32 [1024], replicated, may hold values from 0.5 to 1.5
- norm3_bias: float32 [1024], replicated, may hold values from -1.2 to 1.2
Outputs:
- segment_outputs: bfloat16 [2, 2, 2048, 1024], P('section', None, ('dp', 'mp'))
- input_grads: bfloat16 [2, 2, 2048, 1024], P('section', None, ('dp', 'mp'))
- grad_qkv: float32 [2, 3, 1024, 1024], P('section', None, 'dp', 'mp')
- grad_out: float32 [2, 1024, 1024], P('section', 'dp', 'mp')
- grad_norm1_gain: float32 [2, 1024], P('section', 'dp')
- grad_norm1_bias: float32 [2, 1024], P('section', 'dp')
- grad_up: float32 [2, 1024, 4096], P('section', 'dp', 'mp')
- grad_down: float32 [2, 1024, 4096], P('section', 'dp', 'mp')
- grad_norm2_gain: float32 [2, 1024], P('section', 'dp')
- grad_norm2_bias: float32 [2, 1024], P('section', 'dp')
- grad_cross_qkv: float32 [3, 1024, 1024], P(None, ('section', 'dp'), 'mp')
- grad_cross_out: float32 [1024, 1024], P(('section', 'dp'), 'mp')
- grad_norm3_gain: float32 [1024], P(('section', 'dp'))
- grad_norm3_bias: float32 [1024], P(('section', 'dp'))
All inputs are finite; a program needn't handle non-finite values.
Results may differ from a plain program's by a relative error of at most 0.029.
Values may be sent and summed in bfloat16 or wider, within the bound.
A program may use at most 256 MiB of HBM per device.

v0:
```python
import jax
import jax.numpy as jnp
from jax import lax
from jax.sharding import PartitionSpec as P

HEAD = 64
SLOT = 256
QSLOTS = 4


def from_behind(value, axis, steps):
    count = lax.axis_size(axis)
    leading, last = (max(0, -steps), min(count, count - steps))
    return lax.ppermute(value, axis, [(source, source + steps) for source in range(leading, last)])


def layer_norm(values, gain, bias_term):
    center = values - jnp.mean(values, -1, keepdims=True)
    spread = jnp.mean(center * center, -1, keepdims=True)
    return center * lax.rsqrt(spread + 1e-05) * gain + bias_term


def gelu_exact(values):
    return jax.nn.gelu(values, approximate=False)


def split_heads(block):
    count = block.shape[0] // SLOT
    return block.reshape(count, SLOT, block.shape[1] // HEAD, HEAD)


def attn_probs(queries, keys, causal):
    scores = jnp.einsum(
        "bqhd,bkhd->bhqk",
        split_heads(queries),
        split_heads(keys),
        preferred_element_type=jnp.float32,
    ) * HEAD ** (-0.5)
    if causal is not None:
        places = jnp.arange(SLOT, dtype=jnp.int32)
        allowed = (places[:, None] >= places[None, :]) | jnp.logical_not(causal)
        scores = jnp.where(allowed, scores, -1000000000.0)
    peak = jnp.max(scores, -1, keepdims=True)
    expo = jnp.exp(scores - peak)
    return expo / jnp.sum(expo, -1, keepdims=True)


def attend_forward(queries, keys, values, causal):
    weights = attn_probs(queries, keys, causal)
    context = jnp.einsum(
        "bhqk,bkhd->bqhd",
        weights.astype(jnp.bfloat16),
        split_heads(values),
        preferred_element_type=jnp.float32,
    )
    return context.reshape(queries.shape).astype(jnp.bfloat16)


def attend_backward(queries, keys, values, d_mixed, causal):
    weights = attn_probs(queries, keys, causal)
    shaped_d = split_heads(d_mixed)
    d_values = jnp.einsum(
        "bhqk,bqhd->bkhd",
        weights.astype(jnp.bfloat16),
        shaped_d,
        preferred_element_type=jnp.float32,
    )
    d_weights = jnp.einsum(
        "bqhd,bkhd->bhqk", shaped_d, split_heads(values), preferred_element_type=jnp.float32
    )
    d_scores = (weights * (d_weights - jnp.sum(weights * d_weights, -1, keepdims=True))).astype(
        jnp.bfloat16
    )
    scale = HEAD ** (-0.5)
    d_queries = (
        jnp.einsum(
            "bhqk,bkhd->bqhd", d_scores, split_heads(keys), preferred_element_type=jnp.float32
        )
        * scale
    )
    d_keys = (
        jnp.einsum(
            "bhqk,bqhd->bkhd", d_scores, split_heads(queries), preferred_element_type=jnp.float32
        )
        * scale
    )
    shape = queries.shape
    return (
        d_queries.reshape(shape).astype(jnp.bfloat16),
        d_keys.reshape(shape).astype(jnp.bfloat16),
        d_values.reshape(shape).astype(jnp.bfloat16),
    )


def own_rows(full, rows_dev):
    return lax.dynamic_slice_in_dim(full, lax.axis_index("mp") * rows_dev, rows_dev, 0)


def forward_segment(segment_input, memory, weights, cross_weights, decoder):
    w_qkv, w_out, gain_one, bias_one, w_up, w_down, gain_two, bias_two = weights
    cross_qkv, cross_out, gain_three, bias_three = cross_weights
    gathered, memory_whole = (
        lax.all_gather(segment_input, "mp", axis=0, tiled=True),
        lax.all_gather(memory, "mp", axis=0, tiled=True),
    )
    projected = jnp.einsum(
        "nd,tdc->tnc", gathered, w_qkv, preferred_element_type=jnp.float32
    ).astype(jnp.bfloat16)
    mixed = attend_forward(projected[0], projected[1], projected[2], decoder)
    branch = lax.psum(
        jnp.einsum("nc,dc->nd", mixed, w_out, preferred_element_type=jnp.float32).astype(
            jnp.bfloat16
        ),
        "mp",
    ).astype(jnp.float32)
    first_sum = gathered.astype(jnp.float32) + branch
    normed = layer_norm(first_sum, gain_one, bias_one)
    normed_low = normed.astype(jnp.bfloat16)
    cross_query = jnp.dot(normed_low, cross_qkv[0], preferred_element_type=jnp.float32).astype(
        jnp.bfloat16
    )
    cross_kv = jnp.einsum(
        "nd,tdc->tnc", memory_whole, cross_qkv[1:], preferred_element_type=jnp.float32
    ).astype(jnp.bfloat16)
    cross_mixed = attend_forward(cross_query, cross_kv[0], cross_kv[1], None)
    cross_branch = lax.psum(
        jnp.einsum("nc,dc->nd", cross_mixed, cross_out, preferred_element_type=jnp.float32).astype(
            jnp.bfloat16
        ),
        "mp",
    ).astype(jnp.float32)
    cross_input = normed + cross_branch
    crossed = jnp.where(decoder, layer_norm(cross_input, gain_three, bias_three), normed)
    crossed_low = crossed.astype(jnp.bfloat16)
    hidden_pre = jnp.dot(crossed_low, w_up, preferred_element_type=jnp.float32)
    activated = gelu_exact(hidden_pre).astype(jnp.bfloat16)
    ffn_branch = lax.psum(
        jnp.einsum("nf,df->nd", activated, w_down, preferred_element_type=jnp.float32).astype(
            jnp.bfloat16
        ),
        "mp",
    ).astype(jnp.float32)
    second_sum = crossed + ffn_branch
    result = layer_norm(second_sum, gain_two, bias_two)
    kept = (
        gathered,
        memory_whole,
        projected,
        mixed,
        first_sum,
        normed_low,
        cross_query,
        cross_kv,
        cross_mixed,
        cross_input,
        crossed_low,
        hidden_pre,
        second_sum,
    )
    return (own_rows(result, segment_input.shape[0]), kept)


def masked_add(totals, parts, valid):
    return tuple(
        (total + jnp.where(valid, part, jnp.zeros_like(part)) for total, part in zip(totals, parts))
    )


def backward_segment(grad_own, kept, weights, cross_weights, decoder, carry, cross_carry, valid):
    w_qkv, w_out, gain_one, bias_one, w_up, w_down, gain_two, bias_two = weights
    cross_qkv, cross_out, gain_three, bias_three = cross_weights
    (
        gathered,
        memory_whole,
        projected,
        mixed,
        first_sum,
        normed_low,
        cross_query,
        cross_kv,
        cross_mixed,
        cross_input,
        crossed_low,
        hidden_pre,
        second_sum,
    ) = kept
    rows_dev = grad_own.shape[0]
    d_rows = lax.all_gather(grad_own.astype(jnp.bfloat16), "mp", axis=0, tiled=True).astype(
        jnp.float32
    )
    unused, norm_two_back = jax.vjp(layer_norm, second_sum, gain_two, bias_two)
    d_second, d_gain_two, d_bias_two = norm_two_back(d_rows)
    d_branch = d_second.astype(jnp.bfloat16)
    d_active = jnp.einsum("nd,df->nf", d_branch, w_down, preferred_element_type=jnp.float32)
    activated, gelu_back = jax.vjp(gelu_exact, hidden_pre)
    d_hidden = gelu_back(d_active)[0].astype(jnp.bfloat16)
    grad_down = jnp.einsum(
        "nd,nf->df", d_branch, activated.astype(jnp.bfloat16), preferred_element_type=jnp.float32
    )
    grad_up = jnp.einsum("nd,nf->df", crossed_low, d_hidden, preferred_element_type=jnp.float32)
    feed = masked_add(carry[4:], (grad_up, grad_down, d_gain_two, d_bias_two), valid)
    d_crossed_part = jnp.einsum("nf,df->nd", d_hidden, w_up, preferred_element_type=jnp.float32)
    d_crossed = d_second + lax.psum(d_crossed_part.astype(jnp.bfloat16), "mp").astype(jnp.float32)
    unused_three, norm_three_back = jax.vjp(layer_norm, cross_input, gain_three, bias_three)
    d_cross_input, d_gain_three, d_bias_three = norm_three_back(d_crossed)
    d_cross_input = jnp.where(decoder, d_cross_input, jnp.zeros_like(d_cross_input))
    d_gain_three = jnp.where(decoder, d_gain_three, jnp.zeros_like(d_gain_three))
    d_bias_three = jnp.where(decoder, d_bias_three, jnp.zeros_like(d_bias_three))
    d_cross_branch = d_cross_input.astype(jnp.bfloat16)
    grad_cross_out = jnp.einsum(
        "nd,nc->dc", d_cross_branch, cross_mixed, preferred_element_type=jnp.float32
    )
    d_cross_mixed = jnp.einsum(
        "nd,dc->nc", d_cross_branch, cross_out, preferred_element_type=jnp.float32
    ).astype(jnp.bfloat16)
    d_cross_query, d_cross_keys, d_cross_values = attend_backward(
        cross_query, cross_kv[0], cross_kv[1], d_cross_mixed, None
    )
    d_cross_kv = jnp.stack([d_cross_keys, d_cross_values])
    grad_cross_query = jnp.einsum(
        "nd,nc->dc", normed_low, d_cross_query, preferred_element_type=jnp.float32
    )
    grad_cross_kv = jnp.einsum(
        "nd,tnc->tdc", memory_whole, d_cross_kv, preferred_element_type=jnp.float32
    )
    grad_cross_qkv = jnp.concatenate([grad_cross_query[None], grad_cross_kv], 0)
    d_normed_part = jnp.einsum(
        "nc,dc->nd", d_cross_query, cross_qkv[0], preferred_element_type=jnp.float32
    )
    d_memory_part = jnp.einsum(
        "tnc,tdc->nd", d_cross_kv, cross_qkv[1:], preferred_element_type=jnp.float32
    )
    d_normed_cross, d_memory = (
        lax.psum(d_normed_part.astype(jnp.bfloat16), "mp").astype(jnp.float32),
        lax.psum(d_memory_part.astype(jnp.bfloat16), "mp").astype(jnp.float32),
    )
    d_normed = jnp.where(decoder, d_cross_input + d_normed_cross, d_crossed)
    unused_one, norm_one_back = jax.vjp(layer_norm, first_sum, gain_one, bias_one)
    d_first, d_gain_one, d_bias_one = norm_one_back(d_normed)
    d_attn = d_first.astype(jnp.bfloat16)
    grad_out = jnp.einsum("nd,nc->dc", d_attn, mixed, preferred_element_type=jnp.float32)
    d_mixed = jnp.einsum("nd,dc->nc", d_attn, w_out, preferred_element_type=jnp.float32).astype(
        jnp.bfloat16
    )
    d_queries, d_keys, d_values = attend_backward(
        projected[0], projected[1], projected[2], d_mixed, decoder
    )
    d_projected = jnp.stack([d_queries, d_keys, d_values])
    grad_qkv = jnp.einsum("nd,tnc->tdc", gathered, d_projected, preferred_element_type=jnp.float32)
    d_input_part = jnp.einsum("tnc,tdc->nd", d_projected, w_qkv, preferred_element_type=jnp.float32)
    d_input = d_first + lax.psum(d_input_part.astype(jnp.bfloat16), "mp").astype(jnp.float32)
    attention = masked_add(carry[:4], (grad_qkv, grad_out, d_gain_one, d_bias_one), valid)
    crossing = masked_add(
        cross_carry, (grad_cross_qkv, grad_cross_out, d_gain_three, d_bias_three), valid
    )
    return (
        own_rows(d_input, rows_dev),
        own_rows(d_memory, rows_dev),
        tuple(attention) + tuple(feed),
        crossing,
    )


def store_at(buffer, value, index, valid):
    updated = lax.dynamic_update_index_in_dim(buffer, value, index, 0)
    return jnp.where(valid, updated, buffer)


def row_mask(counts_row, rows_dev):
    position = lax.axis_index(("dp", "mp")) * rows_dev + jnp.arange(rows_dev, dtype=jnp.int32)
    slot_ids = position // SLOT
    question = slot_ids // QSLOTS
    place = slot_ids % QSLOTS
    match = question[:, None] == jnp.arange(counts_row.shape[0], dtype=jnp.int32)[None, :]
    limit = jnp.sum(jnp.where(match, counts_row[None, :], 0), 1)
    return (place < limit).astype(jnp.float32)


def body(
    inputs,
    target_inputs,
    cotangent,
    slot_counts,
    w_qkv,
    w_out,
    norm1_gain,
    norm1_bias,
    w_up,
    w_down,
    norm2_gain,
    norm2_bias,
    cross_qkv,
    cross_out,
    norm3_gain,
    norm3_bias,
):
    weights = (
        w_qkv[0],
        w_out[0],
        norm1_gain[0],
        norm1_bias[0],
        w_up[0],
        w_down[0],
        norm2_gain[0],
        norm2_bias[0],
    )
    cross_weights = (cross_qkv, cross_out, norm3_gain, norm3_bias)
    segment_id = lax.axis_index("section")
    segments = lax.axis_size("section")
    decoder = segment_id == segments - 1
    micro = inputs.shape[0]
    rows_dev = inputs.shape[1]
    ticks = micro + segments - 1
    sources = jnp.where(decoder, target_inputs, inputs)
    sent = jnp.zeros(inputs.shape[1:], jnp.bfloat16)
    memories = jnp.zeros(inputs.shape, jnp.bfloat16)
    layer_outputs = jnp.zeros(inputs.shape, jnp.bfloat16)
    for tick in range(ticks):
        arrived = from_behind(sent, "section", 1)
        slot_index = tick - segment_id
        valid = (slot_index >= 0) & (slot_index < micro)
        index = jnp.clip(slot_index, 0, micro - 1)
        segment_input = lax.dynamic_index_in_dim(sources, index, 0, False)
        result, kept = forward_segment(segment_input, arrived, weights, cross_weights, decoder)
        sent = result.astype(jnp.bfloat16)
        memories = store_at(memories, arrived, index, valid)
        layer_outputs = store_at(layer_outputs, sent, index, valid)
    totals = tuple((jnp.zeros(w.shape, jnp.float32) for w in weights))
    cross_totals = tuple((jnp.zeros(w.shape, jnp.float32) for w in cross_weights))
    back = jnp.zeros(inputs.shape[1:], jnp.bfloat16)
    input_grads = jnp.zeros(inputs.shape, jnp.bfloat16)
    for tick in range(ticks):
        arrived = from_behind(back, "section", -1)
        slot_index = tick - (segments - 1 - segment_id)
        valid = (slot_index >= 0) & (slot_index < micro)
        index = jnp.clip(slot_index, 0, micro - 1)
        mask = row_mask(lax.dynamic_index_in_dim(slot_counts, index, 0, False), rows_dev)
        top = (
            lax.dynamic_index_in_dim(cotangent, index, 0, False).astype(jnp.float32) * mask[:, None]
        )
        grad_own = jnp.where(decoder, top, arrived.astype(jnp.float32))
        unused, kept = forward_segment(
            lax.dynamic_index_in_dim(sources, index, 0, False),
            lax.dynamic_index_in_dim(memories, index, 0, False),
            weights,
            cross_weights,
            decoder,
        )
        d_input, d_memory, totals, cross_totals = backward_segment(
            grad_own, kept, weights, cross_weights, decoder, totals, cross_totals, valid
        )
        back = d_memory.astype(jnp.bfloat16)
        input_grads = store_at(input_grads, d_input.astype(jnp.bfloat16), index, valid)
    totals = (
        lax.psum_scatter(totals[0], "dp", scatter_dimension=1, tiled=True),
        lax.psum_scatter(totals[1], "dp", scatter_dimension=0, tiled=True),
        lax.psum_scatter(totals[2], "dp", scatter_dimension=0, tiled=True),
        lax.psum_scatter(totals[3], "dp", scatter_dimension=0, tiled=True),
        lax.psum_scatter(totals[4], "dp", scatter_dimension=0, tiled=True),
        lax.psum_scatter(totals[5], "dp", scatter_dimension=0, tiled=True),
        lax.psum_scatter(totals[6], "dp", scatter_dimension=0, tiled=True),
        lax.psum_scatter(totals[7], "dp", scatter_dimension=0, tiled=True),
    )
    grad_qkv, grad_proj, gain_one, bias_one, grad_up, grad_down, gain_two, bias_two = totals
    cross_grad_qkv, cross_grad_out, gain_three, bias_three = (
        lax.psum_scatter(cross_totals[0], ("section", "dp"), scatter_dimension=1, tiled=True),
        lax.psum_scatter(cross_totals[1], ("section", "dp"), scatter_dimension=0, tiled=True),
        lax.psum_scatter(cross_totals[2], ("section", "dp"), scatter_dimension=0, tiled=True),
        lax.psum_scatter(cross_totals[3], ("section", "dp"), scatter_dimension=0, tiled=True),
    )
    return (
        layer_outputs[None],
        input_grads[None],
        grad_qkv[None],
        grad_proj[None],
        gain_one[None],
        bias_one[None],
        grad_up[None],
        grad_down[None],
        gain_two[None],
        bias_two[None],
        cross_grad_qkv,
        cross_grad_out,
        gain_three,
        bias_three,
    )


def solution(mesh):
    return jax.shard_map(
        body,
        mesh=mesh,
        in_specs=(
            P(None, ("dp", "mp"), None),
            P(None, ("dp", "mp"), None),
            P(None, ("dp", "mp"), None),
            P(),
            P("section", None, None, "mp"),
            P("section", None, "mp"),
            P("section", None),
            P("section", None),
            P("section", None, "mp"),
            P("section", None, "mp"),
            P("section", None),
            P("section", None),
            P(None, None, "mp"),
            P(None, "mp"),
            P(),
            P(),
        ),
        out_specs=(
            P("section", None, ("dp", "mp"), None),
            P("section", None, ("dp", "mp"), None),
            P("section", None, "dp", "mp"),
            P("section", "dp", "mp"),
            P("section", "dp"),
            P("section", "dp"),
            P("section", "dp", "mp"),
            P("section", "dp", "mp"),
            P("section", "dp"),
            P("section", "dp"),
            P(None, ("section", "dp"), "mp"),
            P(("section", "dp"), "mp"),
            P(("section", "dp")),
            P(("section", "dp")),
        ),
        check_vma=False,
    )
```

profile of v0, /device:TPU:0, one launch (start us, length us, event | category | flops | bytes accessed | tf_op | source)
XLA Modules:
  0.0 1578.3 jit_solution(6406951210410633155)
XLA Ops:
  8.0 5.7 collective-permute-start
  26.6 3.2 fusion.749
  47.2 3.2 fusion.751
  68.7 3.2 fusion.750
  82.7 13.2 all-gather.5
  102.4 11.7 fusion.199
  121.6 3.3 fusion.753
  127.7 9.2 all-reduce.67.cloned.1.call-done
  142.3 4.3 collective-permute-start.1
  161.3 3.2 fusion.752
  170.9 3.2 fusion.755
  174.1 14.6 all-reduce.41.cloned.1.call-done
  192.4 11.7 fusion.202
  212.0 13.1 all-reduce.65.cloned.1.call-done
  231.0 4.5 collective-permute-start.2
  252.2 3.2 fusion.756
  264.5 15.6 all-reduce.43.cloned.1.call-done
  284.6 7.0 multiply_convert_fusion.8
  306.1 9.5 all-reduce.63.cloned.1.call-done
  322.9 3.1 fusion.757
  343.9 3.1 fusion.758
  351.1 7.7 all-reduce.61.cloned.1.call-done
  366.5 3.0 convolution_convert_fusion.35
  372.8 7.1 multiply_convert_fusion.5
  385.6 4.7 fusion.211
  400.5 13.3 all-reduce.59.cloned.1.call-done
  424.4 3.2 fusion.759
  451.0 13.7 all-reduce.57.cloned.1.call-done
  464.7 3.0 multiply_reduce_fusion.13
  479.9 7.0 multiply_convert_fusion.2
  494.6 4.8 fusion.214
  501.1 3.8 fusion.754
  508.1 4.1 all_gather.50
  512.2 9.8 all-reduce.55.cloned.1.call-done
  526.3 7.2 collective-permute-done.5
  555.2 8.4 all-reduce.53.cloned.1.call-done
  563.6 3.0 multiply_reduce_fusion.12
  572.8 3.1 fusion.760
  596.1 13.8 all-reduce.51.cloned.1.call-done
  609.9 4.6 fusion.719
  616.6 11.7 fusion.205
  628.6 3.3 convolution_bitcast_fusion.3
  636.7 12.4 all-reduce.49.cloned.1.call-done
  649.1 4.1 fusion.717
  658.0 3.0 convolution_convert_fusion.36
  668.8 3.0 convolution_convert_fusion.29
  676.7 3.0 convolution_convert_fusion.22
  698.2 3.0 fusion.167
  714.1 4.0 fusion.13
  718.1 9.6 copy.433
  731.5 4.2 add_bitcast_fusion
  747.3 3.0 fusion.521
  751.9 5.3 select_add_fusion.1
  757.9 3.1 fusion.689
  762.7 5.4 select_add_fusion
  773.3 44.2 %all-reduce.7 = (f32[1024]{0:T(1024)S(1)}, f32[1024]{0:T(1024)S(1)}) all-reduce(f32[1024]{0:T(1024)S(1)} %get-tuple-element.266, f32[1024]{0:T(1024)S(1)} %get-tuple-element.265), channel_id=21, replica_groups=mesh['section'=2,'dp'=8,'mp'=2] {'section','dp'}, use_global_device_ids=true, to_apply=%region_141.142.clone | all-reduce | flops 2048 | bytes 16384
  818.7 3.3 multiply_reduce_fusion.33
  822.1 33.7 %all-reduce.8 = (f32[1024]{0:T(1024)S(1)}, f32[1024]{0:T(1024)S(1)}, f32[1024]{0:T(1024)S(1)}, f32[1024]{0:T(1024)S(1)}) all-reduce(f32[1024]{0:T(1024)S(1)} %select_add_fusion.9, f32[1024]{0:T(1024)S(1)} %select_add_fusion.8, f32[1024]{0:T(1024)S(1)} %get-tuple-element.268, ...), channel_id=13, replica_groups=mesh['section'=2,'dp'=8,'mp'=2] {'dp'}, use_global_device_ids=true, to_apply=%region_121.122.clone | all-reduce | flops 4096 | bytes 32768
  864.3 128.8 %all-reduce.45.cloned.1.call-done = f32[3,1024,512]{2,0,1:T(4,128)} async-done(((f32[3,1024,512]{2,0,1:T(4,128)}), f32[3,1024,512]{2,0,1:T(4,128)}) %all-reduce.45.cloned.1.call-update) | async-done | bytes 6291472
  995.1 119.2 %reduce-scatter.6.cloned.1.call-done = f32[3,128,512]{1,2,0:T(8,128)} async-done(((f32[3,1024,512]{1,2,0:T(8,128)}), f32[3,128,512]{1,2,0:T(8,128)}) %reduce-scatter.6.cloned.1.call-update) | async-done | bytes 786448 | tf_op jit(solution)/shard_map/reduce_scatter | solution.py:355
  1116.6 80.7 %reduce-scatter.14.cloned.1.call-done = f32[64,512]{1,0:T(8,128)} async-done(((f32[1024,512]{1,0:T(8,128)}), f32[64,512]{1,0:T(8,128)}) %reduce-scatter.14.cloned.1.call-update) | async-done | bytes 131088 | tf_op jit(solution)/shard_map/reduce_scatter | solution.py:367
  1197.3 69.1 %reduce-scatter.8.cloned.1.call-done = f32[128,512]{1,0:T(8,128)} async-done(((f32[1024,512]{1,0:T(8,128)}), f32[128,512]{1,0:T(8,128)}) %reduce-scatter.8.cloned.1.call-update) | async-done | bytes 262160 | tf_op jit(solution)/shard_map/reduce_scatter | solution.py:356
  1266.4 152.5 %reduce-scatter.10.cloned.1.call-done = f32[128,2048]{1,0:T(8,128)} async-done(((f32[1024,2048]{1,0:T(8,128)}), f32[128,2048]{1,0:T(8,128)}) %reduce-scatter.10.cloned.1.call-update) | async-done | bytes 1048592 | tf_op jit(solution)/shard_map/reduce_scatter | solution.py:359
  1419.0 152.3 %reduce-scatter.12.cloned.1.call-done = f32[128,2048]{1,0:T(8,128)} async-done(((f32[1024,2048]{1,0:T(8,128)}), f32[128,2048]{1,0:T(8,128)}) %reduce-scatter.12.cloned.1.call-update) | async-done | bytes 1048592 | tf_op jit(solution)/shard_map/reduce_scatter | solution.py:360
  (932 shorter events, 423.5 us)
Async XLA Ops:
  7.2 12.1 copy-start
  7.2 54.2 %all-reduce.37.cloned.1.call-start = ((), (), s32[]{:S(2)}) async-start(), calls=%async_computation.5 | async-start | bytes 1048576 | tf_op jit(solution)/shard_map/psum | solution.py:110
  8.0 45.9 %collective-permute-start = (bf16[128,1024]{1,0:T(8,128)(2,1)}, bf16[128,1024]{1,0:T(8,128)(2,1)}, u32[]{:S(2)}, u32[]{:S(2)}) collective-permute-start(bf16[128,1024]{1,0:T(8,128)(2,1)} %broadcast.951), channel_id=1, source_target_pairs={{0,16},{1,17},{2,18},{3,19},{4,20},{5,21},{6,22},{7,23},{8,24},{9,... | collective-permute-start | bytes 786440 | tf_op jit(solution)/shard_map/ppermute | solution.py:14
  13.6 281.1 %collective-permute-start.3 = (bf16[128,1024]{1,0:T(8,128)(2,1)}, bf16[128,1024]{1,0:T(8,128)(2,1)}, u32[]{:S(2)}, u32[]{:S(2)}) collective-permute-start(bf16[128,1024]{1,0:T(8,128)(2,1)} %broadcast.951), channel_id=1, source_target_pairs={{16,0},{17,1},{18,2},{19,3},{20,4},{21,5},{22,6},{23,7},{24,8},{25... | collective-permute-start | bytes 786440 | tf_op jit(solution)/shard_map/ppermute | solution.py:14
  33.2 65.4 %all-reduce.39.cloned.1.call-start = ((), (), s32[]{:S(2)}) async-start(), calls=%async_computation.6 | async-start | bytes 1048576 | tf_op jit(solution)/shard_map/psum | solution.py:126
  50.4 5.9 copy-start.262
  57.0 7.5 copy-start.118
  57.0 7.5 copy-start.134
  75.3 61.7 %all-reduce.67.cloned.1.call-start = ((), (), s32[]{:S(2)}) async-start(), calls=%async_computation.25 | async-start | bytes 2097152 | tf_op jit(solution)/shard_map/psum | solution.py:137
  114.1 7.5 copy-start.249
  114.1 74.6 %all-reduce.41.cloned.1.call-start = ((), (), s32[]{:S(2)}) async-start(), calls=%async_computation.7 | async-start | bytes 1048576 | tf_op jit(solution)/shard_map/psum | solution.py:126
  139.5 7.1 copy-start.67
  139.5 7.1 copy-start.76
  142.3 10.0 collective-permute-start.1
  167.9 57.3 %all-reduce.65.cloned.1.call-start = ((), (), s32[]{:S(2)}) async-start(), calls=%async_computation.24 | async-start | bytes 2097152 | tf_op jit(solution)/shard_map/psum | solution.py:137
  174.1 30.1 %copy-start.243 = (f32[8,256]{1,0:T(8,128)}, f32[8,256]{1,0:T(8,128)S(1)}, u32[]{:S(2)}) copy-start(f32[8,256]{1,0:T(8,128)S(1)} %get-tuple-element.238) | copy-start | bytes 24580
  204.2 75.9 %all-reduce.43.cloned.1.call-start = ((), (), s32[]{:S(2)}) async-start(), calls=%async_computation.8 | async-start | bytes 1048576 | tf_op jit(solution)/shard_map/psum | solution.py:126
  229.0 53.3 %copy-start.215 = (f32[256]{0:T(256)}, f32[256]{0:T(256)S(1)}, u32[]{:S(2)}) copy-start(f32[256]{0:T(256)S(1)} %broadcast_multiply_fusion.8) | copy-start | bytes 3076
  231.0 10.0 collective-permute-start.2
  236.4 46.0 %copy-start.219 = (f32[256]{0:T(256)}, f32[256]{0:T(256)S(1)}, u32[]{:S(2)}) copy-start(f32[256]{0:T(256)S(1)} %fusion.558) | copy-start | bytes 3076
  240.6 6.4 copy-start.263
  259.5 56.2 %all-reduce.63.cloned.1.call-start = ((), (), s32[]{:S(2)}) async-start(), calls=%async_computation.23 | async-start | bytes 2097152 | tf_op jit(solution)/shard_map/psum | solution.py:110
  284.6 7.0 copy-start.35
  284.6 7.9 copy-start.252
  294.6 64.2 %all-reduce.61.cloned.1.call-start = ((), (), s32[]{:S(2)}) async-start(), calls=%async_computation.22 | async-start | bytes 2097152 | tf_op jit(solution)/shard_map/psum | solution.py:126
  306.1 16.8 %copy-start.180 = (bf16[1,256,512]{1,2,0:T(8,128)(2,1)}, bf16[1,256,512]{1,2,0:T(8,128)(2,1)S(1)}, u32[]{:S(2)}) copy-start(bf16[1,256,512]{1,2,0:T(8,128)(2,1)S(1)} %copy.391) | copy-start | bytes 786436
  326.0 5.7 copy-start.273
  331.7 29.4 %copy-start.233 = (f32[256]{0:T(256)}, f32[256]{0:T(256)S(1)}, u32[]{:S(2)}) copy-start(f32[256]{0:T(256)S(1)} %negate_multiply_fusion.14) | copy-start | bytes 3076
  337.8 76.0 %all-reduce.59.cloned.1.call-start = ((), (), s32[]{:S(2)}) async-start(), calls=%async_computation.21 | async-start | bytes 3145728 | tf_op jit(solution)/shard_map/psum | solution.py:235
  372.8 7.1 copy-start.208
  391.9 72.7 %all-reduce.57.cloned.1.call-start = ((), (), s32[]{:S(2)}) async-start(), calls=%async_computation.20 | async-start | bytes 2097152 | tf_op jit(solution)/shard_map/psum | solution.py:203
  413.8 5.1 copy-start.38
  413.8 6.5 copy-start.30
  413.8 6.5 copy-start.53
  415.6 15.4 collective-permute-start.4
  424.3 5.3 copy-start.179
  427.5 8.5 copy-start.269
  436.0 28.7 %copy-start.235 = (f32[256]{0:T(256)}, f32[256]{0:T(256)S(1)}, u32[]{:S(2)}) copy-start(f32[256]{0:T(256)S(1)} %negate_multiply_fusion.11) | copy-start | bytes 3076
  441.8 80.3 %all-reduce.55.cloned.1.call-start = ((), (), s32[]{:S(2)}) async-start(), calls=%async_computation.19 | async-start | bytes 2097152 | tf_op jit(solution)/shard_map/psum | solution.py:235
  488.0 11.4 copy-start.158
  501.0 62.6 %all-reduce.53.cloned.1.call-start = ((), (), s32[]{:S(2)}) async-start(), calls=%async_computation.18 | async-start | bytes 2097152 | tf_op jit(solution)/shard_map/psum | solution.py:110
  508.1 25.4 %copy-start.250 = (f32[128]{0:T(128)S(1)}, f32[128]{0:T(128)}, u32[]{:S(2)}) copy-start(f32[128]{0:T(128)} %compare_convert_fusion) | copy-start | bytes 1540
  522.1 11.5 copy-start.136
  523.2 10.3 collective-permute-start.5
  526.0 11.7 copy-start.271
  543.4 66.4 %all-reduce.51.cloned.1.call-start = ((), (), s32[]{:S(2)}) async-start(), calls=%async_computation.17 | async-start | bytes 3145728 | tf_op jit(solution)/shard_map/psum | solution.py:126
  588.0 5.4 copy-start.155
  588.0 61.0 %all-reduce.49.cloned.1.call-start = ((), (), s32[]{:S(2)}) async-start(), calls=%async_computation.16 | async-start | bytes 2097152 | tf_op jit(solution)/shard_map/psum | solution.py:137
  616.6 11.9 copy-start.216
  616.6 12.0 copy-start.220
  628.3 231.8 %all-reduce.47.cloned.1.call-start = ((), (), s32[]{:S(2)}) async-start(), calls=%async_computation.15 | async-start | bytes 3145728 | tf_op jit(solution)/shard_map/psum | solution.py:251
  704.9 288.2 %all-reduce.45.cloned.1.call-start = ((), (), s32[]{:S(2)}) async-start(), calls=%async_computation.14 | async-start | bytes 16777216
  727.7 386.6 %reduce-scatter.6.cloned.1.call-start = ((), (), s32[]{:S(2)}) async-start(), calls=%async_computation.9 | async-start | bytes 7077888 | tf_op jit(solution)/shard_map/reduce_scatter | solution.py:355
  735.7 461.6 %reduce-scatter.14.cloned.1.call-start = ((), (), s32[]{:S(2)}) async-start(), calls=%async_computation.13 | async-start | bytes 2228224 | tf_op jit(solution)/shard_map/reduce_scatter | solution.py:367
  741.9 524.5 %reduce-scatter.8.cloned.1.call-start = ((), (), s32[]{:S(2)}) async-start(), calls=%async_computation.10 | async-start | bytes 2359296 | tf_op jit(solution)/shard_map/reduce_scatter | solution.py:356
  747.3 671.7 %reduce-scatter.10.cloned.1.call-start = ((), (), s32[]{:S(2)}) async-start(), calls=%async_computation.11 | async-start | bytes 9437184 | tf_op jit(solution)/shard_map/reduce_scatter | solution.py:359
  757.3 814.0 %reduce-scatter.12.cloned.1.call-start = ((), (), s32[]{:S(2)}) async-start(), calls=%async_computation.12 | async-start | bytes 9437184 | tf_op jit(solution)/shard_map/reduce_scatter | solution.py:360
  768.1 5.0 copy-start.223
  768.1 5.0 copy-start.224
  768.1 5.0 copy-start.227
  768.2 5.0 copy-start.228
  768.2 5.0 copy-start.231
  771.2 86.9 %copy-start.200 = (f32[1,1024]{1,0:T(1,128)S(1)}, f32[1,1024]{1,0:T(1,128)}, u32[]{:S(2)}) copy-start(f32[1,1024]{1,0:T(1,128)} %param.26) | copy-start | bytes 12292
  771.2 86.9 %copy-start.218 = (f32[1,1024]{1,0:T(1,128)S(1)}, f32[1,1024]{1,0:T(1,128)}, u32[]{:S(2)}) copy-start(f32[1,1024]{1,0:T(1,128)} %param.27) | copy-start | bytes 12292
  (237 other events, 618.2 us)
Sparse Core Ops, SparseCore 0:
  33.3 21.8 all-reduce.36
  75.4 21.8 all-reduce.38
  114.2 22.6 all-reduce.66
  168.0 20.6 all-reduce.40
  204.3 20.8 all-reduce.64
  259.6 20.4 all-reduce.42
  294.8 20.8 all-reduce.62
  338.0 20.8 all-reduce.60
  392.0 21.7 all-reduce.58
  441.9 22.7 all-reduce.56
  501.1 20.8 all-reduce.54
  543.6 19.9 all-reduce.52
  588.1 21.7 all-reduce.50
  628.4 20.5 all-reduce.48
  705.0 21.3 all-reduce.46
  733.4 259.6 all-reduce.44
  997.0 117.2 reduce-scatter.5
  1117.1 80.1 reduce-scatter.13
  1201.8 64.5 reduce-scatter.7
  1270.9 148.0 reduce-scatter.9
  1423.2 148.0 reduce-scatter.11
where the time goes:
time: 1590 us; the launch traced here: 1580 us
  waiting for transfers between devices  853 us (54%)
  matrix products  302 us (19%)
  local copies, waits for them, and re-layouts  159 us (10%)
  blocking collectives  125 us (8%)
  other arithmetic  99.9 us (6%)
  starting transfers between devices  21.1 us (1%)
  between operations  18.9 us (1%)
    reduce_scatter x1, waiting for transfers between devices, body(): lax.psum_scatter(totals[4], 'dp', scatter_dimension=0, tiled=True)  153 us
    reduce_scatter x1, waiting for transfers between devices, body(): lax.psum_scatter(totals[5], 'dp', scatter_dimension=0, tiled=True)  152 us
    unnamed x22, waiting for transfers between devices  129 us
    reduce_scatter x1, waiting for transfers between devices, body(): lax.psum_scatter(totals[0], 'dp', scatter_dimension=1, tiled=True)  119 us
    reduce_scatter x1, waiting for transfers between devices, body(): lax.psum_scatter(cross_totals[1], ('section', 'dp'), scatter_dimension=0,...  80.7 us
    unnamed x2, blocking collectives  77.9 us
    reduce_scatter x1, waiting for transfers between devices, body(): lax.psum_scatter(totals[1], 'dp', scatter_dimension=0, tiled=True)  69.1 us
    psum x5, waiting for transfers between devices, forward_segment(): lax.psum(jnp.einsum('nc,dc->nd', cross_mixed, cross_out, preferred_elemen...  51.7 us
  transfers between devices with their start and end apart: 27, of which 21 were waited for; matrix products, arithmetic and copies ran while one was open for 21% of the time, Pallas kernels for 0%

commit v1 on v0

v1 whole, which is shorter than its diff:
```python
import functools

import jax
import jax.numpy as jnp
from jax import lax
from jax.experimental import pallas as pl
from jax.experimental.pallas import tpu as pltpu
from jax.sharding import PartitionSpec as P

HEAD = 64
SLOT = 256
QSLOTS = 4
CHUNK = 512
PAIR = 2 * HEAD
STRIP = 64
EPS = 1e-5
NEG = -1000000000.0
MESH = pl.DeviceIdType.MESH
BF = jnp.bfloat16
F32 = jnp.float32
VM = pltpu.VMEM


def dot_nn(a, b):
    return lax.dot_general(a, b, (((1,), (0,)), ((), ())), preferred_element_type=F32)


def dot_nt(a, b):
    return lax.dot_general(a, b, (((1,), (1,)), ((), ())), preferred_element_type=F32)


def dot_tn(a, b):
    return lax.dot_general(a, b, (((0,), (0,)), ((), ())), preferred_element_type=F32)


def loop(count, body):
    def step(i, carry):
        body(i)
        return carry

    lax.fori_loop(0, count, step, 0)


def head_masks():
    lane = lax.broadcasted_iota(jnp.int32, (1, PAIR), 1)
    first = jnp.where(lane < HEAD, 1.0, 0.0).astype(BF)
    second = jnp.where(lane < HEAD, 0.0, 1.0).astype(BF)
    return first, second


def probs_of(query, keys, mask, limit):
    scores = dot_nt(query * (mask * (HEAD**-0.5)).astype(BF), keys)
    if limit is not None:
        row = lax.broadcasted_iota(jnp.int32, scores.shape, 0)
        col = lax.broadcasted_iota(jnp.int32, scores.shape, 1)
        scores = jnp.where(row + limit >= col, scores, NEG)
    expo = jnp.exp(scores - jnp.max(scores, -1, keepdims=True))
    return expo / jnp.sum(expo, -1, keepdims=True)


def attend_forward(proj, mixed, rows, lanes, limit):
    query, keys, values = proj[0, rows, lanes], proj[1, rows, lanes], proj[2, rows, lanes]
    masks = head_masks()
    low = [probs_of(query, keys, mask, limit).astype(BF) for mask in masks]
    mixed[rows, lanes] = dot_nn(
        jnp.concatenate(low, 1), jnp.concatenate([values * mask for mask in masks], 0)
    ).astype(BF)


def attend_backward(proj, d_mixed, d_proj, rows, lanes, limit):
    query, keys, values = proj[0, rows, lanes], proj[1, rows, lanes], proj[2, rows, lanes]
    grad = d_mixed[rows, lanes]
    masks = head_masks()
    low, d_scores = [], []
    for mask in masks:
        weights = probs_of(query, keys, mask, limit)
        d_weights = dot_nt(grad * mask, values)
        inner = jnp.sum(weights * d_weights, -1, keepdims=True)
        d_scores.append((weights * (d_weights - inner)).astype(BF))
        low.append(weights.astype(BF))
    scale = HEAD**-0.5
    d_proj[2, rows, lanes] = dot_tn(
        jnp.concatenate(low, 0), jnp.concatenate([grad * mask for mask in masks], 0)
    ).astype(BF)
    d_proj[0, rows, lanes] = (
        dot_nn(jnp.concatenate(d_scores, 1), jnp.concatenate([keys * mask for mask in masks], 0))
        * scale
    ).astype(BF)
    d_proj[1, rows, lanes] = (
        dot_tn(jnp.concatenate(d_scores, 0), jnp.concatenate([query * mask for mask in masks], 0))
        * scale
    ).astype(BF)


def norm_forward(value, gain, bias):
    center = value - jnp.mean(value, -1, keepdims=True)
    scale = lax.rsqrt(jnp.mean(center * center, -1, keepdims=True) + EPS)
    unit = center * scale
    return unit, scale, unit * gain + bias


def norm_backward(grad, unit, scale, gain, sums, which):
    fold = lambda v: jnp.sum(v.reshape(v.shape[0] // 8, 8, v.shape[1]), 0)
    sums[which] += fold(grad * unit)
    sums[which + 1] += fold(grad)
    d_unit = grad * gain
    first = jnp.mean(d_unit, -1, keepdims=True)
    second = jnp.mean(d_unit * unit, -1, keepdims=True)
    return scale * (d_unit - first - unit * second)


def layer_kernel(
    sections,
    inputs,
    targets,
    cotangent,
    counts,
    qkv_hbm,
    out_hbm,
    gain1,
    bias1,
    up_hbm,
    down_hbm,
    gain2,
    bias2,
    cross_hbm,
    cross_out_hbm,
    gain3,
    bias3,
    seg_out,
    in_grad,
    norm_out,
    a_out,
    b_out,
    w_qkv,
    w_out,
    w_up,
    w_down,
    w_cross,
    w_cross_out,
    a_fac,
    b_fac,
    proj,
    cross_proj,
    unit1,
    unit2,
    unit3,
    scale1,
    scale2,
    scale3,
    resid,
    slope,
    d_out,
    d_mix,
    sent,
    got,
    half_send,
    half_own,
    half_got,
    sums,
    load_sem,
    x_sem,
    ex_send,
    ex_recv,
    hop_send,
    hop_recv,
    out_sem,
):
    section = lax.axis_index("section")
    dp = lax.axis_index("dp")
    core = lax.axis_index("mp")
    decoder = section == sections - 1
    encoder = section != sections - 1
    mate = (section, dp, 1 - core)
    across = (1 - section, dp, core)
    half = seg_out.shape[2]
    slot = 2 * half
    limit = jnp.where(decoder, 0, slot)
    width = w_up.shape[1]
    parts = width // CHUNK
    own = core * half
    other = (1 - core) * half

    d_branch, crossed, d_attn, layer_in, normed_low, memory, d_cross = (a_fac.at[i] for i in range(7))
    act = b_fac.at[0:parts]
    d_hidden = b_fac.at[parts : 2 * parts]
    mixed = b_fac.at[2 * parts]
    d_proj = b_fac.at[2 * parts + 1 : 2 * parts + 4]
    d_cross_proj = b_fac.at[2 * parts + 4 : 2 * parts + 7]
    cross_mixed = b_fac.at[2 * parts + 7]

    def rows_of(m):
        return pl.ds(pl.multiple_of(m * slot, slot), slot)

    def half_of(m, offset):
        return pl.ds(pl.multiple_of(m * slot + offset, half), half)

    def strip_of(m, k):
        return pl.ds(pl.multiple_of(m * slot + k * STRIP, STRIP), STRIP)

    def lanes_of(j):
        return pl.ds(pl.multiple_of(j * PAIR, PAIR), PAIR)

    barrier = pltpu.get_barrier_semaphore()
    for device in (mate, across):
        pl.semaphore_signal(barrier, inc=1, device_id=device, device_id_type=MESH)

    loads = [
        pltpu.make_async_copy(src, dst, load_sem.at[i])
        for i, (src, dst) in enumerate(
            (
                (qkv_hbm.at[0], w_qkv),
                (out_hbm.at[0], w_out),
                (up_hbm.at[0], w_up),
                (down_hbm.at[0], w_down),
                (cross_hbm, w_cross),
                (cross_out_hbm, w_cross_out),
            )
        )
    ]

    def local_rows(src, dst, m, sem):
        return pltpu.make_async_copy(src.at[m], dst.at[half_of(m, own)], sem)

    def mate_rows(src, dst, m, send, recv):
        return pltpu.make_async_remote_copy(
            src_ref=src.at[m],
            dst_ref=dst.at[half_of(m, own)],
            send_sem=send,
            recv_sem=recv,
            device_id=mate,
            device_id_type=MESH,
        )

    def start_rows(src, dst, base):
        for m in range(2):
            local_rows(src, dst, m, x_sem.at[base + m]).start()
        for m in range(2):
            mate_rows(src, dst, m, x_sem.at[base + 2 + m], x_sem.at[base + 4 + m]).start()

    def wait_rows(src, dst, base, m):
        local_rows(src, dst, m, x_sem.at[base + m]).wait()
        mate_rows(src, dst, m, x_sem.at[base + 2 + m], x_sem.at[base + 4 + m]).wait()

    @pl.when(encoder)
    def _():
        for m in range(2):
            local_rows(inputs, layer_in, m, x_sem.at[m]).start()

    @pl.when(decoder)
    def _():
        for m in range(2):
            local_rows(targets, layer_in, m, x_sem.at[m]).start()

    loads[0].start()
    loads[1].start()
    pl.semaphore_wait(barrier, 2)

    def mate_start(src, dst, base):
        for m in range(2):
            mate_rows(src, dst, m, x_sem.at[base + 2 + m], x_sem.at[base + 4 + m]).start()

    @pl.when(encoder)
    def _():
        mate_start(inputs, layer_in, 0)

    @pl.when(decoder)
    def _():
        mate_start(targets, layer_in, 0)

    for copy in loads[2:]:
        copy.start()

    @pl.when(decoder)
    def _():
        start_rows(cotangent, d_out, 6)

    sums[...] = jnp.zeros_like(sums)

    def exchange(which, buffer, m):
        return pltpu.make_async_remote_copy(
            src_ref=sent.at[rows_of(m)],
            dst_ref=got.at[buffer, rows_of(m)],
            send_sem=ex_send.at[which, m],
            recv_sem=ex_recv.at[which, m],
            device_id=mate,
            device_id_type=MESH,
        )

    def half_exchange(which, m):
        return pltpu.make_async_remote_copy(
            src_ref=half_send.at[which, m],
            dst_ref=half_got.at[which, m],
            send_sem=hop_send.at[4 + which, m],
            recv_sem=hop_recv.at[4 + which, m],
            device_id=mate,
            device_id_type=MESH,
        )

    def across_copy(src, dst, which, m):
        return pltpu.make_async_remote_copy(
            src_ref=src,
            dst_ref=dst.at[half_of(m, own)],
            send_sem=hop_send.at[which, m],
            recv_sem=hop_recv.at[which, m],
            device_id=across,
            device_id_type=MESH,
        )

    def forward_copy(ref, which, m):
        return pltpu.make_async_remote_copy(
            src_ref=ref.at[half_of(m, own)],
            dst_ref=ref.at[half_of(m, own)],
            send_sem=hop_send.at[which, m],
            recv_sem=hop_recv.at[which, m],
            device_id=mate,
            device_id_type=MESH,
        )

    def project_out(value, weight, m):
        for n in range(sent.shape[1] // CHUNK):
            cols = slice(n * CHUNK, (n + 1) * CHUNK)
            sent[rows_of(m), cols] = dot_nt(value, weight[cols, :]).astype(BF)

    def summed(buffer, strip):
        return sent[strip].astype(F32) + got[buffer, strip].astype(F32)

    loads[0].wait()

    def attention_in(m):
        @pl.when(encoder)
        def _():
            wait_rows(inputs, layer_in, 0, m)

        @pl.when(decoder)
        def _():
            wait_rows(targets, layer_in, 0, m)

        rows = rows_of(m)
        for t in range(3):
            proj[t, rows] = dot_nn(layer_in[rows], w_qkv[t]).astype(BF)
        loop(CHUNK // PAIR, lambda j: attend_forward(proj, mixed, rows, lanes_of(j), limit))
        project_out(mixed[rows], w_out, m)
        exchange(0, 0, m).start()

    loads[1].wait()
    loop(2, attention_in)
    for copy in loads[2:]:
        copy.wait()

    def after_attention(m):
        exchange(0, 0, m).wait()

        def norm(k):
            strip = strip_of(m, k)
            unit, scale, value = norm_forward(
                layer_in[strip].astype(F32) + summed(0, strip), gain1[...], bias1[...]
            )
            unit1[strip] = unit.astype(BF)
            scale1[strip] = scale
            resid[strip] = value
            normed_low[strip] = value.astype(BF)
            crossed[strip] = value.astype(BF)

        loop(slot // STRIP, norm)

        @pl.when(decoder)
        def _():
            rows = rows_of(m)
            cross_proj[0, rows] = dot_nn(normed_low[rows], w_cross[0]).astype(BF)
            across_copy(seg_out.at[0, m], memory, 0, m).wait_recv()
            forward_copy(memory, 1, m).start()
            forward_copy(memory, 1, m).wait()
            for t in range(1, 3):
                cross_proj[t, rows] = dot_nn(memory[rows], w_cross[t]).astype(BF)
            loop(
                CHUNK // PAIR,
                lambda j: attend_forward(cross_proj, cross_mixed, rows, lanes_of(j), None),
            )
            project_out(cross_mixed[rows], w_cross_out, m)
            exchange(1, 1, m).start()

    loop(2, after_attention)

    def feed_forward(m):
        rows = rows_of(m)

        @pl.when(decoder)
        def _():
            exchange(1, 1, m).wait()

            def norm(k):
                strip = strip_of(m, k)
                unit, scale, value = norm_forward(
                    resid[strip] + summed(1, strip), gain3[...], bias3[...]
                )
                unit3[strip] = unit.astype(BF)
                scale3[strip] = scale
                resid[strip] = value
                crossed[strip] = value.astype(BF)

            loop(slot // STRIP, norm)

        for n in range(parts):
            pre = dot_nn(crossed[rows], w_up[:, n * CHUNK : (n + 1) * CHUNK])
            rise = 0.5 + 0.5 * lax.erf(pre * (0.5**0.5))
            act[n, rows] = (pre * rise).astype(BF)
            slope[n, rows] = (rise + pre * jnp.exp(-0.5 * pre * pre) * 0.3989422804014327).astype(BF)
        project_out(jnp.concatenate([act[n, rows] for n in range(parts)], 1), w_down, m)
        exchange(2, 2, m).start()

    loop(2, feed_forward)

    def finish_forward(m):
        exchange(2, 2, m).wait()

        def norm(k):
            strip = strip_of(m, k)
            unit, scale, value = norm_forward(
                resid[strip] + summed(2, strip), gain2[...], bias2[...]
            )
            unit2[strip] = unit.astype(BF)
            scale2[strip] = scale
            place = k * STRIP - own

            @pl.when((place >= 0) & (place < half))
            def _():
                seg_out[0, m, pl.ds(pl.multiple_of(lax.rem(k * STRIP, half), STRIP), STRIP)] = (
                    value.astype(BF)
                )

        loop(slot // STRIP, norm)

        @pl.when(encoder)
        def _():
            across_copy(seg_out.at[0, m], memory, 0, m).start()

    loop(2, finish_forward)

    question = dp // QSLOTS
    spot = dp - question * QSLOTS

    def feed_backward(m):
        rows = rows_of(m)

        @pl.when(encoder)
        def _():
            across_copy(half_send.at[0, m], d_out, 2, m).wait_recv()
            forward_copy(d_out, 3, m).start()
            forward_copy(d_out, 3, m).wait()

        @pl.when(decoder)
        def _():
            wait_rows(cotangent, d_out, 6, m)

        keep = jnp.where(spot < counts[m, question], 1.0, 0.0)
        keep = jnp.where(decoder, keep, 1.0)

        def norm(k):
            strip = strip_of(m, k)
            grad = norm_backward(
                d_out[strip].astype(F32) * keep,
                unit2[strip].astype(F32),
                scale2[strip],
                gain2[...],
                sums,
                2,
            )
            resid[strip] = grad
            d_branch[strip] = grad.astype(BF)

        loop(slot // STRIP, norm)
        for n in range(parts):
            grad = dot_nn(d_branch[rows], w_down[:, n * CHUNK : (n + 1) * CHUNK])
            d_hidden[n, rows] = (grad * slope[n, rows].astype(F32)).astype(BF)
        project_out(jnp.concatenate([d_hidden[n, rows] for n in range(parts)], 1), w_up, m)
        exchange(3, 0, m).start()

    loop(2, feed_backward)

    def cross_backward(m):
        rows = rows_of(m)

        def norm(k):
            strip = strip_of(m, k)
            grad = norm_backward(
                resid[strip] + summed(0, strip),
                unit3[strip].astype(F32),
                scale3[strip],
                gain3[...],
                sums,
                4,
            )
            resid[strip] = grad
            d_cross[strip] = grad.astype(BF)

        loop(slot // STRIP, norm)
        d_mix[rows] = dot_nn(d_cross[rows], w_cross_out[...]).astype(BF)
        loop(
            CHUNK // PAIR,
            lambda j: attend_backward(cross_proj, d_mix, d_cross_proj, rows, lanes_of(j), None),
        )

        def memory_part(offset):
            piece = half_of(m, offset)
            return jnp.concatenate([d_cross_proj[1, piece], d_cross_proj[2, piece]], 1)

        def memory_weight(n):
            cols = slice(n * CHUNK, (n + 1) * CHUNK)
            return jnp.concatenate([w_cross[1, cols], w_cross[2, cols]], 1)

        for n in range(sent.shape[1] // CHUNK):
            cols = slice(n * CHUNK, (n + 1) * CHUNK)
            half_send[0, m, :, cols] = dot_nt(memory_part(other), memory_weight(n)).astype(BF)
        half_exchange(0, m).start()
        for n in range(sent.shape[1] // CHUNK):
            cols = slice(n * CHUNK, (n + 1) * CHUNK)
            half_own[m, :, cols] = dot_nt(memory_part(own), memory_weight(n))
        project_out(d_cross_proj[0, rows], w_cross[0], m)
        exchange(4, 1, m).start()
        half_exchange(0, m).wait()
        half_send[0, m] = (half_own[m] + half_got[0, m].astype(F32)).astype(BF)
        across_copy(half_send.at[0, m], d_out, 2, m).start()

    def attention_back(m):
        rows = rows_of(m)

        def norm_rows(buffer):
            def norm(k):
                strip = strip_of(m, k)
                grad = norm_backward(
                    resid[strip] + summed(buffer, strip),
                    unit1[strip].astype(F32),
                    scale1[strip],
                    gain1[...],
                    sums,
                    0,
                )
                resid[strip] = grad
                d_attn[strip] = grad.astype(BF)

            loop(slot // STRIP, norm)

        @pl.when(decoder)
        def _():
            exchange(4, 1, m).wait()

        @pl.when(encoder)
        def _():
            exchange(3, 0, m).wait()

        norm_rows(jnp.where(decoder, 1, 0))
        d_mix[rows] = dot_nn(d_attn[rows], w_out[...]).astype(BF)
        loop(
            CHUNK // PAIR, lambda j: attend_backward(proj, d_mix, d_proj, rows, lanes_of(j), limit)
        )

        def input_part(offset):
            piece = half_of(m, offset)
            return jnp.concatenate([d_proj[t, piece] for t in range(3)], 1)

        def input_weight(n):
            cols = slice(n * CHUNK, (n + 1) * CHUNK)
            return jnp.concatenate([w_qkv[t, cols] for t in range(3)], 1)

        for n in range(sent.shape[1] // CHUNK):
            cols = slice(n * CHUNK, (n + 1) * CHUNK)
            half_send[1, m, :, cols] = dot_nt(input_part(other), input_weight(n)).astype(BF)
        half_exchange(1, m).start()
        for n in range(sent.shape[1] // CHUNK):
            cols = slice(n * CHUNK, (n + 1) * CHUNK)
            half_own[m, :, cols] = dot_nt(input_part(own), input_weight(n))

    @pl.when(decoder)
    def _():
        def both(m):
            exchange(3, 0, m).wait()
            cross_backward(m)

        loop(2, both)

    loop(2, attention_back)

    def finish_backward(m):
        half_exchange(1, m).wait()
        in_grad[0, m] = (
            resid[half_of(m, own)] + half_own[m] + half_got[1, m].astype(F32)
        ).astype(BF)

    loop(2, finish_backward)

    @pl.when(encoder)
    def _():
        for m in range(2):
            across_copy(seg_out.at[0, m], memory, 0, m).wait_send()

    @pl.when(decoder)
    def _():
        for m in range(2):
            across_copy(half_send.at[0, m], d_out, 2, m).wait_send()

    for i in range(6):
        norm_out[i : i + 1] = jnp.sum(sums[i], 0, keepdims=True)
    norm_out[6:8] = jnp.zeros_like(norm_out[6:8])
    copies = [
        pltpu.make_async_copy(a_fac, a_out, out_sem.at[0]),
        pltpu.make_async_copy(b_fac, b_out, out_sem.at[1]),
    ]
    for copy in copies:
        copy.start()
    for copy in copies:
        copy.wait()


def body(
    sections,
    inputs,
    target_inputs,
    cotangent,
    slot_counts,
    w_qkv,
    w_out,
    norm1_gain,
    norm1_bias,
    w_up,
    w_down,
    norm2_gain,
    norm2_bias,
    cross_qkv,
    cross_out,
    norm3_gain,
    norm3_bias,
):
    micro, half, depth = inputs.shape
    rows = micro * 2 * half
    heads = w_out.shape[2]
    width = w_up.shape[2]
    parts = width // CHUNK
    chunks = 2 * parts + 8
    hbm = pl.BlockSpec(memory_space=pl.ANY)
    vmem = pl.BlockSpec(memory_space=VM)
    smem = pl.BlockSpec(memory_space=pltpu.SMEM)
    shape = jax.ShapeDtypeStruct
    seg_out, in_grad, norms, a_fac, b_fac = pl.pallas_call(
        functools.partial(layer_kernel, sections),
        out_shape=(
            shape((1, micro, half, depth), BF),
            shape((1, micro, half, depth), BF),
            shape((8, depth), F32),
            shape((7, rows, depth), BF),
            shape((chunks, rows, CHUNK), BF),
        ),
        in_specs=[hbm, hbm, hbm, smem, hbm, hbm, vmem, vmem, hbm, hbm, vmem, vmem, hbm, hbm, vmem, vmem],
        out_specs=(vmem, vmem, vmem, hbm, hbm),
        scratch_shapes=[
            VM((3, depth, heads), BF),
            VM((depth, heads), BF),
            VM((depth, width), BF),
            VM((depth, width), BF),
            VM((3, depth, heads), BF),
            VM((depth, heads), BF),
            VM((7, rows, depth), BF),
            VM((chunks, rows, CHUNK), BF),
            VM((3, rows, heads), BF),
            VM((3, rows, heads), BF),
            VM((rows, depth), BF),
            VM((rows, depth), BF),
            VM((rows, depth), BF),
            VM((rows, 1), F32),
            VM((rows, 1), F32),
            VM((rows, 1), F32),
            VM((rows, depth), F32),
            VM((parts, rows, CHUNK), BF),
            VM((rows, depth), BF),
            VM((rows, heads), BF),
            VM((rows, depth), BF),
            VM((3, rows, depth), BF),
            VM((2, micro, half, depth), BF),
            VM((micro, half, depth), F32),
            VM((2, micro, half, depth), BF),
            VM((6, 8, depth), F32),
            pltpu.SemaphoreType.DMA((6,)),
            pltpu.SemaphoreType.DMA((12,)),
            pltpu.SemaphoreType.DMA((5, micro)),
            pltpu.SemaphoreType.DMA((5, micro)),
            pltpu.SemaphoreType.DMA((6, micro)),
            pltpu.SemaphoreType.DMA((6, micro)),
            pltpu.SemaphoreType.DMA((2,)),
        ],
        compiler_params=pltpu.CompilerParams(
            collective_id=0, has_side_effects=True, vmem_limit_bytes=60 * 2**20
        ),
        name="layers",
    )(
        inputs,
        target_inputs,
        cotangent,
        slot_counts,
        w_qkv,
        w_out,
        norm1_gain,
        norm1_bias,
        w_up,
        w_down,
        norm2_gain,
        norm2_bias,
        cross_qkv,
        cross_out,
        norm3_gain[None],
        norm3_bias[None],
    )
    decoder = lax.axis_index("section") == sections - 1

    def weight_grad(left, first, count):
        return jnp.einsum(
            "nd,tnc->tdc", a_fac[left], b_fac[first : first + count], preferred_element_type=F32
        ).astype(BF)

    def shared(grad, axes, dim):
        return lax.psum_scatter(grad, axes, scatter_dimension=dim, tiled=True)

    def wide(grad):
        return jnp.swapaxes(grad, 0, 1).reshape(depth, -1)

    grad_down = shared(wide(weight_grad(0, 0, parts)), "dp", 0)
    grad_up = shared(wide(weight_grad(1, parts, parts)), "dp", 0)
    grad_out = shared(weight_grad(2, 2 * parts, 1)[0], "dp", 0)
    grad_qkv = shared(weight_grad(3, 2 * parts + 1, 3), "dp", 1)
    cross = jnp.concatenate(
        [
            weight_grad(4, 2 * parts + 4, 1),
            weight_grad(5, 2 * parts + 5, 2),
            weight_grad(6, 2 * parts + 7, 1),
        ],
        0,
    )
    cross = shared(jnp.where(decoder, cross, jnp.zeros_like(cross)), ("section", "dp"), 1)
    small = shared(norms[:4], "dp", 1)
    norm3 = jnp.where(decoder, norms[4:6], jnp.zeros_like(norms[4:6]))
    norm3 = shared(norm3, ("section", "dp"), 1)
    return (
        seg_out,
        in_grad,
        grad_qkv[None].astype(F32),
        grad_out[None].astype(F32),
        small[0:1],
        small[1:2],
        grad_up[None].astype(F32),
        grad_down[None].astype(F32),
        small[2:3],
        small[3:4],
        cross[:3].astype(F32),
        cross[3].astype(F32),
        norm3[0],
        norm3[1],
    )


def solution(mesh):
    return jax.shard_map(
        functools.partial(body, mesh.shape["section"]),
        mesh=mesh,
        in_specs=(
            P(None, ("dp", "mp"), None),
            P(None, ("dp", "mp"), None),
            P(None, ("dp", "mp"), None),
            P(),
            P("section", None, None, "mp"),
            P("section", None, "mp"),
            P("section", None),
            P("section", None),
            P("section", None, "mp"),
            P("section", None, "mp"),
            P("section", None),
            P("section", None),
            P(None, None, "mp"),
            P(None, "mp"),
            P(),
            P(),
        ),
        out_specs=(
            P("section", None, ("dp", "mp"), None),
            P("section", None, ("dp", "mp"), None),
            P("section", None, "dp", "mp"),
            P("section", "dp", "mp"),
            P("section", "dp"),
            P("section", "dp"),
            P("section", "dp", "mp"),
            P("section", "dp", "mp"),
            P("section", "dp"),
            P("section", "dp"),
            P(None, ("section", "dp"), "mp"),
            P(("section", "dp"), "mp"),
            P(("section", "dp")),
            P(("section", "dp")),
        ),
        check_vma=False,
    )
```

time: 1590 us -> 766 us (0.48)
  waiting for transfers between devices: 853 us -> 558 us
  matrix products: 302 us -> 25.4 us
  blocking collectives: 125 us -> 0 us
  local copies, waits for them, and re-layouts: 159 us -> 50.6 us
  Pallas kernels: 0 us -> 105 us
  other arithmetic: 99.9 us -> 9.5 us
  starting transfers between devices: 21.1 us -> 0.51 us
    reduce_scatter x5 -> x2, waiting for transfers between devices: 574 us -> 177 us  [shared(): return lax.psum_scatter(grad, axes, scatter_dimension=dim, tiled=True)]
    unnamed x22 -> x12, waiting for transfers between devices: 129 us -> 381 us
    dot_general x116 -> x7, matrix products: 263 us -> 25.4 us  [weight_grad(): jnp.einsum('nd,tnc->tdc', a_fac[left], b_fac[first:first + count], prefer...]
    psum x15 -> x0, waiting for transfers between devices: 141 us -> none  [the longest x5 51.7 us: forward_segment(): lax.psum(jnp.einsum('nc,dc->nd', cross_mixed, cross_out, preferred_elemen...]
    pallas_call x0 -> x1, Pallas kernels: none -> 105 us  [body(): pl.pallas_call(functools.partial(layer_kernel, sections), out_shape=(shap...]
    unnamed x2 -> x0, blocking collectives: 77.9 us -> none
    reduce_sum x51 -> x0, other arithmetic: 65.1 us -> none  [the longest x22 26.4 us: layer_norm(): center = values - jnp.mean(values, -1, keepdims=True)]
    slice x42 -> x3, local copies, waits for them, and re-layouts: 62 us -> 2.76 us  [the longest x1 1.09 us: body(): small[3:4]]
  transfers between devices with their start and end apart: 27 -> 7, of which waited for: 21 -> 7; matrix products, arithmetic and copies ran while one was open for 21% -> 10% of each run, Pallas kernels for 0% -> 0%
where the time goes in v1:
time: 766 us; the launch traced here: 764 us
  waiting for transfers between devices  558 us (73%)
  Pallas kernels  105 us (14%)
  local copies, waits for them, and re-layouts  50.6 us (7%)
  matrix products  25.4 us (3%)
  between operations  14.9 us (2%)
  other arithmetic  9.5 us (1%)
    unnamed x12, waiting for transfers between devices  381 us
    reduce_scatter x2, waiting for transfers between devices, shared(): return lax.psum_scatter(grad, axes, scatter_dimension=dim, tiled=True)  177 us
    pallas_call x1, Pallas kernels, body(): pl.pallas_call(functools.partial(layer_kernel, sections), out_shape=(shap...  105 us
    unnamed x27, local copies, waits for them, and re-layouts  26.9 us
    dot_general x7, matrix products, weight_grad(): jnp.einsum('nd,tnc->tdc', a_fac[left], b_fac[first:first + count], prefer...  25.4 us
  transfers between devices with their start and end apart: 7, of which 7 were waited for; matrix products, arithmetic and copies ran while one was open for 10% of the time, Pallas kernels for 0%

profile of v1, /device:TPU:0, one launch (start us, length us, event | category | flops | bytes accessed | tf_op | source)
XLA Modules:
  0.0 764.4 jit_solution(11352767128969929331)
XLA Ops:
  7.2 0.0 reduce-scatter.25.cloned.1.call-start
  7.2 105.4 %layers.1 = (bf16[1,2,128,1024]{3,2,1,0:T(8,128)(2,1)}, bf16[1,2,128,1024]{3,2,1,0:T(8,128)(2,1)}, f32[8,1024]{1,0:T(8,128)}, bf16[7,512,1024]{2,1,0:T(8,128)(2,1)}, bf16[16,512,512]{2,1,0:T(8,128)(2,1)}) custom-call(bf16[2,128,1024]{2,1,0:T(8,128)(2,1)} %inputs.1, bf16[2,128,1024]{2,1,0:T(8,128)(2,1)} %targets.1, bf16[2,128,1024]{2,1,0:T(8,128)(2,1)} %cotangent.1, ...), custom_call_target="tpu_custom_call" | custom-call | tf_op jit(solution)/shard_map/layers/pallas_call | solution.py:644
  112.7 0.8 slice_select_fusion
  113.4 1.0 copy.60
  114.5 0.0 reduce-scatter.25.cloned.1.call-update
  114.5 0.0 reduce-scatter.23.cloned.1.call-start
  114.5 0.8 slice.76
  115.3 1.0 copy.58
  116.3 0.0 reduce-scatter.23.cloned.1.call-update
  116.4 0.0 reduce-scatter.21.cloned.1.call-start
  116.4 2.1 fusion.2
  118.5 1.3 copy.56
  119.9 0.0 reduce-scatter.21.cloned.1.call-update
  119.9 0.0 all-reduce.3.cloned.1.call-start
  119.9 2.1 fusion.4
  122.1 2.1 fusion.3
  124.2 2.8 convert_bitcast_fusion.1
  127.0 2.3 maximum_select_fusion
  129.3 7.9 %copy.46 = bf16[4,1024,512]{2,0,1:T(4,128)(2,1)} copy(bf16[4,1024,512]{1,2,0:T(8,128)(2,1)} %maximum_select_fusion) | data formatting | bytes 8388608 | tf_op jit(solution)/shard_map/jit(_where)/select_n | solution.py:737
  137.2 0.0 all-reduce.3.cloned.1.call-update
  137.2 0.0 reduce-scatter.19.cloned.1.call-start
  137.3 3.5 convert_bitcast_fusion
  140.8 5.7 copy.54
  146.5 4.9 copy.69
  151.5 0.0 reduce-scatter.19.cloned.1.call-update
  151.5 0.3 reduce-scatter.15.cloned.1.call-start
  151.8 6.3 convolution_convert_fusion.1
  158.1 6.5 copy.42
  164.6 0.0 reduce-scatter.15.cloned.1.call-update
  164.7 0.0 reduce-scatter.17.cloned.1.call-start
  164.7 6.3 convolution_convert_fusion
  171.1 6.5 copy.44
  177.6 0.0 reduce-scatter.17.cloned.1.call-update
  177.6 0.6 copy-done.2
  178.3 0.6 dynamic-slice
  179.5 12.1 %reduce-scatter.25.cloned.1.call-done = f32[64,2]{1,0:T(8,128)} async-done(((f32[1024,2]{1,0:T(8,128)}), f32[64,2]{1,0:T(8,128)}) %reduce-scatter.25.cloned.1.call-update) | async-done | bytes 528
  191.5 0.9 fusion.26
  192.4 0.6 copy.68
  193.0 0.6 copy.67
  193.6 60.4 %reduce-scatter.23.cloned.1.call-done = f32[128,4]{1,0:T(8,128)} async-done(((f32[1024,4]{1,0:T(8,128)}), f32[128,4]{1,0:T(8,128)}) %reduce-scatter.23.cloned.1.call-update) | async-done | bytes 2064
  254.0 1.1 fusion.25
  255.1 0.6 copy.66
  255.7 0.6 copy.65
  256.3 0.6 copy.64
  256.9 0.6 copy.63
  257.5 63.0 %reduce-scatter.21.cloned.1.call-done = bf16[128,512]{1,0:T(8,128)(2,1)} async-done(((bf16[1024,512]{1,0:T(8,128)(2,1)}), bf16[128,512]{1,0:T(8,128)(2,1)}) %reduce-scatter.21.cloned.1.call-update) | async-done | bytes 131088
  320.5 1.0 copy.57
  321.6 0.8 copy.48
  322.4 171.8 %all-reduce.3.cloned.1.call-done = bf16[4,1024,512]{2,0,1:T(4,128)(2,1)} async-done(((bf16[4,1024,512]{2,0,1:T(4,128)(2,1)}), bf16[4,1024,512]{2,0,1:T(4,128)(2,1)}) %all-reduce.3.cloned.1.call-update) | async-done | bytes 4194320
  494.2 1.0 dynamic-slice_convert_fusion
  495.2 0.9 copy.49
  496.1 1.1 dynamic-slice_convert_fusion.1
  497.2 0.7 copy.71
  497.9 73.2 %reduce-scatter.19.cloned.1.call-done = bf16[128,1536]{1,0:T(8,128)(2,1)} async-done(((bf16[1024,1536]{1,0:T(8,128)(2,1)}), bf16[128,1536]{1,0:T(8,128)(2,1)}) %reduce-scatter.19.cloned.1.call-update) | async-done | bytes 393232
  571.1 1.7 reshape.74
  572.8 0.3 copy.55
  573.1 0.1 bitcast_convert_fusion.2
  573.2 1.1 copy.47
  574.3 87.6 %reduce-scatter.15.cloned.1.call-done = bf16[128,2048]{1,0:T(8,128)(2,1)} async-done(((bf16[1024,2048]{1,0:T(8,128)(2,1)}), bf16[128,2048]{1,0:T(8,128)(2,1)}) %reduce-scatter.15.cloned.1.call-update) | async-done | bytes 524304 | tf_op jit(solution)/shard_map/reduce_scatter | solution.py:720
  662.0 2.1 bitcast_convert_fusion.1
  664.1 89.8 %reduce-scatter.17.cloned.1.call-done = bf16[128,2048]{1,0:T(8,128)(2,1)} async-done(((bf16[1024,2048]{1,0:T(8,128)(2,1)}), bf16[128,2048]{1,0:T(8,128)(2,1)}) %reduce-scatter.17.cloned.1.call-update) | async-done | bytes 524304 | tf_op jit(solution)/shard_map/reduce_scatter | solution.py:720
  753.9 2.1 bitcast_convert_fusion
  756.0 0.8 copy.75
  756.8 0.8 copy.76
  (6 shorter events, 0.0 us)
Async XLA Ops:
  7.2 184.4 %reduce-scatter.25.cloned.1.call-start = ((), (), s32[]{:S(2)}) async-start(), calls=%async_computation.11 | async-start | bytes 557056
  114.5 139.6 %reduce-scatter.23.cloned.1.call-start = ((), (), s32[]{:S(2)}) async-start(), calls=%async_computation.10 | async-start | bytes 589824
  116.4 204.1 %reduce-scatter.21.cloned.1.call-start = ((), (), s32[]{:S(2)}) async-start(), calls=%async_computation.9 | async-start | bytes 1179648
  119.9 374.3 %all-reduce.3.cloned.1.call-start = ((), (), s32[]{:S(2)}) async-start(), calls=%async_computation.12 | async-start | bytes 8388608
  137.2 433.9 %reduce-scatter.19.cloned.1.call-start = ((), (), s32[]{:S(2)}) async-start(), calls=%async_computation.8 | async-start | bytes 3538944
  151.5 510.4 %reduce-scatter.15.cloned.1.call-start = ((), (), s32[]{:S(2)}) async-start(), calls=%async_computation.6 | async-start | bytes 4718592 | tf_op jit(solution)/shard_map/reduce_scatter | solution.py:720
  164.7 589.2 %reduce-scatter.17.cloned.1.call-start = ((), (), s32[]{:S(2)}) async-start(), calls=%async_computation.7 | async-start | bytes 4718592 | tf_op jit(solution)/shard_map/reduce_scatter | solution.py:720
  177.6 0.7 copy-start.2
  496.1 259.9 %copy-start.1 = (bf16[1,2,128,1024]{3,2,1,0:T(8,128)(2,1)S(1)}, bf16[1,2,128,1024]{3,2,1,0:T(8,128)(2,1)}, u32[]{:S(2)}) copy-start(bf16[1,2,128,1024]{3,2,1,0:T(8,128)(2,1)} %get-tuple-element.72) | copy-start | bytes 1572868
  497.9 258.9 %copy-start = (bf16[1,2,128,1024]{3,2,1,0:T(8,128)(2,1)S(1)}, bf16[1,2,128,1024]{3,2,1,0:T(8,128)(2,1)}, u32[]{:S(2)}) copy-start(bf16[1,2,128,1024]{3,2,1,0:T(8,128)(2,1)} %get-tuple-element.73) | copy-start | bytes 1572868
Sparse Core Ops, SparseCore 0:
  114.6 76.8 reduce-scatter.24
  195.8 58.1 reduce-scatter.22
  258.0 62.4 reduce-scatter.20
  326.9 167.2 all-reduce.2
  497.6 73.4 reduce-scatter.18
  574.6 87.3 reduce-scatter.14
  666.0 87.8 reduce-scatter.16

commit v2 on v1

--- a/solution.py
+++ b/solution.py
@@ -109,8 +109,379 @@
     return scale * (d_unit - first - unit * second)
 
 
+class GradientShare:
+    AHEAD = 8
+    WINDOW = 4
+    DEPTH = 6
+    FINAL = 8
+
+    def __init__(self, size, section, dp, core, decoder, a_fac, b_fac, tiles, w_up, w_down, w_cross, slope, resid, *share):
+        (self.pair_got, self.acc, self.nb, self.pair_send, self.pair_recv, self.line_send, self.line_recv,
+         self.cross_send, self.cross_recv, self.norm_send, self.norm_recv, self.final_sem,
+         self.pair_credit, self.left_credit, self.right_credit, self.cross_credit) = share
+        self.line = size // 2
+        self.section, self.dp, self.core = section, dp, core
+        self.decoder, self.encoder = decoder, jnp.logical_not(decoder)
+        self.z, self.y = dp // 2, lax.rem(dp, 2)
+        self.a_fac, self.b_fac, self.tiles = a_fac, b_fac, tiles
+        self.w_up, self.w_down, self.w_cross, self.slope, self.resid = w_up, w_down, w_cross, slope, resid
+        self.rows = a_fac.shape[2] // size
+        self.own_chunks = b_fac.shape[0] - 4
+        self.chunks = self.own_chunks + 2
+        self.partner = (section, dp + 1 - 2 * self.y, core)
+        self.right = (section, dp + 2, core)
+        self.left = (section, dp - 2, core)
+        self.across = (1 - section, dp, core)
+        self.has_left, self.has_right = self.z > 0, self.z < self.line - 1
+
+    def greet(self, barrier):
+        pl.semaphore_signal(barrier, inc=1, device_id=self.partner, device_id_type=MESH)
+
+        @pl.when(self.has_left)
+        def _():
+            pl.semaphore_signal(barrier, inc=1, device_id=self.left, device_id_type=MESH)
+
+        @pl.when(self.has_right)
+        def _():
+            pl.semaphore_signal(barrier, inc=1, device_id=self.right, device_id_type=MESH)
+
+        return 1 + jnp.where(self.has_left, 1, 0) + jnp.where(self.has_right, 1, 0)
+
+    def tile_rows(self, k):
+        return pl.ds(pl.multiple_of(k * self.rows, self.rows), self.rows)
+
+    def cols(self, k):
+        return pl.ds(pl.multiple_of(k * CHUNK, CHUNK), CHUNK)
+
+    def pair_slot(self, i, k):
+        return self.w_down.at[self.tile_rows(lax.rem(i, self.AHEAD)), self.cols(k)]
+
+    def pair_copy(self, i, k):
+        slot = lax.rem(i, self.AHEAD) * self.line + k
+        return pltpu.make_async_remote_copy(
+            src_ref=self.pair_slot(i, k),
+            dst_ref=self.pair_got.at[slot],
+            send_sem=self.pair_send.at[slot],
+            recv_sem=self.pair_recv.at[slot],
+            device_id=self.partner,
+            device_id_type=MESH,
+        )
+
+    def line_slot(self, i, k):
+        slot = lax.rem(i, self.DEPTH) * self.line + k
+        return self.w_cross.at[slot // 8, self.tile_rows(lax.rem(slot, 8))]
+
+    def line_got(self, side, i, k):
+        return self.w_up.at[self.tile_rows(lax.rem(i, self.WINDOW) * 2 + side), self.cols(k)]
+
+    def line_copy(self, side, i, k):
+        return pltpu.make_async_remote_copy(
+            src_ref=self.line_slot(i, k),
+            dst_ref=self.line_got(side, i, k),
+            send_sem=self.line_send.at[lax.rem(i, self.DEPTH) * self.line + k],
+            recv_sem=self.line_recv.at[side, lax.rem(i, self.WINDOW) * self.line + k],
+            device_id=self.left if side else self.right,
+            device_id_type=MESH,
+        )
+
+    def cross_copy(self, q):
+        return pltpu.make_async_remote_copy(
+            src_ref=self.slope.at[q],
+            dst_ref=self.slope.at[q],
+            send_sem=self.cross_send.at[q],
+            recv_sem=self.cross_recv.at[q],
+            device_id=self.across,
+            device_id_type=MESH,
+        )
+
+    def own_tile(self, i, k, y):
+        main = i < self.own_chunks
+
+        @pl.when(main)
+        def _():
+            left = jnp.minimum(i // 4, 2) + jnp.where(i > 8, 1, 0)
+            shard = k * 2 + y
+            self.acc[...] = dot_tn(self.a_fac[left, :, self.tile_rows(shard)], self.b_fac[i])
+
+        first = (i - self.own_chunks) * 2
+        small = self.rows // 2
+
+        @pl.when(jnp.logical_not(main) & self.decoder)
+        def _():
+            base = self.a_fac.shape[2] // 2
+            for e in range(2):
+                q = first + e
+                block = dot_tn(
+                    self.a_fac[4 + (q + 1) // 2, :, pl.ds(pl.multiple_of(base + k * self.rows, self.rows), self.rows)],
+                    self.b_fac[self.own_chunks + q],
+                )
+                self.acc[e * small : (e + 1) * small] = jnp.where(y == 0, block[:small], block[small:])
+
+        @pl.when(jnp.logical_not(main) & self.encoder)
+        def _():
+            for e in range(2):
+                place = pl.ds(pl.multiple_of(k * self.rows + y * small, small), small)
+                self.acc[e * small : (e + 1) * small] = self.slope[first + e, place].astype(F32)
+
+    def pair_step(self, i):
+        @pl.when(i >= self.AHEAD)
+        def _():
+            pl.semaphore_wait(self.pair_credit, 1)
+
+        @pl.when((i >= self.own_chunks) & self.encoder)
+        def _():
+            for e in range(2):
+                self.cross_copy((i - self.own_chunks) * 2 + e).wait_recv()
+
+        def one(k):
+            @pl.when(i >= self.AHEAD)
+            def _():
+                self.pair_copy(i, k).wait_send()
+
+            self.own_tile(i, k, 1 - self.y)
+            slot = self.pair_slot(i, k)
+            slot[...] = self.acc[...].astype(BF)
+            self.pair_copy(i, k).start()
+
+        loop(self.line, one)
+
+    def begin(self):
+        @pl.when(self.has_left)
+        def _():
+            pl.semaphore_signal(self.right_credit, inc=self.WINDOW, device_id=self.left, device_id_type=MESH)
+
+        @pl.when(self.has_right)
+        def _():
+            pl.semaphore_signal(self.left_credit, inc=self.WINDOW, device_id=self.right, device_id_type=MESH)
+
+        @pl.when(self.encoder)
+        def _():
+            pl.semaphore_signal(self.cross_credit, inc=1, device_id=self.across, device_id_type=MESH)
+
+        loop(self.AHEAD, self.pair_step)
+
+    def line_step(self, i):
+        @pl.when(self.has_right)
+        def _():
+            pl.semaphore_wait(self.right_credit, 1)
+
+        @pl.when(self.has_left)
+        def _():
+            pl.semaphore_wait(self.left_credit, 1)
+
+        def partial(k):
+            self.own_tile(i, k, self.y)
+            self.pair_copy(i, k).wait_recv()
+            slot = lax.rem(i, self.AHEAD) * self.line + k
+            self.acc[...] += self.pair_got[slot].astype(F32)
+
+        def arrived(side, k):
+            self.line_copy(side, i, k).wait_recv()
+            self.acc[...] += self.line_got(side, i, k)[...].astype(F32)
+
+        def send(side, k, inner):
+            @pl.when(i >= self.DEPTH)
+            def _():
+                self.line_copy(side, i, k).wait_send()
+
+            partial(k)
+
+            @pl.when(inner)
+            def _():
+                arrived(side, k)
+
+            slot = self.line_slot(i, k)
+            slot[...] = self.acc[...].astype(BF)
+            self.line_copy(side, i, k).start()
+
+        def to_right(j):
+            k = self.line - 1 - j
+
+            @pl.when(k > self.z)
+            def _():
+                send(0, k, self.has_left)
+
+        def to_left(k):
+            @pl.when(k < self.z)
+            def _():
+                send(1, k, self.has_right)
+
+        loop(self.line - 1, to_right)
+        loop(self.line - 1, to_left)
+        partial(self.z)
+
+        @pl.when(self.has_left)
+        def _():
+            arrived(0, self.z)
+
+        @pl.when(self.has_right)
+        def _():
+            arrived(1, self.z)
+
+        @pl.when(i >= self.FINAL)
+        def _():
+            self.final_copy(i).wait()
+
+        slot = self.final_slot(i)
+        slot[...] = self.acc[...]
+        self.final_copy(i).start()
+
+        @pl.when(i + self.WINDOW < self.chunks)
+        def _():
+            @pl.when(self.has_left)
+            def _():
+                pl.semaphore_signal(self.right_credit, inc=1, device_id=self.left, device_id_type=MESH)
+
+            @pl.when(self.has_right)
+            def _():
+                pl.semaphore_signal(self.left_credit, inc=1, device_id=self.right, device_id_type=MESH)
+
+        @pl.when(i + self.AHEAD < self.chunks)
+        def _():
+            pl.semaphore_signal(self.pair_credit, inc=1, device_id=self.partner, device_id_type=MESH)
+            self.pair_step(i + self.AHEAD)
+
+    def final_slot(self, i):
+        slot = lax.rem(i, self.FINAL)
+        return self.resid.at[self.tile_rows(slot // 2), self.cols(lax.rem(slot, 2))]
+
+    def final_copy(self, i):
+        return pltpu.make_async_copy(
+            self.final_slot(i), self.tiles.at[i], self.final_sem.at[lax.rem(i, self.FINAL)]
+        )
+
+    def cross_part(self):
+        @pl.when(self.decoder)
+        def _():
+            pl.semaphore_wait(self.cross_credit, 1)
+
+            def one(q):
+                def tile(k):
+                    self.slope[q, self.tile_rows(k)] = dot_tn(
+                        self.a_fac[4 + (q + 1) // 2, :, self.tile_rows(k)],
+                        self.b_fac[self.own_chunks + q],
+                    ).astype(BF)
+
+                loop(4, tile)
+                self.cross_copy(q).start()
+
+            loop(4, one)
+
+    def norm_copy(self, src, dst, device):
+        return pltpu.make_async_remote_copy(
+            src_ref=self.nb.at[src],
+            dst_ref=self.nb.at[dst],
+            send_sem=self.norm_send.at[dst],
+            recv_sem=self.norm_recv.at[dst],
+            device_id=device,
+            device_id_type=MESH,
+        )
+
+    def norms(self, sums, norm_out, norm3_out):
+        nb, has_left, has_right = self.nb, self.has_left, self.has_right
+        for i in range(6):
+            nb[0, i : i + 1] = jnp.sum(sums[i], 0, keepdims=True)
+        nb[0, 6:8] = jnp.zeros_like(nb[0, 6:8])
+        to_right = self.norm_copy(3, 1, self.right)
+        to_left = self.norm_copy(4, 2, self.left)
+        nb[3] = nb[0]
+        nb[4] = nb[0]
+        nb[5] = nb[0]
+
+        @pl.when(jnp.logical_not(has_left))
+        def _():
+            to_right.start()
+
+        @pl.when(jnp.logical_not(has_right))
+        def _():
+            to_left.start()
+
+        @pl.when(has_left)
+        def _():
+            to_right.wait_recv()
+            nb[5] += nb[1]
+
+            @pl.when(has_right)
+            def _():
+                nb[3] += nb[1]
+                to_right.start()
+
+        @pl.when(has_right)
+        def _():
+            to_left.wait_recv()
+            nb[5] += nb[2]
+
+            @pl.when(has_left)
+            def _():
+                nb[4] += nb[2]
+                to_left.start()
+
+        self.norm_copy(5, 6, self.partner).start()
+        self.norm_out, self.norm3_out = norm_out, norm3_out
+
+    def finish_norms(self):
+        nb = self.nb
+        self.norm_copy(5, 6, self.partner).wait()
+
+        @pl.when(self.has_right)
+        def _():
+            self.norm_copy(3, 1, self.right).wait_send()
+
+        @pl.when(self.has_left)
+        def _():
+            self.norm_copy(4, 2, self.left).wait_send()
+
+        nb[7] = nb[5] + nb[6]
+        hand = self.norm_copy(7, 8, self.across)
+
+        @pl.when(self.decoder)
+        def _():
+            hand.start()
+            nb[8] = nb[7]
+
+        self.norm_out[...] = nb[7, :, pl.ds(pl.multiple_of(self.dp * 128, 128), 128)]
+
+        @pl.when(self.encoder)
+        def _():
+            hand.wait_recv()
+
+        place = self.section * self.line * 2 + self.dp
+        block = nb[8, :, pl.ds(pl.multiple_of(place // 2 * 128, 128), 128)]
+        self.norm3_out[...] = jnp.where(self.y == 0, block, pltpu.roll(block, 64, 1))
+
+        @pl.when(self.decoder)
+        def _():
+            hand.wait_send()
+
+    def run(self):
+        loop(self.chunks - 2, self.line_step)
+        self.finish_norms()
+        loop(2, lambda p: self.line_step(self.chunks - 2 + p))
+
+    def drain(self):
+        for slot in range(self.AHEAD):
+            for k in range(self.line):
+                self.pair_copy(slot, k).wait_send()
+
+        for slot in range(self.DEPTH):
+            for k in range(self.line):
+
+                @pl.when(self.z != k)
+                def _():
+                    self.line_copy(0, slot, k).wait_send()
+
+        for slot in range(self.FINAL):
+            self.final_copy(slot).wait()
+
+        @pl.when(self.decoder)
+        def _():
+            for q in range(4):
+                self.cross_copy(q).wait_send()
+
+
 def layer_kernel(
     sections,
+    ring,
     inputs,
     targets,
     cotangent,
@@ -130,8 +501,8 @@
     seg_out,
     in_grad,
     norm_out,
-    a_out,
-    b_out,
+    first_out,
+    second_out,
     w_qkv,
     w_out,
     w_up,
@@ -165,6 +536,7 @@
     hop_send,
     hop_recv,
     out_sem,
+    *share,
 ):
     section = lax.axis_index("section")
     dp = lax.axis_index("dp")
@@ -204,6 +576,11 @@
     barrier = pltpu.get_barrier_semaphore()
     for device in (mate, across):
         pl.semaphore_signal(barrier, inc=1, device_id=device, device_id_type=MESH)
+    if ring:
+        total = GradientShare(ring, section, dp, core, decoder, a_fac, b_fac, first_out, w_up, w_down, w_cross, slope, resid, *share)
+        greeted = 2 + total.greet(barrier)
+    else:
+        greeted = 2
 
     loads = [
         pltpu.make_async_copy(src, dst, load_sem.at[i])
@@ -254,7 +631,7 @@
 
     loads[0].start()
     loads[1].start()
-    pl.semaphore_wait(barrier, 2)
+    pl.semaphore_wait(barrier, greeted)
 
     def mate_start(src, dst, base):
         for m in range(2):
@@ -477,6 +854,8 @@
         exchange(3, 0, m).start()
 
     loop(2, feed_backward)
+    if ring:
+        total.begin()
 
     def cross_backward(m):
         rows = rows_of(m)
@@ -599,12 +978,19 @@
         for m in range(2):
             across_copy(half_send.at[0, m], d_out, 2, m).wait_send()
 
+    if ring:
+        total.norms(sums, norm_out, second_out)
+        total.cross_part()
+        total.run()
+        total.drain()
+        return
+
     for i in range(6):
         norm_out[i : i + 1] = jnp.sum(sums[i], 0, keepdims=True)
     norm_out[6:8] = jnp.zeros_like(norm_out[6:8])
     copies = [
-        pltpu.make_async_copy(a_fac, a_out, out_sem.at[0]),
-        pltpu.make_async_copy(b_fac, b_out, out_sem.at[1]),
+        pltpu.make_async_copy(a_fac, first_out, out_sem.at[0]),
+        pltpu.make_async_copy(b_fac, second_out, out_sem.at[1]),
     ]
     for copy in copies:
         copy.start()
@@ -614,6 +1000,7 @@
 
 def body(
     sections,
+    ring,
     inputs,
     target_inputs,
     cotangent,
@@ -641,17 +1028,54 @@
     vmem = pl.BlockSpec(memory_space=VM)
     smem = pl.BlockSpec(memory_space=pltpu.SMEM)
     shape = jax.ShapeDtypeStruct
-    seg_out, in_grad, norms, a_fac, b_fac = pl.pallas_call(
-        functools.partial(layer_kernel, sections),
+    if ring:
+        results = (
+            shape((8, depth // ring), F32),
+            shape((chunks - 2, depth // ring, CHUNK), F32),
+            shape((8, depth // ring), F32),
+        )
+        places = (vmem, hbm, vmem)
+    else:
+        results = (
+            shape((8, depth), F32),
+            shape((7, rows, depth), BF),
+            shape((chunks, rows, CHUNK), BF),
+        )
+        places = (vmem, hbm, hbm)
+    dma = pltpu.SemaphoreType.DMA
+    regular = pltpu.SemaphoreType.REGULAR
+    tile = (depth // ring, CHUNK) if ring else None
+    share = (
+        [
+            VM((GradientShare.AHEAD * 4,) + tile, BF),
+            VM(tile, F32),
+            VM((9, 8, depth), F32),
+            dma((GradientShare.AHEAD * 4,)),
+            dma((GradientShare.AHEAD * 4,)),
+            dma((GradientShare.DEPTH * 4,)),
+            dma((2, GradientShare.WINDOW * 4)),
+            dma((4,)),
+            dma((4,)),
+            dma((9,)),
+            dma((9,)),
+            dma((GradientShare.FINAL,)),
+            regular,
+            regular,
+            regular,
+            regular,
+        ]
+        if ring
+        else []
+    )
+    seg_out, in_grad, norms, first, second = pl.pallas_call(
+        functools.partial(layer_kernel, sections, ring),
         out_shape=(
             shape((1, micro, half, depth), BF),
             shape((1, micro, half, depth), BF),
-            shape((8, depth), F32),
-            shape((7, rows, depth), BF),
-            shape((chunks, rows, CHUNK), BF),
-        ),
+        )
+        + results,
         in_specs=[hbm, hbm, hbm, smem, hbm, hbm, vmem, vmem, hbm, hbm, vmem, vmem, hbm, hbm, vmem, vmem],
-        out_specs=(vmem, vmem, vmem, hbm, hbm),
+        out_specs=(vmem, vmem) + places,
         scratch_shapes=[
             VM((3, depth, heads), BF),
             VM((depth, heads), BF),
@@ -686,7 +1110,8 @@
             pltpu.SemaphoreType.DMA((6, micro)),
             pltpu.SemaphoreType.DMA((6, micro)),
             pltpu.SemaphoreType.DMA((2,)),
-        ],
+        ]
+        + share,
         compiler_params=pltpu.CompilerParams(
             collective_id=0, has_side_effects=True, vmem_limit_bytes=60 * 2**20
         ),
@@ -709,6 +1134,29 @@
         norm3_gain[None],
         norm3_bias[None],
     )
+    if ring:
+        own = lambda first_one, count: jnp.swapaxes(
+            first[first_one : first_one + count], 0, 1
+        ).reshape(1, depth // ring, count * CHUNK)
+        cross = first[2 * parts + 4 :].reshape(4, depth // ring // 2, CHUNK)
+        lanes = depth // ring // 2
+        return (
+            seg_out,
+            in_grad,
+            first[None, 2 * parts + 1 : 2 * parts + 4],
+            first[2 * parts : 2 * parts + 1],
+            norms[0:1],
+            norms[1:2],
+            own(parts, parts),
+            own(0, parts),
+            norms[2:3],
+            norms[3:4],
+            cross[:3],
+            cross[3],
+            second[4, :lanes],
+            second[5, :lanes],
+        )
+    a_fac, b_fac = first, second
     decoder = lax.axis_index("section") == sections - 1
 
     def weight_grad(left, first, count):
@@ -757,8 +1205,9 @@
 
 
 def solution(mesh):
+    ring = 8 if mesh.shape["dp"] == 8 else 0
     return jax.shard_map(
-        functools.partial(body, mesh.shape["section"]),
+        functools.partial(body, mesh.shape["section"], ring),
         mesh=mesh,
         in_specs=(
             P(None, ("dp", "mp"), None),

time: 766 us -> 405 us (0.53)
  waiting for transfers between devices: 558 us -> 0 us
  Pallas kernels: 105 us -> 388 us
  local copies, waits for them, and re-layouts: 50.6 us -> 14 us
  matrix products: 25.4 us -> 0 us
  between operations: 14.9 us -> 0.71 us
  other arithmetic: 9.5 us -> 0 us
    unnamed x12 -> x0, waiting for transfers between devices: 381 us -> none
    pallas_call x1, Pallas kernels: 105 us -> 388 us  [body(): pl.pallas_call(functools.partial(layer_kernel, sections, ring), out_shape...]
    reduce_scatter x2 -> x0, waiting for transfers between devices: 177 us -> none  [shared(): return lax.psum_scatter(grad, axes, scatter_dimension=dim, tiled=True)]
    dot_general x7 -> x0, matrix products: 25.4 us -> none  [weight_grad(): jnp.einsum('nd,tnc->tdc', a_fac[left], b_fac[first:first + count], prefer...]
    unnamed x27 -> x10, local copies, waits for them, and re-layouts: 26.9 us -> 4.22 us
    reshape x2 -> x0, local copies, waits for them, and re-layouts: 13 us -> none  [wide(): return jnp.swapaxes(grad, 0, 1).reshape(depth, -1)]
    select_n x1 -> x0, local copies, waits for them, and re-layouts: 7.86 us -> none  [body(): jnp.where(decoder, cross, jnp.zeros_like(cross))]
  transfers between devices with their start and end apart: 7 -> 0, of which waited for: 7 -> 0; matrix products, arithmetic and copies ran while one was open for 10% -> 0% of each run, Pallas kernels for 0% -> 0%
where the time goes in v2:
time: 405 us; the launch traced here: 402 us
  Pallas kernels  388 us (96%)
  local copies, waits for them, and re-layouts  14 us (3%)
    pallas_call x1, Pallas kernels, body(): pl.pallas_call(functools.partial(layer_kernel, sections, ring), out_shape...  388 us

profile of v2, /device:TPU:0, one launch (start us, length us, event | category | flops | bytes accessed | tf_op | source)
XLA Modules:
  0.0 402.3 jit_solution(3054769012434020385)
XLA Ops:
  0.7 387.6 %layers.1 = (bf16[1,2,128,1024]{3,2,1,0:T(8,128)(2,1)}, bf16[1,2,128,1024]{3,2,1,0:T(8,128)(2,1)}, f32[8,128]{1,0:T(8,128)}, f32[14,128,512]{2,1,0:T(8,128)}, f32[8,128]{1,0:T(8,128)}) custom-call(bf16[2,128,1024]{2,1,0:T(8,128)(2,1)} %inputs.1, bf16[2,128,1024]{2,1,0:T(8,128)(2,1)} %targets.1, bf16[2,128,1024]{2,1,0:T(8,128)(2,1)} %cotangent.1, ...), custom_call_target="tpu_custom_call" | custom-call | tf_op jit(solution)/shard_map/layers/pallas_call | solution.py:1070
  388.3 0.0 copy-start
  388.3 1.4 slice_bitcast_fusion.4
  389.6 1.4 fusion
  391.0 1.7 slice.40
  392.7 1.1 slice.47
  393.8 0.7 slice_bitcast_fusion.3
  394.4 0.8 slice.52
  395.2 2.1 slice_bitcast_fusion.2
  397.3 0.0 copy-done
  397.3 0.2 slice_bitcast_fusion
  397.4 0.3 copy.31
  397.8 0.0 copy-start.2
  397.8 0.0 copy-start.1
  397.8 1.3 copy.33
  399.1 0.3 copy.30
  399.4 1.3 copy.32
  400.7 0.0 copy-done.2
  400.7 0.8 copy.36
  401.5 0.0 copy-done.1
  401.5 0.8 copy.37
Async XLA Ops:
  388.3 9.0 %copy-start = (f32[14,128,512]{2,1,0:T(8,128)S(1)}, f32[14,128,512]{2,1,0:T(8,128)}, u32[]{:S(2)}) copy-start(f32[14,128,512]{2,1,0:T(8,128)} %get-tuple-element.21) | copy-start | bytes 11010052
  397.8 3.0 copy-start.2
  397.8 3.8 copy-start.1

commit v3 on v2

--- a/solution.py
+++ b/solution.py
@@ -111,7 +111,7 @@
 
 class GradientShare:
     AHEAD = 8
-    WINDOW = 4
+    WINDOW = 6
     DEPTH = 6
     FINAL = 8
 
@@ -171,15 +171,19 @@
         slot = lax.rem(i, self.DEPTH) * self.line + k
         return self.w_cross.at[slot // 8, self.tile_rows(lax.rem(slot, 8))]
 
-    def line_got(self, side, i, k):
-        return self.w_up.at[self.tile_rows(lax.rem(i, self.WINDOW) * 2 + side), self.cols(k)]
-
-    def line_copy(self, side, i, k):
+    def line_place(self, side, i, k, z):
+        return lax.rem(i, self.WINDOW) * (self.line + 1) + (self.line - z + k if side else k - z)
+
+    def line_got(self, place):
+        return self.w_up.at[self.tile_rows(place // 4), self.cols(lax.rem(place, 4))]
+
+    def line_copy(self, side, i, k, receiver):
+        place = self.line_place(side, i, k, receiver)
         return pltpu.make_async_remote_copy(
             src_ref=self.line_slot(i, k),
-            dst_ref=self.line_got(side, i, k),
+            dst_ref=self.line_got(place),
             send_sem=self.line_send.at[lax.rem(i, self.DEPTH) * self.line + k],
-            recv_sem=self.line_recv.at[side, lax.rem(i, self.WINDOW) * self.line + k],
+            recv_sem=self.line_recv.at[place],
             device_id=self.left if side else self.right,
             device_id_type=MESH,
         )
@@ -260,63 +264,75 @@
 
         loop(self.AHEAD, self.pair_step)
 
-    def line_step(self, i):
-        @pl.when(self.has_right)
-        def _():
-            pl.semaphore_wait(self.right_credit, 1)
-
-        @pl.when(self.has_left)
-        def _():
-            pl.semaphore_wait(self.left_credit, 1)
-
-        def partial(k):
-            self.own_tile(i, k, self.y)
-            self.pair_copy(i, k).wait_recv()
-            slot = lax.rem(i, self.AHEAD) * self.line + k
-            self.acc[...] += self.pair_got[slot].astype(F32)
-
-        def arrived(side, k):
-            self.line_copy(side, i, k).wait_recv()
-            self.acc[...] += self.line_got(side, i, k)[...].astype(F32)
-
-        def send(side, k, inner):
-            @pl.when(i >= self.DEPTH)
-            def _():
-                self.line_copy(side, i, k).wait_send()
-
-            partial(k)
-
-            @pl.when(inner)
-            def _():
-                arrived(side, k)
-
-            slot = self.line_slot(i, k)
-            slot[...] = self.acc[...].astype(BF)
-            self.line_copy(side, i, k).start()
-
-        def to_right(j):
+    def line_step(self, t):
+        last = self.line - 1
+        self.within(t - self.z, self.has_right, self.to_right)
+        self.within(t - (last - self.z), self.has_left, self.to_left)
+        self.within(t - last, True, self.finish)
+
+    def within(self, i, more, body):
+        @pl.when((i >= 0) & (i < self.chunks) & more)
+        def _():
+            body(i)
+
+    def partial(self, i, k):
+        self.own_tile(i, k, self.y)
+        self.pair_copy(i, k).wait_recv()
+        self.acc[...] += self.pair_got[lax.rem(i, self.AHEAD) * self.line + k].astype(F32)
+
+    def arrived(self, side, i, k):
+        self.line_copy(side, i, k, self.z).wait_recv()
+        self.acc[...] += self.line_got(self.line_place(side, i, k, self.z))[...].astype(F32)
+
+    def send(self, side, i, k, inner):
+        receiver = self.z - 1 if side else self.z + 1
+
+        @pl.when(i >= self.DEPTH)
+        def _():
+            self.line_copy(side, i, k, receiver).wait_send()
+
+        self.partial(i, k)
+
+        @pl.when(inner)
+        def _():
+            self.arrived(side, i, k)
+
+        slot = self.line_slot(i, k)
+        slot[...] = self.acc[...].astype(BF)
+        self.line_copy(side, i, k, receiver).start()
+
+    def to_right(self, i):
+        pl.semaphore_wait(self.right_credit, 1)
+
+        def one(j):
             k = self.line - 1 - j
 
             @pl.when(k > self.z)
             def _():
-                send(0, k, self.has_left)
-
-        def to_left(k):
+                self.send(0, i, k, self.has_left)
+
+        loop(self.line - 1, one)
+
+    def to_left(self, i):
+        pl.semaphore_wait(self.left_credit, 1)
+
+        def one(k):
             @pl.when(k < self.z)
             def _():
-                send(1, k, self.has_right)
-
-        loop(self.line - 1, to_right)
-        loop(self.line - 1, to_left)
-        partial(self.z)
+                self.send(1, i, k, self.has_right)
+
+        loop(self.line - 1, one)
+
+    def finish(self, i):
+        self.partial(i, self.z)
 
         @pl.when(self.has_left)
         def _():
-            arrived(0, self.z)
+            self.arrived(0, i, self.z)
 
         @pl.when(self.has_right)
         def _():
-            arrived(1, self.z)
+            self.arrived(1, i, self.z)
 
         @pl.when(i >= self.FINAL)
         def _():
@@ -454,9 +470,9 @@
             hand.wait_send()
 
     def run(self):
-        loop(self.chunks - 2, self.line_step)
+        loop(self.chunks, self.line_step)
         self.finish_norms()
-        loop(2, lambda p: self.line_step(self.chunks - 2 + p))
+        loop(self.line - 1, lambda p: self.line_step(self.chunks + p))
 
     def drain(self):
         for slot in range(self.AHEAD):
@@ -468,7 +484,7 @@
 
                 @pl.when(self.z != k)
                 def _():
-                    self.line_copy(0, slot, k).wait_send()
+                    self.line_copy(0, slot, k, 0).wait_send()
 
         for slot in range(self.FINAL):
             self.final_copy(slot).wait()
@@ -1053,7 +1069,7 @@
             dma((GradientShare.AHEAD * 4,)),
             dma((GradientShare.AHEAD * 4,)),
             dma((GradientShare.DEPTH * 4,)),
-            dma((2, GradientShare.WINDOW * 4)),
+            dma((GradientShare.WINDOW * 5,)),
             dma((4,)),
             dma((4,)),
             dma((9,)),

time: 405 us -> 287 us (0.71)
  Pallas kernels: 388 us -> 272 us
    pallas_call x1, Pallas kernels: 388 us -> 272 us  [body(): pl.pallas_call(functools.partial(layer_kernel, sections, ring), out_shape...]
where the time goes in v3:
time: 287 us; the launch traced here: 286 us
  Pallas kernels  272 us (95%)
  local copies, waits for them, and re-layouts  14 us (5%)
    pallas_call x1, Pallas kernels, body(): pl.pallas_call(functools.partial(layer_kernel, sections, ring), out_shape...  272 us

profile of v3, /device:TPU:0, one launch (start us, length us, event | category | flops | bytes accessed | tf_op | source)
XLA Modules:
  0.0 286.4 jit_solution(12876427059564020887)
XLA Ops:
  0.7 271.7 %layers.1 = (bf16[1,2,128,1024]{3,2,1,0:T(8,128)(2,1)}, bf16[1,2,128,1024]{3,2,1,0:T(8,128)(2,1)}, f32[8,128]{1,0:T(8,128)}, f32[14,128,512]{2,1,0:T(8,128)}, f32[8,128]{1,0:T(8,128)}) custom-call(bf16[2,128,1024]{2,1,0:T(8,128)(2,1)} %inputs.1, bf16[2,128,1024]{2,1,0:T(8,128)(2,1)} %targets.1, bf16[2,128,1024]{2,1,0:T(8,128)(2,1)} %cotangent.1, ...), custom_call_target="tpu_custom_call" | custom-call | tf_op jit(solution)/shard_map/layers/pallas_call | solution.py:1086
  272.4 0.0 copy-start
  272.4 1.4 slice_bitcast_fusion.4
  273.8 1.4 fusion
  275.1 1.7 slice.40
  276.8 1.1 slice.47
  277.9 0.7 slice_bitcast_fusion.3
  278.5 0.8 slice.52
  279.3 2.1 slice_bitcast_fusion.2
  281.4 0.0 copy-done
  281.4 0.2 slice_bitcast_fusion
  281.5 0.3 copy.31
  281.9 0.0 copy-start.2
  281.9 0.0 copy-start.1
  281.9 1.3 copy.33
  283.2 0.3 copy.30
  283.5 1.3 copy.32
  284.8 0.0 copy-done.2
  284.8 0.8 copy.36
  285.6 0.0 copy-done.1
  285.6 0.8 copy.37
Async XLA Ops:
  272.4 9.0 %copy-start = (f32[14,128,512]{2,1,0:T(8,128)S(1)}, f32[14,128,512]{2,1,0:T(8,128)}, u32[]{:S(2)}) copy-start(f32[14,128,512]{2,1,0:T(8,128)} %get-tuple-element.21) | copy-start | bytes 11010052
  281.9 3.0 %copy-start.2 = (bf16[1,2,128,1024]{3,2,1,0:T(8,128)(2,1)S(1)}, bf16[1,2,128,1024]{3,2,1,0:T(8,128)(2,1)}, u32[]{:S(2)}) copy-start(bf16[1,2,128,1024]{3,2,1,0:T(8,128)(2,1)} %get-tuple-element.60) | copy-start | bytes 1572868
  281.9 3.8 %copy-start.1 = (bf16[1,2,128,1024]{3,2,1,0:T(8,128)(2,1)S(1)}, bf16[1,2,128,1024]{3,2,1,0:T(8,128)(2,1)}, u32[]{:S(2)}) copy-start(bf16[1,2,128,1024]{3,2,1,0:T(8,128)(2,1)} %get-tuple-element.61) | copy-start | bytes 1572868

commit v4 on v3

--- a/solution.py
+++ b/solution.py
@@ -48,48 +48,60 @@
     return first, second
 
 
-def probs_of(query, keys, mask, limit):
+def expos_of(query, keys, mask, limit):
     scores = dot_nt(query * (mask * (HEAD**-0.5)).astype(BF), keys)
     if limit is not None:
         row = lax.broadcasted_iota(jnp.int32, scores.shape, 0)
         col = lax.broadcasted_iota(jnp.int32, scores.shape, 1)
         scores = jnp.where(row + limit >= col, scores, NEG)
     expo = jnp.exp(scores - jnp.max(scores, -1, keepdims=True))
-    return expo / jnp.sum(expo, -1, keepdims=True)
-
-
-def attend_forward(proj, mixed, rows, lanes, limit):
-    query, keys, values = proj[0, rows, lanes], proj[1, rows, lanes], proj[2, rows, lanes]
+    return expo, 1.0 / jnp.sum(expo, -1, keepdims=True)
+
+
+def attend_forward(proj, mixed, rows, limit):
     masks = head_masks()
-    low = [probs_of(query, keys, mask, limit).astype(BF) for mask in masks]
-    mixed[rows, lanes] = dot_nn(
-        jnp.concatenate(low, 1), jnp.concatenate([values * mask for mask in masks], 0)
-    ).astype(BF)
-
-
-def attend_backward(proj, d_mixed, d_proj, rows, lanes, limit):
-    query, keys, values = proj[0, rows, lanes], proj[1, rows, lanes], proj[2, rows, lanes]
-    grad = d_mixed[rows, lanes]
+    for j in range(CHUNK // PAIR):
+        lanes = slice(j * PAIR, (j + 1) * PAIR)
+        query, keys, values = proj[0, rows, lanes], proj[1, rows, lanes], proj[2, rows, lanes]
+        low = []
+        for mask in masks:
+            expo, share = expos_of(query, keys, mask, limit)
+            low.append((expo * share).astype(BF))
+        mixed[rows, lanes] = dot_nn(
+            jnp.concatenate(low, 1), jnp.concatenate([values * mask for mask in masks], 0)
+        ).astype(BF)
+
+
+def attend_backward(proj, d_mixed, d_proj, rows, limit):
     masks = head_masks()
-    low, d_scores = [], []
-    for mask in masks:
-        weights = probs_of(query, keys, mask, limit)
-        d_weights = dot_nt(grad * mask, values)
-        inner = jnp.sum(weights * d_weights, -1, keepdims=True)
-        d_scores.append((weights * (d_weights - inner)).astype(BF))
-        low.append(weights.astype(BF))
     scale = HEAD**-0.5
-    d_proj[2, rows, lanes] = dot_tn(
-        jnp.concatenate(low, 0), jnp.concatenate([grad * mask for mask in masks], 0)
-    ).astype(BF)
-    d_proj[0, rows, lanes] = (
-        dot_nn(jnp.concatenate(d_scores, 1), jnp.concatenate([keys * mask for mask in masks], 0))
-        * scale
-    ).astype(BF)
-    d_proj[1, rows, lanes] = (
-        dot_tn(jnp.concatenate(d_scores, 0), jnp.concatenate([query * mask for mask in masks], 0))
-        * scale
-    ).astype(BF)
+    for j in range(CHUNK // PAIR):
+        lanes = slice(j * PAIR, (j + 1) * PAIR)
+        query, keys, values = proj[0, rows, lanes], proj[1, rows, lanes], proj[2, rows, lanes]
+        grad = d_mixed[rows, lanes]
+        low, d_scores = [], []
+        for mask in masks:
+            expo, share = expos_of(query, keys, mask, limit)
+            weights = expo * share
+            d_weights = dot_nt(grad * mask, values)
+            inner = jnp.sum(weights * d_weights, -1, keepdims=True)
+            d_scores.append((weights * (d_weights - inner)).astype(BF))
+            low.append(weights.astype(BF))
+        d_proj[2, rows, lanes] = dot_tn(
+            jnp.concatenate(low, 0), jnp.concatenate([grad * mask for mask in masks], 0)
+        ).astype(BF)
+        d_proj[0, rows, lanes] = (
+            dot_nn(
+                jnp.concatenate(d_scores, 1), jnp.concatenate([keys * mask for mask in masks], 0)
+            )
+            * scale
+        ).astype(BF)
+        d_proj[1, rows, lanes] = (
+            dot_tn(
+                jnp.concatenate(d_scores, 0), jnp.concatenate([query * mask for mask in masks], 0)
+            )
+            * scale
+        ).astype(BF)
 
 
 def norm_forward(value, gain, bias):
@@ -112,26 +124,30 @@
 class GradientShare:
     AHEAD = 8
     WINDOW = 6
-    DEPTH = 6
+    DEPTH = 4
     FINAL = 8
-
-    def __init__(self, size, section, dp, core, decoder, a_fac, b_fac, tiles, w_up, w_down, w_cross, slope, resid, *share):
-        (self.pair_got, self.acc, self.nb, self.pair_send, self.pair_recv, self.line_send, self.line_recv,
-         self.cross_send, self.cross_recv, self.norm_send, self.norm_recv, self.final_sem,
+    EARLY = 4
+
+    def __init__(self, size, section, dp, core, decoder, a_fac, b_fac, tiles, w_up, w_down, held, slope, resid, *share):
+        (self.pair_got, self.acc, self.nb, self.late_sent, self.late_got, self.late_acc, self.pair_send,
+         self.pair_recv, self.line_send, self.line_recv, self.cross_send, self.cross_recv, self.norm_send,
+         self.norm_recv, self.late_send, self.late_recv, self.factor_send, self.factor_recv, self.final_sem,
          self.pair_credit, self.left_credit, self.right_credit, self.cross_credit) = share
         self.line = size // 2
         self.section, self.dp, self.core = section, dp, core
         self.decoder, self.encoder = decoder, jnp.logical_not(decoder)
         self.z, self.y = dp // 2, lax.rem(dp, 2)
         self.a_fac, self.b_fac, self.tiles = a_fac, b_fac, tiles
-        self.w_up, self.w_down, self.w_cross, self.slope, self.resid = w_up, w_down, w_cross, slope, resid
+        self.w_up, self.w_down, self.held, self.slope, self.resid = w_up, w_down, held, slope, resid
         self.rows = a_fac.shape[2] // size
         self.own_chunks = b_fac.shape[0] - 4
-        self.chunks = self.own_chunks + 2
+        self.positions = self.own_chunks + 2 + jnp.where(decoder, 2, 0)
+        self.pairs = self.positions - self.EARLY
         self.partner = (section, dp + 1 - 2 * self.y, core)
         self.right = (section, dp + 2, core)
         self.left = (section, dp - 2, core)
         self.across = (1 - section, dp, core)
+        self.mate = (section, dp, 1 - core)
         self.has_left, self.has_right = self.z > 0, self.z < self.line - 1
 
     def greet(self, barrier):
@@ -147,56 +163,103 @@
 
         return 1 + jnp.where(self.has_left, 1, 0) + jnp.where(self.has_right, 1, 0)
 
+    def remote(self, src, dst, send, recv, device):
+        return pltpu.make_async_remote_copy(
+            src_ref=src, dst_ref=dst, send_sem=send, recv_sem=recv, device_id=device, device_id_type=MESH
+        )
+
     def tile_rows(self, k):
         return pl.ds(pl.multiple_of(k * self.rows, self.rows), self.rows)
 
     def cols(self, k):
         return pl.ds(pl.multiple_of(k * CHUNK, CHUNK), CHUNK)
 
-    def pair_slot(self, i, k):
-        return self.w_down.at[self.tile_rows(lax.rem(i, self.AHEAD)), self.cols(k)]
-
-    def pair_copy(self, i, k):
-        slot = lax.rem(i, self.AHEAD) * self.line + k
-        return pltpu.make_async_remote_copy(
-            src_ref=self.pair_slot(i, k),
-            dst_ref=self.pair_got.at[slot],
-            send_sem=self.pair_send.at[slot],
-            recv_sem=self.pair_recv.at[slot],
-            device_id=self.partner,
-            device_id_type=MESH,
-        )
-
-    def line_slot(self, i, k):
-        slot = lax.rem(i, self.DEPTH) * self.line + k
-        return self.w_cross.at[slot // 8, self.tile_rows(lax.rem(slot, 8))]
-
-    def line_place(self, side, i, k, z):
-        return lax.rem(i, self.WINDOW) * (self.line + 1) + (self.line - z + k if side else k - z)
+    def pair_slot(self, j, k):
+        return self.w_down.at[self.tile_rows(lax.rem(j, self.AHEAD)), self.cols(k)]
+
+    def pair_copy(self, j, k):
+        slot = lax.rem(j, self.AHEAD) * self.line + k
+        return self.remote(
+            self.pair_slot(j, k), self.pair_got.at[slot], self.pair_send.at[slot], self.pair_recv.at[slot], self.partner
+        )
+
+    def line_slot(self, p, k):
+        slot = lax.rem(p, self.DEPTH) * self.line + k
+        return self.held.at[slot // 8, self.tile_rows(lax.rem(slot, 4)), self.cols(lax.rem(slot // 4, 2))]
+
+    def line_place(self, side, p, k, z):
+        return lax.rem(p, self.WINDOW) * (self.line + 1) + (self.line - z + k if side else k - z)
 
     def line_got(self, place):
         return self.w_up.at[self.tile_rows(place // 4), self.cols(lax.rem(place, 4))]
 
-    def line_copy(self, side, i, k, receiver):
-        place = self.line_place(side, i, k, receiver)
-        return pltpu.make_async_remote_copy(
-            src_ref=self.line_slot(i, k),
-            dst_ref=self.line_got(place),
-            send_sem=self.line_send.at[lax.rem(i, self.DEPTH) * self.line + k],
-            recv_sem=self.line_recv.at[place],
-            device_id=self.left if side else self.right,
-            device_id_type=MESH,
+    def line_copy(self, side, p, k, receiver):
+        place = self.line_place(side, p, k, receiver)
+        return self.remote(
+            self.line_slot(p, k),
+            self.line_got(place),
+            self.line_send.at[lax.rem(p, self.DEPTH) * self.line + k],
+            self.line_recv.at[place],
+            self.left if side else self.right,
         )
 
     def cross_copy(self, q):
-        return pltpu.make_async_remote_copy(
-            src_ref=self.slope.at[q],
-            dst_ref=self.slope.at[q],
-            send_sem=self.cross_send.at[q],
-            recv_sem=self.cross_recv.at[q],
-            device_id=self.across,
-            device_id_type=MESH,
-        )
+        return self.remote(
+            self.slope.at[q], self.slope.at[q], self.cross_send.at[q], self.cross_recv.at[q], self.across
+        )
+
+    def late_copy(self, e):
+        return self.remote(
+            self.late_sent.at[e], self.late_got.at[e], self.late_send.at[e], self.late_recv.at[e], self.partner
+        )
+
+    def act_copy(self, n, m):
+        rows = pl.ds(pl.multiple_of(m * SLOT, SLOT), SLOT)
+        return self.remote(
+            self.b_fac.at[n, rows],
+            self.a_fac.at[5 + n // 2, rows, pl.ds(n % 2 * CHUNK, CHUNK)],
+            self.factor_send.at[n * 2 + m],
+            self.factor_recv.at[n * 2 + m],
+            self.partner,
+        )
+
+    def branch_copy(self, k):
+        rows = pl.ds(pl.multiple_of(self.core * SLOT, SLOT), SLOT)
+        return self.remote(
+            self.a_fac.at[0, rows, self.tile_rows(k * 2 + 1 - self.y)],
+            self.a_fac.at[4, rows, pl.ds(k * self.rows, self.rows)],
+            self.factor_send.at[8 + k],
+            self.factor_recv.at[8 + k],
+            self.partner,
+        )
+
+    def branch_forward(self):
+        rows = pl.ds(pl.multiple_of(self.core * SLOT, SLOT), SLOT)
+        part = self.a_fac.at[4, rows, pl.ds(0, CHUNK)]
+        return self.remote(part, part, self.factor_send.at[12], self.factor_recv.at[12], self.mate)
+
+    def send_act(self, m):
+        @pl.when(self.encoder)
+        def _():
+            for n in range(4):
+                self.act_copy(n, m).start()
+
+    def send_branch(self, m):
+        @pl.when(self.encoder & (self.core == m))
+        def _():
+            for k in range(4):
+                self.branch_copy(k).start()
+
+    def take_factors(self):
+        for k in range(4):
+            self.branch_copy(k).wait_recv()
+        self.branch_forward().start()
+        for m in range(2):
+            for n in range(4):
+                self.act_copy(n, m).wait()
+        for k in range(4):
+            self.branch_copy(k).wait_send()
+        self.branch_forward().wait()
 
     def own_tile(self, i, k, y):
         main = i < self.own_chunks
@@ -206,6 +269,12 @@
             left = jnp.minimum(i // 4, 2) + jnp.where(i > 8, 1, 0)
             shard = k * 2 + y
             self.acc[...] = dot_tn(self.a_fac[left, :, self.tile_rows(shard)], self.b_fac[i])
+
+        @pl.when((i < 4) & self.encoder)
+        def _():
+            self.acc[...] += dot_tn(
+                self.a_fac[4, :, self.tile_rows(k)], self.a_fac[5 + i // 2, :, self.cols(lax.rem(i, 2))]
+            )
 
         first = (i - self.own_chunks) * 2
         small = self.rows // 2
@@ -227,8 +296,10 @@
                 place = pl.ds(pl.multiple_of(k * self.rows + y * small, small), small)
                 self.acc[e * small : (e + 1) * small] = self.slope[first + e, place].astype(F32)
 
-    def pair_step(self, i):
-        @pl.when(i >= self.AHEAD)
+    def pair_step(self, j):
+        i = j + jnp.where(self.decoder, 2, 4)
+
+        @pl.when(j >= self.AHEAD)
         def _():
             pl.semaphore_wait(self.pair_credit, 1)
 
@@ -238,14 +309,14 @@
                 self.cross_copy((i - self.own_chunks) * 2 + e).wait_recv()
 
         def one(k):
-            @pl.when(i >= self.AHEAD)
+            @pl.when(j >= self.AHEAD)
             def _():
-                self.pair_copy(i, k).wait_send()
+                self.pair_copy(j, k).wait_send()
 
             self.own_tile(i, k, 1 - self.y)
-            slot = self.pair_slot(i, k)
+            slot = self.pair_slot(j, k)
             slot[...] = self.acc[...].astype(BF)
-            self.pair_copy(i, k).start()
+            self.pair_copy(j, k).start()
 
         loop(self.line, one)
 
@@ -262,7 +333,20 @@
         def _():
             pl.semaphore_signal(self.cross_credit, inc=1, device_id=self.across, device_id_type=MESH)
 
-        loop(self.AHEAD, self.pair_step)
+    def between(self, m):
+        for e in range(2):
+            self.pair_step(2 * m + e)
+        self.line_step(m)
+
+    def before(self, m):
+        @pl.when(self.encoder & (m == 0))
+        def _():
+            self.take_factors()
+
+        first = jnp.where(self.decoder, 4 + m, 2 * m)
+        last = jnp.where(self.decoder, 5 + m, 2 * m + 2)
+        lax.fori_loop(first, last, lambda j, carry: (self.pair_step(j), carry)[1], 0)
+        self.line_step(jnp.where(self.decoder, 2 + m, m))
 
     def line_step(self, t):
         last = self.line - 1
@@ -270,38 +354,46 @@
         self.within(t - (last - self.z), self.has_left, self.to_left)
         self.within(t - last, True, self.finish)
 
-    def within(self, i, more, body):
-        @pl.when((i >= 0) & (i < self.chunks) & more)
-        def _():
-            body(i)
-
-    def partial(self, i, k):
-        self.own_tile(i, k, self.y)
-        self.pair_copy(i, k).wait_recv()
-        self.acc[...] += self.pair_got[lax.rem(i, self.AHEAD) * self.line + k].astype(F32)
-
-    def arrived(self, side, i, k):
-        self.line_copy(side, i, k, self.z).wait_recv()
-        self.acc[...] += self.line_got(self.line_place(side, i, k, self.z))[...].astype(F32)
-
-    def send(self, side, i, k, inner):
+    def within(self, p, more, body):
+        @pl.when((p >= 0) & (p < self.positions) & more)
+        def _():
+            body(p)
+
+    def partial(self, p, k):
+        early = p < self.EARLY
+        line_first = early & self.decoder
+        i = jnp.where(line_first, p // 2, p - jnp.where(self.decoder, 2, 0))
+        y = jnp.where(line_first & (lax.rem(p, 2) == 0), 1 - self.y, self.y)
+        self.own_tile(i, k, y)
+
+        @pl.when(jnp.logical_not(early))
+        def _():
+            j = p - self.EARLY
+            self.pair_copy(j, k).wait_recv()
+            self.acc[...] += self.pair_got[lax.rem(j, self.AHEAD) * self.line + k].astype(F32)
+
+    def arrived(self, side, p, k):
+        self.line_copy(side, p, k, self.z).wait_recv()
+        self.acc[...] += self.line_got(self.line_place(side, p, k, self.z))[...].astype(F32)
+
+    def send(self, side, p, k, inner):
         receiver = self.z - 1 if side else self.z + 1
 
-        @pl.when(i >= self.DEPTH)
-        def _():
-            self.line_copy(side, i, k, receiver).wait_send()
-
-        self.partial(i, k)
+        @pl.when(p >= self.DEPTH)
+        def _():
+            self.line_copy(side, p, k, receiver).wait_send()
+
+        self.partial(p, k)
 
         @pl.when(inner)
         def _():
-            self.arrived(side, i, k)
-
-        slot = self.line_slot(i, k)
+            self.arrived(side, p, k)
+
+        slot = self.line_slot(p, k)
         slot[...] = self.acc[...].astype(BF)
-        self.line_copy(side, i, k, receiver).start()
-
-    def to_right(self, i):
+        self.line_copy(side, p, k, receiver).start()
+
+    def to_right(self, p):
         pl.semaphore_wait(self.right_credit, 1)
 
         def one(j):
@@ -309,40 +401,55 @@
 
             @pl.when(k > self.z)
             def _():
-                self.send(0, i, k, self.has_left)
+                self.send(0, p, k, self.has_left)
 
         loop(self.line - 1, one)
 
-    def to_left(self, i):
+    def to_left(self, p):
         pl.semaphore_wait(self.left_credit, 1)
 
         def one(k):
             @pl.when(k < self.z)
             def _():
-                self.send(1, i, k, self.has_right)
+                self.send(1, p, k, self.has_right)
 
         loop(self.line - 1, one)
 
-    def finish(self, i):
-        self.partial(i, self.z)
+    def finish(self, p):
+        self.partial(p, self.z)
 
         @pl.when(self.has_left)
         def _():
-            self.arrived(0, i, self.z)
+            self.arrived(0, p, self.z)
 
         @pl.when(self.has_right)
         def _():
-            self.arrived(1, i, self.z)
-
-        @pl.when(i >= self.FINAL)
-        def _():
-            self.final_copy(i).wait()
-
-        slot = self.final_slot(i)
-        slot[...] = self.acc[...]
-        self.final_copy(i).start()
-
-        @pl.when(i + self.WINDOW < self.chunks)
+            self.arrived(1, p, self.z)
+
+        line_first = (p < self.EARLY) & self.decoder
+
+        @pl.when(line_first & (lax.rem(p, 2) == 0))
+        def _():
+            self.late_sent[p // 2] = self.acc[...].astype(BF)
+            self.late_copy(p // 2).start()
+
+        @pl.when(line_first & (lax.rem(p, 2) == 1))
+        def _():
+            self.late_acc[p // 2] = self.acc[...]
+
+        @pl.when(jnp.logical_not(line_first))
+        def _():
+            i = p - jnp.where(self.decoder, 2, 0)
+
+            @pl.when(i >= self.FINAL + jnp.where(self.decoder, 2, 0))
+            def _():
+                self.final_copy(i).wait()
+
+            slot = self.final_slot(i)
+            slot[...] = self.acc[...]
+            self.final_copy(i).start()
+
+        @pl.when(p + self.WINDOW < self.positions)
         def _():
             @pl.when(self.has_left)
             def _():
@@ -352,10 +459,10 @@
             def _():
                 pl.semaphore_signal(self.left_credit, inc=1, device_id=self.right, device_id_type=MESH)
 
-        @pl.when(i + self.AHEAD < self.chunks)
+        @pl.when((p >= self.EARLY) & (p - self.EARLY + self.AHEAD < self.pairs))
         def _():
             pl.semaphore_signal(self.pair_credit, inc=1, device_id=self.partner, device_id_type=MESH)
-            self.pair_step(i + self.AHEAD)
+            self.pair_step(p - self.EARLY + self.AHEAD)
 
     def final_slot(self, i):
         slot = lax.rem(i, self.FINAL)
@@ -384,33 +491,29 @@
             loop(4, one)
 
     def norm_copy(self, src, dst, device):
-        return pltpu.make_async_remote_copy(
-            src_ref=self.nb.at[src],
-            dst_ref=self.nb.at[dst],
-            send_sem=self.norm_send.at[dst],
-            recv_sem=self.norm_recv.at[dst],
-            device_id=device,
-            device_id_type=MESH,
-        )
-
-    def norms(self, sums, norm_out, norm3_out):
+        return self.remote(self.nb.at[src], self.nb.at[dst], self.norm_send.at[dst], self.norm_recv.at[dst], device)
+
+    def start_norms(self, sums):
         nb, has_left, has_right = self.nb, self.has_left, self.has_right
         for i in range(6):
             nb[0, i : i + 1] = jnp.sum(sums[i], 0, keepdims=True)
         nb[0, 6:8] = jnp.zeros_like(nb[0, 6:8])
-        to_right = self.norm_copy(3, 1, self.right)
-        to_left = self.norm_copy(4, 2, self.left)
         nb[3] = nb[0]
         nb[4] = nb[0]
         nb[5] = nb[0]
 
         @pl.when(jnp.logical_not(has_left))
         def _():
-            to_right.start()
+            self.norm_copy(3, 1, self.right).start()
 
         @pl.when(jnp.logical_not(has_right))
         def _():
-            to_left.start()
+            self.norm_copy(4, 2, self.left).start()
+
+    def middle_norms(self):
+        nb, has_left, has_right = self.nb, self.has_left, self.has_right
+        to_right = self.norm_copy(3, 1, self.right)
+        to_left = self.norm_copy(4, 2, self.left)
 
         @pl.when(has_left)
         def _():
@@ -433,9 +536,8 @@
                 to_left.start()
 
         self.norm_copy(5, 6, self.partner).start()
-        self.norm_out, self.norm3_out = norm_out, norm3_out
-
-    def finish_norms(self):
+
+    def finish_norms(self, norm_out, norm3_out):
         nb = self.nb
         self.norm_copy(5, 6, self.partner).wait()
 
@@ -455,7 +557,7 @@
             hand.start()
             nb[8] = nb[7]
 
-        self.norm_out[...] = nb[7, :, pl.ds(pl.multiple_of(self.dp * 128, 128), 128)]
+        norm_out[...] = nb[7, :, pl.ds(pl.multiple_of(self.dp * 128, 128), 128)]
 
         @pl.when(self.encoder)
         def _():
@@ -463,18 +565,43 @@
 
         place = self.section * self.line * 2 + self.dp
         block = nb[8, :, pl.ds(pl.multiple_of(place // 2 * 128, 128), 128)]
-        self.norm3_out[...] = jnp.where(self.y == 0, block, pltpu.roll(block, 64, 1))
+        norm3_out[...] = jnp.where(self.y == 0, block, pltpu.roll(block, 64, 1))
 
         @pl.when(self.decoder)
         def _():
             hand.wait_send()
 
-    def run(self):
-        loop(self.chunks, self.line_step)
-        self.finish_norms()
-        loop(self.line - 1, lambda p: self.line_step(self.chunks + p))
+    def run(self, sums, norm_out, norm3_out):
+        self.start_norms(sums)
+        first = jnp.where(self.decoder, 6, 4)
+        lax.fori_loop(first, self.AHEAD, lambda j, carry: (self.pair_step(j), carry)[1], 0)
+        self.cross_part()
+
+        def step(t, carry):
+            self.line_step(t)
+
+            @pl.when(t == 5)
+            def _():
+                self.middle_norms()
+
+            @pl.when(t == self.positions - 1)
+            def _():
+                self.finish_norms(norm_out, norm3_out)
+
+            return carry
+
+        lax.fori_loop(jnp.where(self.decoder, 4, 2), self.positions + self.line - 1, step, 0)
 
     def drain(self):
+        @pl.when(self.decoder)
+        def _():
+            for e in range(2):
+                self.late_copy(e).wait()
+                self.final_copy(e).wait()
+                slot = self.final_slot(e)
+                slot[...] = self.late_acc[e] + self.late_got[e].astype(F32)
+                self.final_copy(e).start()
+
         for slot in range(self.AHEAD):
             for k in range(self.line):
                 self.pair_copy(slot, k).wait_send()
@@ -530,20 +657,20 @@
     proj,
     cross_proj,
     unit1,
-    unit2,
+    held,
     unit3,
     scale1,
     scale2,
     scale3,
     resid,
     slope,
-    d_out,
     d_mix,
     sent,
     got,
     half_send,
     half_own,
     half_got,
+    low_out,
     sums,
     load_sem,
     x_sem,
@@ -566,6 +693,7 @@
     limit = jnp.where(decoder, 0, slot)
     width = w_up.shape[1]
     parts = width // CHUNK
+    two, three = jnp.where(decoder, 0, 1), jnp.where(decoder, 1, 0)
     own = core * half
     other = (1 - core) * half
 
@@ -577,6 +705,8 @@
     d_cross_proj = b_fac.at[2 * parts + 4 : 2 * parts + 7]
     cross_mixed = b_fac.at[2 * parts + 7]
 
+    unit2, d_out = held.at[0], held.at[1]
+
     def rows_of(m):
         return pl.ds(pl.multiple_of(m * slot, slot), slot)
 
@@ -586,14 +716,17 @@
     def strip_of(m, k):
         return pl.ds(pl.multiple_of(m * slot + k * STRIP, STRIP), STRIP)
 
-    def lanes_of(j):
-        return pl.ds(pl.multiple_of(j * PAIR, PAIR), PAIR)
+    def strips(body):
+        for k in range(slot // STRIP):
+            body(k)
 
     barrier = pltpu.get_barrier_semaphore()
     for device in (mate, across):
         pl.semaphore_signal(barrier, inc=1, device_id=device, device_id_type=MESH)
     if ring:
-        total = GradientShare(ring, section, dp, core, decoder, a_fac, b_fac, first_out, w_up, w_down, w_cross, slope, resid, *share)
+        total = GradientShare(
+            ring, section, dp, core, decoder, a_fac, b_fac, first_out, w_up, w_down, held, slope, resid, *share
+        )
         greeted = 2 + total.greet(barrier)
     else:
         greeted = 2
@@ -732,7 +865,7 @@
         rows = rows_of(m)
         for t in range(3):
             proj[t, rows] = dot_nn(layer_in[rows], w_qkv[t]).astype(BF)
-        loop(CHUNK // PAIR, lambda j: attend_forward(proj, mixed, rows, lanes_of(j), limit))
+        attend_forward(proj, mixed, rows, limit)
         project_out(mixed[rows], w_out, m)
         exchange(0, 0, m).start()
 
@@ -752,24 +885,22 @@
             unit1[strip] = unit.astype(BF)
             scale1[strip] = scale
             resid[strip] = value
-            normed_low[strip] = value.astype(BF)
+            low_out[pl.ds(k * STRIP, STRIP)] = value.astype(BF)
             crossed[strip] = value.astype(BF)
 
-        loop(slot // STRIP, norm)
+        strips(norm)
 
         @pl.when(decoder)
         def _():
             rows = rows_of(m)
-            cross_proj[0, rows] = dot_nn(normed_low[rows], w_cross[0]).astype(BF)
+            normed_low[rows] = low_out[...]
+            cross_proj[0, rows] = dot_nn(low_out[...], w_cross[0]).astype(BF)
             across_copy(seg_out.at[0, m], memory, 0, m).wait_recv()
             forward_copy(memory, 1, m).start()
             forward_copy(memory, 1, m).wait()
             for t in range(1, 3):
                 cross_proj[t, rows] = dot_nn(memory[rows], w_cross[t]).astype(BF)
-            loop(
-                CHUNK // PAIR,
-                lambda j: attend_forward(cross_proj, cross_mixed, rows, lanes_of(j), None),
-            )
+            attend_forward(cross_proj, cross_mixed, rows, None)
             project_out(cross_mixed[rows], w_cross_out, m)
             exchange(1, 1, m).start()
 
@@ -792,37 +923,34 @@
                 resid[strip] = value
                 crossed[strip] = value.astype(BF)
 
-            loop(slot // STRIP, norm)
+            strips(norm)
 
         for n in range(parts):
             pre = dot_nn(crossed[rows], w_up[:, n * CHUNK : (n + 1) * CHUNK])
             rise = 0.5 + 0.5 * lax.erf(pre * (0.5**0.5))
             act[n, rows] = (pre * rise).astype(BF)
             slope[n, rows] = (rise + pre * jnp.exp(-0.5 * pre * pre) * 0.3989422804014327).astype(BF)
+        if ring:
+            total.send_act(m)
         project_out(jnp.concatenate([act[n, rows] for n in range(parts)], 1), w_down, m)
-        exchange(2, 2, m).start()
+        exchange(2, two, m).start()
 
     loop(2, feed_forward)
 
     def finish_forward(m):
-        exchange(2, 2, m).wait()
+        exchange(2, two, m).wait()
 
         def norm(k):
             strip = strip_of(m, k)
             unit, scale, value = norm_forward(
-                resid[strip] + summed(2, strip), gain2[...], bias2[...]
+                resid[strip] + summed(two, strip), gain2[...], bias2[...]
             )
             unit2[strip] = unit.astype(BF)
             scale2[strip] = scale
-            place = k * STRIP - own
-
-            @pl.when((place >= 0) & (place < half))
-            def _():
-                seg_out[0, m, pl.ds(pl.multiple_of(lax.rem(k * STRIP, half), STRIP), STRIP)] = (
-                    value.astype(BF)
-                )
-
-        loop(slot // STRIP, norm)
+            low_out[pl.ds(k * STRIP, STRIP)] = value.astype(BF)
+
+        strips(norm)
+        seg_out[0, m] = low_out[pl.ds(pl.multiple_of(own, half), half)]
 
         @pl.when(encoder)
         def _():
@@ -862,12 +990,14 @@
             resid[strip] = grad
             d_branch[strip] = grad.astype(BF)
 
-        loop(slot // STRIP, norm)
+        strips(norm)
+        if ring:
+            total.send_branch(m)
         for n in range(parts):
             grad = dot_nn(d_branch[rows], w_down[:, n * CHUNK : (n + 1) * CHUNK])
             d_hidden[n, rows] = (grad * slope[n, rows].astype(F32)).astype(BF)
         project_out(jnp.concatenate([d_hidden[n, rows] for n in range(parts)], 1), w_up, m)
-        exchange(3, 0, m).start()
+        exchange(3, three, m).start()
 
     loop(2, feed_backward)
     if ring:
@@ -879,7 +1009,7 @@
         def norm(k):
             strip = strip_of(m, k)
             grad = norm_backward(
-                resid[strip] + summed(0, strip),
+                resid[strip] + summed(three, strip),
                 unit3[strip].astype(F32),
                 scale3[strip],
                 gain3[...],
@@ -889,12 +1019,9 @@
             resid[strip] = grad
             d_cross[strip] = grad.astype(BF)
 
-        loop(slot // STRIP, norm)
+        strips(norm)
         d_mix[rows] = dot_nn(d_cross[rows], w_cross_out[...]).astype(BF)
-        loop(
-            CHUNK // PAIR,
-            lambda j: attend_backward(cross_proj, d_mix, d_cross_proj, rows, lanes_of(j), None),
-        )
+        attend_backward(cross_proj, d_mix, d_cross_proj, rows, None)
 
         def memory_part(offset):
             piece = half_of(m, offset)
@@ -912,7 +1039,7 @@
             cols = slice(n * CHUNK, (n + 1) * CHUNK)
             half_own[m, :, cols] = dot_nt(memory_part(own), memory_weight(n))
         project_out(d_cross_proj[0, rows], w_cross[0], m)
-        exchange(4, 1, m).start()
+        exchange(4, 0, m).start()
         half_exchange(0, m).wait()
         half_send[0, m] = (half_own[m] + half_got[0, m].astype(F32)).astype(BF)
         across_copy(half_send.at[0, m], d_out, 2, m).start()
@@ -934,21 +1061,19 @@
                 resid[strip] = grad
                 d_attn[strip] = grad.astype(BF)
 
-            loop(slot // STRIP, norm)
+            strips(norm)
 
         @pl.when(decoder)
         def _():
-            exchange(4, 1, m).wait()
+            exchange(4, 0, m).wait()
 
         @pl.when(encoder)
         def _():
-            exchange(3, 0, m).wait()
-
-        norm_rows(jnp.where(decoder, 1, 0))
+            exchange(3, three, m).wait()
+
+        norm_rows(0)
         d_mix[rows] = dot_nn(d_attn[rows], w_out[...]).astype(BF)
-        loop(
-            CHUNK // PAIR, lambda j: attend_backward(proj, d_mix, d_proj, rows, lanes_of(j), limit)
-        )
+        attend_backward(proj, d_mix, d_proj, rows, limit)
 
         def input_part(offset):
             piece = half_of(m, offset)
@@ -969,12 +1094,19 @@
     @pl.when(decoder)
     def _():
         def both(m):
-            exchange(3, 0, m).wait()
+            if ring:
+                total.between(m)
+            exchange(3, three, m).wait()
             cross_backward(m)
 
         loop(2, both)
 
-    loop(2, attention_back)
+    def last_part(m):
+        if ring:
+            total.before(m)
+        attention_back(m)
+
+    loop(2, last_part)
 
     def finish_backward(m):
         half_exchange(1, m).wait()
@@ -995,9 +1127,7 @@
             across_copy(half_send.at[0, m], d_out, 2, m).wait_send()
 
     if ring:
-        total.norms(sums, norm_out, second_out)
-        total.cross_part()
-        total.run()
+        total.run(sums, norm_out, second_out)
         total.drain()
         return
 
@@ -1010,6 +1140,32 @@
     ]
     for copy in copies:
         copy.start()
+    for copy in copies:
+        copy.wait()
+
+
+def unpack_kernel(parts, seg, grads, norms, tiles, norm3, *outs):
+    (seg_out, in_grad, qkv, proj_out, gain1, bias1, up, down, gain2, bias2, cross, cross_out, gain3, bias3, sems) = outs
+    rows = tiles.shape[1]
+    small = rows // 2
+    copies = [(seg, seg_out), (grads, in_grad)]
+    for n in range(parts):
+        cols = slice(n * CHUNK, (n + 1) * CHUNK)
+        copies.append((tiles.at[n], down.at[0, :, cols]))
+        copies.append((tiles.at[parts + n], up.at[0, :, cols]))
+    copies.append((tiles.at[2 * parts], proj_out.at[0]))
+    for t in range(3):
+        copies.append((tiles.at[2 * parts + 1 + t], qkv.at[0, t]))
+    for q in range(4):
+        source = tiles.at[2 * parts + 4 + q // 2, pl.ds(q % 2 * small, small)]
+        copies.append((source, cross.at[q] if q < 3 else cross_out))
+    copies = [pltpu.make_async_copy(src, dst, sems.at[i]) for i, (src, dst) in enumerate(copies)]
+    for copy in copies:
+        copy.start()
+    for i, ref in enumerate((gain1, bias1, gain2, bias2)):
+        ref[...] = norms[i : i + 1]
+    gain3[...] = norm3[4:5, :small]
+    bias3[...] = norm3[5:6, :small]
     for copy in copies:
         copy.wait()
 
@@ -1066,6 +1222,9 @@
             VM((GradientShare.AHEAD * 4,) + tile, BF),
             VM(tile, F32),
             VM((9, 8, depth), F32),
+            VM((2,) + tile, BF),
+            VM((2,) + tile, BF),
+            VM((2,) + tile, F32),
             dma((GradientShare.AHEAD * 4,)),
             dma((GradientShare.AHEAD * 4,)),
             dma((GradientShare.DEPTH * 4,)),
@@ -1074,6 +1233,10 @@
             dma((4,)),
             dma((9,)),
             dma((9,)),
+            dma((2,)),
+            dma((2,)),
+            dma((13,)),
+            dma((13,)),
             dma((GradientShare.FINAL,)),
             regular,
             regular,
@@ -1104,20 +1267,20 @@
             VM((3, rows, heads), BF),
             VM((3, rows, heads), BF),
             VM((rows, depth), BF),
-            VM((rows, depth), BF),
+            VM((2, rows, depth), BF),
             VM((rows, depth), BF),
             VM((rows, 1), F32),
             VM((rows, 1), F32),
             VM((rows, 1), F32),
             VM((rows, depth), F32),
             VM((parts, rows, CHUNK), BF),
-            VM((rows, depth), BF),
             VM((rows, heads), BF),
             VM((rows, depth), BF),
-            VM((3, rows, depth), BF),
+            VM((2, rows, depth), BF),
             VM((2, micro, half, depth), BF),
             VM((micro, half, depth), F32),
             VM((2, micro, half, depth), BF),
+            VM((2 * half, depth), BF),
             VM((6, 8, depth), F32),
             pltpu.SemaphoreType.DMA((6,)),
             pltpu.SemaphoreType.DMA((12,)),
@@ -1151,27 +1314,33 @@
         norm3_bias[None],
     )
     if ring:
-        own = lambda first_one, count: jnp.swapaxes(
-            first[first_one : first_one + count], 0, 1
-        ).reshape(1, depth // ring, count * CHUNK)
-        cross = first[2 * parts + 4 :].reshape(4, depth // ring // 2, CHUNK)
-        lanes = depth // ring // 2
-        return (
-            seg_out,
-            in_grad,
-            first[None, 2 * parts + 1 : 2 * parts + 4],
-            first[2 * parts : 2 * parts + 1],
-            norms[0:1],
-            norms[1:2],
-            own(parts, parts),
-            own(0, parts),
-            norms[2:3],
-            norms[3:4],
-            cross[:3],
-            cross[3],
-            second[4, :lanes],
-            second[5, :lanes],
-        )
+        lanes = depth // ring
+        row = shape((1, lanes), F32)
+        small = shape((1, lanes // 2), F32)
+        outs = pl.pallas_call(
+            functools.partial(unpack_kernel, parts),
+            out_shape=(
+                shape(seg_out.shape, BF),
+                shape(in_grad.shape, BF),
+                shape((1, 3, lanes, heads), F32),
+                shape((1, lanes, heads), F32),
+                row,
+                row,
+                shape((1, lanes, width), F32),
+                shape((1, lanes, width), F32),
+                row,
+                row,
+                shape((3, lanes // 2, heads), F32),
+                shape((lanes // 2, heads), F32),
+                small,
+                small,
+            ),
+            in_specs=[hbm, hbm, vmem, hbm, vmem],
+            out_specs=(vmem,) * 14,
+            scratch_shapes=[pltpu.SemaphoreType.DMA((2 * parts + 10,))],
+            name="unpack",
+        )(seg_out, in_grad, norms, first, second)
+        return outs[:12] + (outs[12][0], outs[13][0])
     a_fac, b_fac = first, second
     decoder = lax.axis_index("section") == sections - 1
 

time: 287 us -> 237 us (0.83)
  Pallas kernels: 272 us -> 236 us
  local copies, waits for them, and re-layouts: 14 us -> 0 us
    pallas_call x1, Pallas kernels: 272 us -> 231 us  [body(): pl.pallas_call(functools.partial(layer_kernel, sections, ring), out_shape...]
    pallas_call x0 -> x1, Pallas kernels: none -> 5.32 us  [body(): pl.pallas_call(functools.partial(unpack_kernel, parts), out_shape=(shape(...]
    slice x4 -> x0, local copies, waits for them, and re-layouts: 4.87 us -> none  [the longest x1 1.67 us: body(): first[2 * parts:2 * parts + 1]]
    unnamed x10 -> x0, local copies, waits for them, and re-layouts: 4.22 us -> none
where the time goes in v4:
time: 237 us
  Pallas kernels  236 us (100%)
    pallas_call x1, Pallas kernels, body(): pl.pallas_call(functools.partial(layer_kernel, sections, ring), out_shape...  231 us
    pallas_call x1, Pallas kernels, body(): pl.pallas_call(functools.partial(unpack_kernel, parts), out_shape=(shape(...  5.32 us

profile of v4, /device:TPU:0, one launch (start us, length us, event | category | flops | bytes accessed | tf_op | source)
XLA Modules:
  0.0 236.7 jit_solution(15589975274826562118)
XLA Ops:
  0.7 230.6 %layers.1 = (bf16[1,2,128,1024]{3,2,1,0:T(8,128)(2,1)}, bf16[1,2,128,1024]{3,2,1,0:T(8,128)(2,1)}, f32[8,128]{1,0:T(8,128)}, f32[14,128,512]{2,1,0:T(8,128)}, f32[8,128]{1,0:T(8,128)}) custom-call(bf16[2,128,1024]{2,1,0:T(8,128)(2,1)} %inputs.1, bf16[2,128,1024]{2,1,0:T(8,128)(2,1)} %targets.1, bf16[2,128,1024]{2,1,0:T(8,128)(2,1)} %cotangent.1, ...), custom_call_target="tpu_custom_call" | custom-call | tf_op jit(solution)/shard_map/layers/pallas_call | solution.py:1249
  231.2 5.3 %unpack.1 = (bf16[1,2,128,1024]{3,2,1,0:T(8,128)(2,1)}, bf16[1,2,128,1024]{3,2,1,0:T(8,128)(2,1)}, f32[1,3,128,512]{3,2,1,0:T(8,128)}, f32[1,128,512]{2,1,0:T(8,...) custom-call(bf16[1,2,128,1024]{3,2,1,0:T(8,128)(2,1)} %get-tuple-ele, ...), custom_call_target="tpu_custom_call" | custom-call | tf_op jit(solution)/shard_map/unpack/pallas_call | solution.py:1320

commit v5 on v4

--- a/solution.py
+++ b/solution.py
@@ -49,13 +49,13 @@
 
 
 def expos_of(query, keys, mask, limit):
-    scores = dot_nt(query * (mask * (HEAD**-0.5)).astype(BF), keys)
+    scores = dot_nt(keys, query * (mask * (HEAD**-0.5)).astype(BF))
     if limit is not None:
-        row = lax.broadcasted_iota(jnp.int32, scores.shape, 0)
-        col = lax.broadcasted_iota(jnp.int32, scores.shape, 1)
-        scores = jnp.where(row + limit >= col, scores, NEG)
-    expo = jnp.exp(scores - jnp.max(scores, -1, keepdims=True))
-    return expo, 1.0 / jnp.sum(expo, -1, keepdims=True)
+        key = lax.broadcasted_iota(jnp.int32, scores.shape, 0)
+        place = lax.broadcasted_iota(jnp.int32, scores.shape, 1)
+        scores = jnp.where(place + limit >= key, scores, NEG)
+    expo = jnp.exp(scores - jnp.max(scores, 0, keepdims=True))
+    return expo, 1.0 / jnp.sum(expo, 0, keepdims=True)
 
 
 def attend_forward(proj, mixed, rows, limit):
@@ -67,9 +67,8 @@
         for mask in masks:
             expo, share = expos_of(query, keys, mask, limit)
             low.append((expo * share).astype(BF))
-        mixed[rows, lanes] = dot_nn(
-            jnp.concatenate(low, 1), jnp.concatenate([values * mask for mask in masks], 0)
-        ).astype(BF)
+        turned = dot_tn(jnp.concatenate([values * mask for mask in masks], 0), jnp.concatenate(low, 0))
+        mixed[rows, lanes] = turned.T.astype(BF)
 
 
 def attend_backward(proj, d_mixed, d_proj, rows, limit):
@@ -83,25 +82,23 @@
         for mask in masks:
             expo, share = expos_of(query, keys, mask, limit)
             weights = expo * share
-            d_weights = dot_nt(grad * mask, values)
-            inner = jnp.sum(weights * d_weights, -1, keepdims=True)
+            d_weights = dot_nt(values, grad * mask)
+            inner = jnp.sum(weights * d_weights, 0, keepdims=True)
             d_scores.append((weights * (d_weights - inner)).astype(BF))
             low.append(weights.astype(BF))
-        d_proj[2, rows, lanes] = dot_tn(
-            jnp.concatenate(low, 0), jnp.concatenate([grad * mask for mask in masks], 0)
+        d_proj[2, rows, lanes] = dot_nn(
+            jnp.concatenate(low, 1), jnp.concatenate([grad * mask for mask in masks], 0)
         ).astype(BF)
-        d_proj[0, rows, lanes] = (
+        d_proj[1, rows, lanes] = (
             dot_nn(
-                jnp.concatenate(d_scores, 1), jnp.concatenate([keys * mask for mask in masks], 0)
+                jnp.concatenate(d_scores, 1), jnp.concatenate([query * mask for mask in masks], 0)
             )
             * scale
         ).astype(BF)
-        d_proj[1, rows, lanes] = (
-            dot_tn(
-                jnp.concatenate(d_scores, 0), jnp.concatenate([query * mask for mask in masks], 0)
-            )
-            * scale
-        ).astype(BF)
+        turned = dot_tn(
+            jnp.concatenate([keys * mask for mask in masks], 0), jnp.concatenate(d_scores, 0)
+        )
+        d_proj[0, rows, lanes] = (turned.T * scale).astype(BF)
 
 
 def norm_forward(value, gain, bias):
@@ -128,8 +125,9 @@
     FINAL = 8
     EARLY = 4
 
-    def __init__(self, size, section, dp, core, decoder, a_fac, b_fac, tiles, w_up, w_down, held, slope, resid, *share):
-        (self.pair_got, self.acc, self.nb, self.late_sent, self.late_got, self.late_acc, self.pair_send,
+    def __init__(self, size, section, dp, core, decoder, a_fac, b_fac, tiles, w_up, w_down, held, slope, resid, acc, *share):
+        self.acc = acc
+        (self.pair_got, self.nb, self.late_sent, self.late_got, self.late_acc, self.pair_send,
          self.pair_recv, self.line_send, self.line_recv, self.cross_send, self.cross_recv, self.norm_send,
          self.norm_recv, self.late_send, self.late_recv, self.factor_send, self.factor_recv, self.final_sem,
          self.pair_credit, self.left_credit, self.right_credit, self.cross_credit) = share
@@ -261,40 +259,41 @@
             self.branch_copy(k).wait_send()
         self.branch_forward().wait()
 
-    def own_tile(self, i, k, y):
-        main = i < self.own_chunks
-
-        @pl.when(main)
-        def _():
-            left = jnp.minimum(i // 4, 2) + jnp.where(i > 8, 1, 0)
-            shard = k * 2 + y
-            self.acc[...] = dot_tn(self.a_fac[left, :, self.tile_rows(shard)], self.b_fac[i])
-
-        @pl.when((i < 4) & self.encoder)
-        def _():
-            self.acc[...] += dot_tn(
-                self.a_fac[4, :, self.tile_rows(k)], self.a_fac[5 + i // 2, :, self.cols(lax.rem(i, 2))]
-            )
-
+    def left_of(self, i):
+        return jnp.minimum(i // 4, 2) + jnp.where(i > 8, 1, 0)
+
+    def cross_tile(self, i, k, y):
         first = (i - self.own_chunks) * 2
         small = self.rows // 2
-
-        @pl.when(jnp.logical_not(main) & self.decoder)
-        def _():
-            base = self.a_fac.shape[2] // 2
+        base = self.a_fac.shape[2] // 2
+
+        def product(e):
+            q = first + e
+            block = dot_tn(
+                self.a_fac[4 + (q + 1) // 2, :, pl.ds(pl.multiple_of(base + k * self.rows, self.rows), self.rows)],
+                self.b_fac[self.own_chunks + q],
+            )
+            return jnp.where(y == 0, block[:small], block[small:])
+
+        def given(e):
+            place = pl.ds(pl.multiple_of(k * self.rows + y * small, small), small)
+            return self.slope[first + e, place].astype(F32)
+
+        return product, given
+
+    def cross_into(self, ref, i, k, y):
+        product, given = self.cross_tile(i, k, y)
+        small = self.rows // 2
+
+        @pl.when(self.decoder)
+        def _():
             for e in range(2):
-                q = first + e
-                block = dot_tn(
-                    self.a_fac[4 + (q + 1) // 2, :, pl.ds(pl.multiple_of(base + k * self.rows, self.rows), self.rows)],
-                    self.b_fac[self.own_chunks + q],
-                )
-                self.acc[e * small : (e + 1) * small] = jnp.where(y == 0, block[:small], block[small:])
-
-        @pl.when(jnp.logical_not(main) & self.encoder)
+                ref[e * small : (e + 1) * small] = product(e).astype(ref.dtype)
+
+        @pl.when(self.encoder)
         def _():
             for e in range(2):
-                place = pl.ds(pl.multiple_of(k * self.rows + y * small, small), small)
-                self.acc[e * small : (e + 1) * small] = self.slope[first + e, place].astype(F32)
+                ref[e * small : (e + 1) * small] = given(e).astype(ref.dtype)
 
     def pair_step(self, j):
         i = j + jnp.where(self.decoder, 2, 4)
@@ -302,23 +301,31 @@
         @pl.when(j >= self.AHEAD)
         def _():
             pl.semaphore_wait(self.pair_credit, 1)
-
-        @pl.when((i >= self.own_chunks) & self.encoder)
-        def _():
-            for e in range(2):
-                self.cross_copy((i - self.own_chunks) * 2 + e).wait_recv()
-
-        def one(k):
-            @pl.when(j >= self.AHEAD)
+            for k in range(self.line):
+                self.pair_copy(j, k).wait_send()
+
+        @pl.when(i < self.own_chunks)
+        def _():
+            left = self.left_of(i)
+            factor = jnp.concatenate(
+                [self.a_fac[left, :, self.tile_rows(k * 2 + 1 - self.y)] for k in range(self.line)], 1
+            )
+            block = dot_tn(factor, self.b_fac[i]).astype(BF)
+            for k in range(self.line):
+                slot = self.pair_slot(j, k)
+                slot[...] = block[k * self.rows : (k + 1) * self.rows]
+
+        @pl.when(i >= self.own_chunks)
+        def _():
+            @pl.when(self.encoder)
             def _():
-                self.pair_copy(j, k).wait_send()
-
-            self.own_tile(i, k, 1 - self.y)
-            slot = self.pair_slot(j, k)
-            slot[...] = self.acc[...].astype(BF)
+                for e in range(2):
+                    self.cross_copy((i - self.own_chunks) * 2 + e).wait_recv()
+
+            loop(self.line, lambda k: self.cross_into(self.pair_slot(j, k), i, k, 1 - self.y))
+
+        for k in (0, 3, 1, 2):
             self.pair_copy(j, k).start()
-
-        loop(self.line, one)
 
     def begin(self):
         @pl.when(self.has_left)
@@ -334,8 +341,10 @@
             pl.semaphore_signal(self.cross_credit, inc=1, device_id=self.across, device_id_type=MESH)
 
     def between(self, m):
-        for e in range(2):
-            self.pair_step(2 * m + e)
+        @pl.when(m == 0)
+        def _():
+            loop(2, self.pair_step)
+
         self.line_step(m)
 
     def before(self, m):
@@ -343,99 +352,132 @@
         def _():
             self.take_factors()
 
-        first = jnp.where(self.decoder, 4 + m, 2 * m)
-        last = jnp.where(self.decoder, 5 + m, 2 * m + 2)
-        lax.fori_loop(first, last, lambda j, carry: (self.pair_step(j), carry)[1], 0)
-        self.line_step(jnp.where(self.decoder, 2 + m, m))
+        self.line_step(jnp.where(self.decoder, 2, 0) + 2 * m)
+        first = jnp.where(self.decoder, 2, 0) + 2 * m
+        lax.fori_loop(first, first + 2, lambda j, carry: (self.pair_step(j), carry)[1], 0)
+
+    def middle(self, m):
+        self.line_step(jnp.where(self.decoder, 3, 1) + 2 * m)
+
+    def entry(self, t, e):
+        last = self.line - 1
+        on = last - self.z
+        k = jnp.where(e == last, self.z, jnp.where(e < on, last - e, e - on))
+        hops = jnp.where(k > self.z, self.z, last - self.z)
+        p = t - jnp.where(e == last, last, hops)
+        valid = (p >= 0) & (p < self.positions)
+        line_first = (p < self.EARLY) & self.decoder
+        i = jnp.where(line_first, p // 2, p - jnp.where(self.decoder, 2, 0))
+        y = jnp.where(line_first & (lax.rem(p, 2) == 0), 1 - self.y, self.y)
+        return k, p, valid, i, y
 
     def line_step(self, t):
         last = self.line - 1
-        self.within(t - self.z, self.has_right, self.to_right)
-        self.within(t - (last - self.z), self.has_left, self.to_left)
-        self.within(t - last, True, self.finish)
-
-    def within(self, p, more, body):
-        @pl.when((p >= 0) & (p < self.positions) & more)
-        def _():
-            body(p)
-
-    def partial(self, p, k):
-        early = p < self.EARLY
-        line_first = early & self.decoder
-        i = jnp.where(line_first, p // 2, p - jnp.where(self.decoder, 2, 0))
-        y = jnp.where(line_first & (lax.rem(p, 2) == 0), 1 - self.y, self.y)
-        self.own_tile(i, k, y)
-
-        @pl.when(jnp.logical_not(early))
-        def _():
-            j = p - self.EARLY
-            self.pair_copy(j, k).wait_recv()
-            self.acc[...] += self.pair_got[lax.rem(j, self.AHEAD) * self.line + k].astype(F32)
+
+        def held_at(p):
+            return (p >= 0) & (p < self.positions)
+
+        @pl.when(held_at(t - self.z) & self.has_right)
+        def _():
+            pl.semaphore_wait(self.right_credit, 1)
+
+        @pl.when(held_at(t - (last - self.z)) & self.has_left)
+        def _():
+            pl.semaphore_wait(self.left_credit, 1)
+
+        for e in range(self.line):
+            k, p, valid, i, y = self.entry(t, e)
+            i = jnp.clip(i, 0, self.own_chunks - 1)
+            self.acc[e] = dot_tn(self.a_fac[self.left_of(i), :, self.tile_rows(k * 2 + y)], self.b_fac[i])
+
+        @pl.when(self.encoder & (t < self.EARLY + last))
+        def _():
+            for e in range(self.line):
+                k, p, valid, i, y = self.entry(t, e)
+                n = jnp.clip(i, 0, self.EARLY - 1)
+                part = dot_tn(
+                    self.a_fac[4, :, self.tile_rows(k)], self.a_fac[5 + n // 2, :, self.cols(lax.rem(n, 2))]
+                )
+                self.acc[e] += jnp.where(i < self.EARLY, part, 0.0)
+
+        def one(e):
+            k, p, valid, i, y = self.entry(t, e)
+
+            @pl.when(valid)
+            def _():
+                acc = self.acc.at[e]
+
+                @pl.when(i >= self.own_chunks)
+                def _():
+                    self.cross_into(acc, i, k, y)
+
+                @pl.when(p >= self.EARLY)
+                def _():
+                    j = p - self.EARLY
+                    self.pair_copy(j, k).wait_recv()
+                    acc[...] += self.pair_got[lax.rem(j, self.AHEAD) * self.line + k].astype(F32)
+
+                @pl.when(e < last)
+                def _():
+                    self.send(p, k, acc)
+
+                @pl.when(e == last)
+                def _():
+                    self.finish(p, acc)
+
+        loop(self.line, one)
 
     def arrived(self, side, p, k):
         self.line_copy(side, p, k, self.z).wait_recv()
-        self.acc[...] += self.line_got(self.line_place(side, p, k, self.z))[...].astype(F32)
-
-    def send(self, side, p, k, inner):
-        receiver = self.z - 1 if side else self.z + 1
-
-        @pl.when(p >= self.DEPTH)
-        def _():
-            self.line_copy(side, p, k, receiver).wait_send()
-
-        self.partial(p, k)
-
-        @pl.when(inner)
-        def _():
-            self.arrived(side, p, k)
-
+        return self.line_got(self.line_place(side, p, k, self.z))[...].astype(F32)
+
+    def send(self, p, k, acc):
         slot = self.line_slot(p, k)
-        slot[...] = self.acc[...].astype(BF)
-        self.line_copy(side, p, k, receiver).start()
-
-    def to_right(self, p):
-        pl.semaphore_wait(self.right_credit, 1)
-
-        def one(j):
-            k = self.line - 1 - j
-
-            @pl.when(k > self.z)
+
+        def to(side, receiver, inner):
+            copy = self.line_copy(side, p, k, receiver)
+
+            @pl.when(p >= self.DEPTH)
             def _():
-                self.send(0, p, k, self.has_left)
-
-        loop(self.line - 1, one)
-
-    def to_left(self, p):
-        pl.semaphore_wait(self.left_credit, 1)
-
-        def one(k):
-            @pl.when(k < self.z)
+                copy.wait_send()
+
+            @pl.when(inner)
             def _():
-                self.send(1, p, k, self.has_right)
-
-        loop(self.line - 1, one)
-
-    def finish(self, p):
-        self.partial(p, self.z)
-
+                slot[...] = (acc[...] + self.arrived(side, p, k)).astype(BF)
+
+            @pl.when(jnp.logical_not(inner))
+            def _():
+                slot[...] = acc[...].astype(BF)
+
+            copy.start()
+
+        @pl.when(k > self.z)
+        def _():
+            to(0, self.z + 1, self.has_left)
+
+        @pl.when(k < self.z)
+        def _():
+            to(1, self.z - 1, self.has_right)
+
+    def finish(self, p, acc):
         @pl.when(self.has_left)
         def _():
-            self.arrived(0, p, self.z)
+            acc[...] += self.arrived(0, p, self.z)
 
         @pl.when(self.has_right)
         def _():
-            self.arrived(1, p, self.z)
+            acc[...] += self.arrived(1, p, self.z)
 
         line_first = (p < self.EARLY) & self.decoder
 
         @pl.when(line_first & (lax.rem(p, 2) == 0))
         def _():
-            self.late_sent[p // 2] = self.acc[...].astype(BF)
+            self.late_sent[p // 2] = acc[...].astype(BF)
             self.late_copy(p // 2).start()
 
         @pl.when(line_first & (lax.rem(p, 2) == 1))
         def _():
-            self.late_acc[p // 2] = self.acc[...]
+            self.late_acc[p // 2] = acc[...]
 
         @pl.when(jnp.logical_not(line_first))
         def _():
@@ -445,9 +487,18 @@
             def _():
                 self.final_copy(i).wait()
 
-            slot = self.final_slot(i)
-            slot[...] = self.acc[...]
-            self.final_copy(i).start()
+            first = self.encoder & (i == 0)
+
+            @pl.when(first)
+            def _():
+                self.late_acc[0] = acc[...]
+                pltpu.make_async_copy(self.late_acc.at[0], self.tiles.at[0], self.final_sem.at[0]).start()
+
+            @pl.when(jnp.logical_not(first))
+            def _():
+                slot = self.final_slot(i)
+                slot[...] = acc[...]
+                self.final_copy(i).start()
 
         @pl.when(p + self.WINDOW < self.positions)
         def _():
@@ -580,7 +631,7 @@
         def step(t, carry):
             self.line_step(t)
 
-            @pl.when(t == 5)
+            @pl.when(t == 8)
             def _():
                 self.middle_norms()
 
@@ -590,7 +641,7 @@
 
             return carry
 
-        lax.fori_loop(jnp.where(self.decoder, 4, 2), self.positions + self.line - 1, step, 0)
+        lax.fori_loop(jnp.where(self.decoder, 6, 4), self.positions + self.line - 1, step, 0)
 
     def drain(self):
         @pl.when(self.decoder)
@@ -668,8 +719,8 @@
     sent,
     got,
     half_send,
-    half_own,
     half_got,
+    spare,
     low_out,
     sums,
     load_sem,
@@ -725,7 +776,7 @@
         pl.semaphore_signal(barrier, inc=1, device_id=device, device_id_type=MESH)
     if ring:
         total = GradientShare(
-            ring, section, dp, core, decoder, a_fac, b_fac, first_out, w_up, w_down, held, slope, resid, *share
+            ring, section, dp, core, decoder, a_fac, b_fac, first_out, w_up, w_down, held, slope, resid, spare, *share
         )
         greeted = 2 + total.greet(barrier)
     else:
@@ -904,7 +955,6 @@
             project_out(cross_mixed[rows], w_cross_out, m)
             exchange(1, 1, m).start()
 
-    loop(2, after_attention)
 
     def feed_forward(m):
         rows = rows_of(m)
@@ -935,7 +985,6 @@
         project_out(jnp.concatenate([act[n, rows] for n in range(parts)], 1), w_down, m)
         exchange(2, two, m).start()
 
-    loop(2, feed_forward)
 
     def finish_forward(m):
         exchange(2, two, m).wait()
@@ -956,7 +1005,17 @@
         def _():
             across_copy(seg_out.at[0, m], memory, 0, m).start()
 
-    loop(2, finish_forward)
+    def forward_parts(m):
+        after_attention(m)
+
+        @pl.when(m == 1)
+        def _():
+            finish_forward(0)
+
+        feed_forward(m)
+
+    loop(2, forward_parts)
+    finish_forward(1)
 
     question = dp // QSLOTS
     spot = dp - question * QSLOTS
@@ -1037,11 +1096,13 @@
         half_exchange(0, m).start()
         for n in range(sent.shape[1] // CHUNK):
             cols = slice(n * CHUNK, (n + 1) * CHUNK)
-            half_own[m, :, cols] = dot_nt(memory_part(own), memory_weight(n))
+            spare[n] = dot_nt(memory_part(own), memory_weight(n))
         project_out(d_cross_proj[0, rows], w_cross[0], m)
         exchange(4, 0, m).start()
         half_exchange(0, m).wait()
-        half_send[0, m] = (half_own[m] + half_got[0, m].astype(F32)).astype(BF)
+        for n in range(sent.shape[1] // CHUNK):
+            cols = slice(n * CHUNK, (n + 1) * CHUNK)
+            half_send[0, m, :, cols] = (spare[n] + half_got[0, m, :, cols].astype(F32)).astype(BF)
         across_copy(half_send.at[0, m], d_out, 2, m).start()
 
     def attention_back(m):
@@ -1075,6 +1136,9 @@
         d_mix[rows] = dot_nn(d_attn[rows], w_out[...]).astype(BF)
         attend_backward(proj, d_mix, d_proj, rows, limit)
 
+        if ring:
+            total.middle(m)
+
         def input_part(offset):
             piece = half_of(m, offset)
             return jnp.concatenate([d_proj[t, piece] for t in range(3)], 1)
@@ -1089,7 +1153,7 @@
         half_exchange(1, m).start()
         for n in range(sent.shape[1] // CHUNK):
             cols = slice(n * CHUNK, (n + 1) * CHUNK)
-            half_own[m, :, cols] = dot_nt(input_part(own), input_weight(n))
+            resid[half_of(m, own), cols] += dot_nt(input_part(own), input_weight(n))
 
     @pl.when(decoder)
     def _():
@@ -1111,7 +1175,7 @@
     def finish_backward(m):
         half_exchange(1, m).wait()
         in_grad[0, m] = (
-            resid[half_of(m, own)] + half_own[m] + half_got[1, m].astype(F32)
+            resid[half_of(m, own)] + half_got[1, m].astype(F32)
         ).astype(BF)
 
     loop(2, finish_backward)
@@ -1145,28 +1209,31 @@
 
 
 def unpack_kernel(parts, seg, grads, norms, tiles, norm3, *outs):
-    (seg_out, in_grad, qkv, proj_out, gain1, bias1, up, down, gain2, bias2, cross, cross_out, gain3, bias3, sems) = outs
+    (seg_out, in_grad, qkv, proj_out, gain1, bias1, up, down, gain2, bias2, cross, cross_out, gain3, bias3,
+     rows16, rows32, come, go) = outs
     rows = tiles.shape[1]
     small = rows // 2
-    copies = [(seg, seg_out), (grads, in_grad)]
-    for n in range(parts):
-        cols = slice(n * CHUNK, (n + 1) * CHUNK)
-        copies.append((tiles.at[n], down.at[0, :, cols]))
-        copies.append((tiles.at[parts + n], up.at[0, :, cols]))
-    copies.append((tiles.at[2 * parts], proj_out.at[0]))
-    for t in range(3):
-        copies.append((tiles.at[2 * parts + 1 + t], qkv.at[0, t]))
+    moves = [(seg.at[0], rows16.at[0], seg_out.at[0]), (grads.at[0], rows16.at[1], in_grad.at[0])]
+    whole = [down.at[0, :, n * CHUNK : (n + 1) * CHUNK] for n in range(parts)]
+    whole += [up.at[0, :, n * CHUNK : (n + 1) * CHUNK] for n in range(parts)]
+    whole += [proj_out.at[0]] + [qkv.at[0, t] for t in range(3)]
+    for n, target in enumerate(whole):
+        moves.append((tiles.at[n], rows32.at[n], target))
     for q in range(4):
-        source = tiles.at[2 * parts + 4 + q // 2, pl.ds(q % 2 * small, small)]
-        copies.append((source, cross.at[q] if q < 3 else cross_out))
-    copies = [pltpu.make_async_copy(src, dst, sems.at[i]) for i, (src, dst) in enumerate(copies)]
-    for copy in copies:
+        n, half = 2 * parts + 4 + q // 2, pl.ds(q % 2 * small, small)
+        moves.append((tiles.at[n, half], rows32.at[n, half], cross.at[q] if q < 3 else cross_out))
+    first = [pltpu.make_async_copy(src, mid, come.at[i]) for i, (src, mid, dst) in enumerate(moves)]
+    second = [pltpu.make_async_copy(mid, dst, go.at[i]) for i, (src, mid, dst) in enumerate(moves)]
+    for copy in first:
         copy.start()
     for i, ref in enumerate((gain1, bias1, gain2, bias2)):
         ref[...] = norms[i : i + 1]
     gain3[...] = norm3[4:5, :small]
     bias3[...] = norm3[5:6, :small]
-    for copy in copies:
+    for a, b in zip(first, second):
+        a.wait()
+        b.start()
+    for copy in second:
         copy.wait()
 
 
@@ -1220,7 +1287,6 @@
     share = (
         [
             VM((GradientShare.AHEAD * 4,) + tile, BF),
-            VM(tile, F32),
             VM((9, 8, depth), F32),
             VM((2,) + tile, BF),
             VM((2,) + tile, BF),
@@ -1278,8 +1344,8 @@
             VM((rows, depth), BF),
             VM((2, rows, depth), BF),
             VM((2, micro, half, depth), BF),
-            VM((micro, half, depth), F32),
             VM((2, micro, half, depth), BF),
+            VM((4, half, CHUNK), F32),
             VM((2 * half, depth), BF),
             VM((6, 8, depth), F32),
             pltpu.SemaphoreType.DMA((6,)),
@@ -1336,8 +1402,13 @@
                 small,
             ),
             in_specs=[hbm, hbm, vmem, hbm, vmem],
-            out_specs=(vmem,) * 14,
-            scratch_shapes=[pltpu.SemaphoreType.DMA((2 * parts + 10,))],
+            out_specs=(hbm, hbm, hbm, hbm, vmem, vmem, hbm, hbm, vmem, vmem, hbm, hbm, vmem, vmem),
+            scratch_shapes=[
+                VM((2, micro, half, depth), BF),
+                VM((chunks - 2, lanes, CHUNK), F32),
+                dma((2 * parts + 10,)),
+                dma((2 * parts + 10,)),
+            ],
             name="unpack",
         )(seg_out, in_grad, norms, first, second)
         return outs[:12] + (outs[12][0], outs[13][0])

time: 237 us -> 224 us (0.945)
  Pallas kernels: 236 us -> 223 us
    pallas_call x1, Pallas kernels: 231 us -> 218 us  [body(): pl.pallas_call(functools.partial(layer_kernel, sections, ring), out_shape...]
where the time goes in v5:
time: 224 us
  Pallas kernels  223 us (100%)
    pallas_call x1, Pallas kernels, body(): pl.pallas_call(functools.partial(layer_kernel, sections, ring), out_shape...  218 us
    pallas_call x1, Pallas kernels, body(): pl.pallas_call(functools.partial(unpack_kernel, parts), out_shape=(shape(...  5.35 us

profile of v5, /device:TPU:0, one launch (start us, length us, event | category | flops | bytes accessed | tf_op | source)
XLA Modules:
  0.0 224.2 jit_solution(72890163166892049)
XLA Ops:
  0.7 218.0 %layers.1 = (bf16[1,2,128,1024]{3,2,1,0:T(8,128)(2,1)}, bf16[1,2,128,1024]{3,2,1,0:T(8,128)(2,1)}, f32[8,128]{1,0:T(8,128)}, f32[14,128,512]{2,1,0:T(8,128)}, f32[8,128]{1,0:T(8,128)}) custom-call(bf16[2,128,1024]{2,1,0:T(8,128)(2,1)} %inputs.1, bf16[2,128,1024]{2,1,0:T(8,128)(2,1)} %targets.1, bf16[2,128,1024]{2,1,0:T(8,128)(2,1)} %cotangent.1, ...), custom_call_target="tpu_custom_call" | custom-call | tf_op jit(solution)/shard_map/layers/pallas_call | solution.py:1315
  218.6 5.3 %unpack.1 = (bf16[1,2,128,1024]{3,2,1,0:T(8,128)(2,1)}, bf16[1,2,128,1024]{3,2,1,0:T(8,128)(2,1)}, f32[1,3,128,512]{3,2,1,0:T(8,128)}, f32[1,128,512]{2,1,0:T(8,...) custom-call(bf16[1,2,128,1024]{3,2,1,0:T(8,128)(2,1)} %get-tuple-ele, ...), custom_call_target="tpu_custom_call" | custom-call | tf_op jit(solution)/shard_map/unpack/pallas_call | solution.py:1386

commit v6 on v5

--- a/solution.py
+++ b/solution.py
@@ -123,6 +123,7 @@
     WINDOW = 6
     DEPTH = 4
     FINAL = 8
+    PIECES = 2
     EARLY = 4
 
     def __init__(self, size, section, dp, core, decoder, a_fac, b_fac, tiles, w_up, w_down, held, slope, resid, acc, *share):
@@ -191,13 +192,16 @@
     def line_got(self, place):
         return self.w_up.at[self.tile_rows(place // 4), self.cols(lax.rem(place, 4))]
 
-    def line_copy(self, side, p, k, receiver):
+    def piece(self, h):
+        return pl.ds(h * (self.rows // self.PIECES), self.rows // self.PIECES)
+
+    def line_copy(self, side, p, k, receiver, h):
         place = self.line_place(side, p, k, receiver)
         return self.remote(
-            self.line_slot(p, k),
-            self.line_got(place),
-            self.line_send.at[lax.rem(p, self.DEPTH) * self.line + k],
-            self.line_recv.at[place],
+            self.line_slot(p, k).at[self.piece(h)],
+            self.line_got(place).at[self.piece(h)],
+            self.line_send.at[lax.rem(p, self.DEPTH) * self.line + k, h],
+            self.line_recv.at[place, h],
             self.left if side else self.right,
         )
 
@@ -248,10 +252,12 @@
             for k in range(4):
                 self.branch_copy(k).start()
 
-    def take_factors(self):
+    def pass_factors(self):
         for k in range(4):
             self.branch_copy(k).wait_recv()
         self.branch_forward().start()
+
+    def take_factors(self):
         for m in range(2):
             for n in range(4):
                 self.act_copy(n, m).wait()
@@ -340,24 +346,28 @@
         def _():
             pl.semaphore_signal(self.cross_credit, inc=1, device_id=self.across, device_id_type=MESH)
 
-    def between(self, m):
-        @pl.when(m == 0)
-        def _():
-            loop(2, self.pair_step)
-
-        self.line_step(m)
+    def between(self):
+        loop(2, self.pair_step)
+        self.line_step(0)
 
     def before(self, m):
-        @pl.when(self.encoder & (m == 0))
-        def _():
-            self.take_factors()
-
-        self.line_step(jnp.where(self.decoder, 2, 0) + 2 * m)
+        opening = self.encoder & (m == 0)
+
+        @pl.when(opening)
+        def _():
+            self.pass_factors()
+
         first = jnp.where(self.decoder, 2, 0) + 2 * m
         lax.fori_loop(first, first + 2, lambda j, carry: (self.pair_step(j), carry)[1], 0)
 
+        @pl.when(opening)
+        def _():
+            self.take_factors()
+
+        self.line_step(jnp.where(self.decoder, 1, 0) + 2 * m)
+
     def middle(self, m):
-        self.line_step(jnp.where(self.decoder, 3, 1) + 2 * m)
+        self.line_step(jnp.where(self.decoder, 2, 1) + 2 * m)
 
     def entry(self, t, e):
         last = self.line - 1
@@ -427,29 +437,32 @@
 
         loop(self.line, one)
 
-    def arrived(self, side, p, k):
-        self.line_copy(side, p, k, self.z).wait_recv()
-        return self.line_got(self.line_place(side, p, k, self.z))[...].astype(F32)
+    def arrived(self, side, p, k, h):
+        self.line_copy(side, p, k, self.z, h).wait_recv()
+        return self.line_got(self.line_place(side, p, k, self.z))[self.piece(h)].astype(F32)
 
     def send(self, p, k, acc):
         slot = self.line_slot(p, k)
 
         def to(side, receiver, inner):
-            copy = self.line_copy(side, p, k, receiver)
+            copies = [self.line_copy(side, p, k, receiver, h) for h in range(self.PIECES)]
 
             @pl.when(p >= self.DEPTH)
             def _():
-                copy.wait_send()
+                for copy in copies:
+                    copy.wait_send()
 
             @pl.when(inner)
             def _():
-                slot[...] = (acc[...] + self.arrived(side, p, k)).astype(BF)
+                for h, copy in enumerate(copies):
+                    slot[self.piece(h)] = (acc[self.piece(h)] + self.arrived(side, p, k, h)).astype(BF)
+                    copy.start()
 
             @pl.when(jnp.logical_not(inner))
             def _():
                 slot[...] = acc[...].astype(BF)
-
-            copy.start()
+                for copy in copies:
+                    copy.start()
 
         @pl.when(k > self.z)
         def _():
@@ -462,11 +475,13 @@
     def finish(self, p, acc):
         @pl.when(self.has_left)
         def _():
-            acc[...] += self.arrived(0, p, self.z)
+            for h in range(self.PIECES):
+                acc[self.piece(h)] += self.arrived(0, p, self.z, h)
 
         @pl.when(self.has_right)
         def _():
-            acc[...] += self.arrived(1, p, self.z)
+            for h in range(self.PIECES):
+                acc[self.piece(h)] += self.arrived(1, p, self.z, h)
 
         line_first = (p < self.EARLY) & self.decoder
 
@@ -588,26 +603,28 @@
 
         self.norm_copy(5, 6, self.partner).start()
 
+    def hand_norms(self):
+        nb = self.nb
+        self.norm_copy(5, 6, self.partner).wait()
+
+        @pl.when(self.has_right)
+        def _():
+            self.norm_copy(3, 1, self.right).wait_send()
+
+        @pl.when(self.has_left)
+        def _():
+            self.norm_copy(4, 2, self.left).wait_send()
+
+        nb[7] = nb[5] + nb[6]
+
+        @pl.when(self.decoder)
+        def _():
+            self.norm_copy(7, 8, self.across).start()
+            nb[8] = nb[7]
+
     def finish_norms(self, norm_out, norm3_out):
         nb = self.nb
-        self.norm_copy(5, 6, self.partner).wait()
-
-        @pl.when(self.has_right)
-        def _():
-            self.norm_copy(3, 1, self.right).wait_send()
-
-        @pl.when(self.has_left)
-        def _():
-            self.norm_copy(4, 2, self.left).wait_send()
-
-        nb[7] = nb[5] + nb[6]
         hand = self.norm_copy(7, 8, self.across)
-
-        @pl.when(self.decoder)
-        def _():
-            hand.start()
-            nb[8] = nb[7]
-
         norm_out[...] = nb[7, :, pl.ds(pl.multiple_of(self.dp * 128, 128), 128)]
 
         @pl.when(self.encoder)
@@ -631,17 +648,18 @@
         def step(t, carry):
             self.line_step(t)
 
-            @pl.when(t == 8)
+            @pl.when(t == 6)
             def _():
                 self.middle_norms()
 
-            @pl.when(t == self.positions - 1)
+            @pl.when(t == self.own_chunks + 1)
             def _():
-                self.finish_norms(norm_out, norm3_out)
+                self.hand_norms()
 
             return carry
 
-        lax.fori_loop(jnp.where(self.decoder, 6, 4), self.positions + self.line - 1, step, 0)
+        lax.fori_loop(jnp.where(self.decoder, 5, 4), self.positions + self.line - 1, step, 0)
+        self.finish_norms(norm_out, norm3_out)
 
     def drain(self):
         @pl.when(self.decoder)
@@ -662,7 +680,8 @@
 
                 @pl.when(self.z != k)
                 def _():
-                    self.line_copy(0, slot, k, 0).wait_send()
+                    for h in range(self.PIECES):
+                        self.line_copy(0, slot, k, 0, h).wait_send()
 
         for slot in range(self.FINAL):
             self.final_copy(slot).wait()
@@ -692,11 +711,13 @@
     cross_out_hbm,
     gain3,
     bias3,
-    seg_out,
-    in_grad,
+    seg_hbm,
+    grad_hbm,
     norm_out,
     first_out,
     second_out,
+    seg_out,
+    in_grad,
     w_qkv,
     w_out,
     w_up,
@@ -815,9 +836,15 @@
         for m in range(2):
             mate_rows(src, dst, m, x_sem.at[base + 2 + m], x_sem.at[base + 4 + m]).start()
 
+    def wait_local(src, dst, base, m):
+        local_rows(src, dst, m, x_sem.at[base + m]).wait()
+
+    def wait_mate(src, dst, base, m):
+        mate_rows(src, dst, m, x_sem.at[base + 2 + m], x_sem.at[base + 4 + m]).wait()
+
     def wait_rows(src, dst, base, m):
-        local_rows(src, dst, m, x_sem.at[base + m]).wait()
-        mate_rows(src, dst, m, x_sem.at[base + 2 + m], x_sem.at[base + 4 + m]).wait()
+        wait_local(src, dst, base, m)
+        wait_mate(src, dst, base, m)
 
     @pl.when(encoder)
     def _():
@@ -904,18 +931,35 @@
 
     loads[0].wait()
 
+    def project(m, offset):
+        piece = half_of(m, offset)
+        for t in range(3):
+            proj[t, piece] = dot_nn(layer_in[piece], w_qkv[t]).astype(BF)
+
+    def own_rows(m):
+        @pl.when(encoder)
+        def _():
+            wait_local(inputs, layer_in, 0, m)
+
+        @pl.when(decoder)
+        def _():
+            wait_local(targets, layer_in, 0, m)
+
+        project(m, own)
+
+    loop(2, own_rows)
+
     def attention_in(m):
         @pl.when(encoder)
         def _():
-            wait_rows(inputs, layer_in, 0, m)
+            wait_mate(inputs, layer_in, 0, m)
 
         @pl.when(decoder)
         def _():
-            wait_rows(targets, layer_in, 0, m)
+            wait_mate(targets, layer_in, 0, m)
 
         rows = rows_of(m)
-        for t in range(3):
-            proj[t, rows] = dot_nn(layer_in[rows], w_qkv[t]).astype(BF)
+        project(m, other)
         attend_forward(proj, mixed, rows, limit)
         project_out(mixed[rows], w_out, m)
         exchange(0, 0, m).start()
@@ -1013,9 +1057,6 @@
             finish_forward(0)
 
         feed_forward(m)
-
-    loop(2, forward_parts)
-    finish_forward(1)
 
     question = dp // QSLOTS
     spot = dp - question * QSLOTS
@@ -1058,7 +1099,16 @@
         project_out(jnp.concatenate([d_hidden[n, rows] for n in range(parts)], 1), w_up, m)
         exchange(3, three, m).start()
 
-    loop(2, feed_backward)
+    loop(2, forward_parts)
+
+    @pl.when(decoder)
+    def _():
+        feed_backward(0)
+
+    finish_forward(1)
+    seg_leaves = pltpu.make_async_copy(seg_out, seg_hbm, out_sem.at[2])
+    seg_leaves.start()
+    lax.fori_loop(jnp.where(decoder, 1, 0), 2, lambda m, carry: (feed_backward(m), carry)[1], 0)
     if ring:
         total.begin()
 
@@ -1080,6 +1130,11 @@
 
         strips(norm)
         d_mix[rows] = dot_nn(d_cross[rows], w_cross_out[...]).astype(BF)
+
+        @pl.when(m == 1)
+        def _():
+            memory_leaves(0)
+
         attend_backward(cross_proj, d_mix, d_cross_proj, rows, None)
 
         def memory_part(offset):
@@ -1096,13 +1151,20 @@
         half_exchange(0, m).start()
         for n in range(sent.shape[1] // CHUNK):
             cols = slice(n * CHUNK, (n + 1) * CHUNK)
-            spare[n] = dot_nt(memory_part(own), memory_weight(n))
+            spare[2 * m + n] = dot_nt(memory_part(own), memory_weight(n))
         project_out(d_cross_proj[0, rows], w_cross[0], m)
         exchange(4, 0, m).start()
+        @pl.when(m == 1)
+        def _():
+            memory_leaves(1)
+
+    def memory_leaves(m):
         half_exchange(0, m).wait()
         for n in range(sent.shape[1] // CHUNK):
             cols = slice(n * CHUNK, (n + 1) * CHUNK)
-            half_send[0, m, :, cols] = (spare[n] + half_got[0, m, :, cols].astype(F32)).astype(BF)
+            half_send[0, m, :, cols] = (
+                spare[2 * m + n] + half_got[0, m, :, cols].astype(F32)
+            ).astype(BF)
         across_copy(half_send.at[0, m], d_out, 2, m).start()
 
     def attention_back(m):
@@ -1157,9 +1219,10 @@
 
     @pl.when(decoder)
     def _():
+        if ring:
+            total.between()
+
         def both(m):
-            if ring:
-                total.between(m)
             exchange(3, three, m).wait()
             cross_backward(m)
 
@@ -1179,6 +1242,8 @@
         ).astype(BF)
 
     loop(2, finish_backward)
+    grad_leaves = pltpu.make_async_copy(in_grad, grad_hbm, out_sem.at[3])
+    grad_leaves.start()
 
     @pl.when(encoder)
     def _():
@@ -1193,11 +1258,15 @@
     if ring:
         total.run(sums, norm_out, second_out)
         total.drain()
+        seg_leaves.wait()
+        grad_leaves.wait()
         return
 
     for i in range(6):
         norm_out[i : i + 1] = jnp.sum(sums[i], 0, keepdims=True)
     norm_out[6:8] = jnp.zeros_like(norm_out[6:8])
+    seg_leaves.wait()
+    grad_leaves.wait()
     copies = [
         pltpu.make_async_copy(a_fac, first_out, out_sem.at[0]),
         pltpu.make_async_copy(b_fac, second_out, out_sem.at[1]),
@@ -1293,8 +1362,8 @@
             VM((2,) + tile, F32),
             dma((GradientShare.AHEAD * 4,)),
             dma((GradientShare.AHEAD * 4,)),
-            dma((GradientShare.DEPTH * 4,)),
-            dma((GradientShare.WINDOW * 5,)),
+            dma((GradientShare.DEPTH * 4, GradientShare.PIECES)),
+            dma((GradientShare.WINDOW * 5, GradientShare.PIECES)),
             dma((4,)),
             dma((4,)),
             dma((9,)),
@@ -1320,8 +1389,10 @@
         )
         + results,
         in_specs=[hbm, hbm, hbm, smem, hbm, hbm, vmem, vmem, hbm, hbm, vmem, vmem, hbm, hbm, vmem, vmem],
-        out_specs=(vmem, vmem) + places,
+        out_specs=(hbm, hbm) + places,
         scratch_shapes=[
+            VM((1, micro, half, depth), BF),
+            VM((1, micro, half, depth), BF),
             VM((3, depth, heads), BF),
             VM((depth, heads), BF),
             VM((depth, width), BF),
@@ -1354,7 +1425,7 @@
             pltpu.SemaphoreType.DMA((5, micro)),
             pltpu.SemaphoreType.DMA((6, micro)),
             pltpu.SemaphoreType.DMA((6, micro)),
-            pltpu.SemaphoreType.DMA((2,)),
+            pltpu.SemaphoreType.DMA((4,)),
         ]
         + share,
         compiler_params=pltpu.CompilerParams(

time: 224 us -> 220 us (0.982)
  Pallas kernels: 223 us -> 219 us
    pallas_call x1, Pallas kernels: 218 us -> 213 us  [body(): pl.pallas_call(functools.partial(layer_kernel, sections, ring), out_shape...]
where the time goes in v6:
time: 220 us; the launch traced here: 219 us
  Pallas kernels  219 us (100%)
    pallas_call x1, Pallas kernels, body(): pl.pallas_call(functools.partial(layer_kernel, sections, ring), out_shape...  213 us
    pallas_call x1, Pallas kernels, body(): pl.pallas_call(functools.partial(unpack_kernel, parts), out_shape=(shape(...  5.35 us

profile of v6, /device:TPU:0, one launch (start us, length us, event | category | flops | bytes accessed | tf_op | source)
XLA Modules:
  0.0 219.5 jit_solution(60583995083350019)
XLA Ops:
  0.7 213.3 %layers.1 = (bf16[1,2,128,1024]{3,2,1,0:T(8,128)(2,1)}, bf16[1,2,128,1024]{3,2,1,0:T(8,128)(2,1)}, f32[8,128]{1,0:T(8,128)}, f32[14,128,512]{2,1,0:T(8,128)}, f32[8,128]{1,0:T(8,128)}) custom-call(bf16[2,128,1024]{2,1,0:T(8,128)(2,1)} %inputs.1, bf16[2,128,1024]{2,1,0:T(8,128)(2,1)} %targets.1, bf16[2,128,1024]{2,1,0:T(8,128)(2,1)} %cotangent.1, ...), custom_call_target="tpu_custom_call" | custom-call | tf_op jit(solution)/shard_map/layers/pallas_call | solution.py:1384
  213.9 5.3 %unpack.1 = (bf16[1,2,128,1024]{3,2,1,0:T(8,128)(2,1)}, bf16[1,2,128,1024]{3,2,1,0:T(8,128)(2,1)}, f32[1,3,128,512]{3,2,1,0:T(8,128)}, f32[1,128,512]{2,1,0:T(8,...) custom-call(bf16[1,2,128,1024]{3,2,1,0:T(8,128)(2,1)} %get-tuple-ele, ...), custom_call_target="tpu_custom_call" | custom-call | tf_op jit(solution)/shard_map/unpack/pallas_call | solution.py:1457

commit v7 on v6

--- a/solution.py
+++ b/solution.py
@@ -128,7 +128,7 @@
 
     def __init__(self, size, section, dp, core, decoder, a_fac, b_fac, tiles, w_up, w_down, held, slope, resid, acc, *share):
         self.acc = acc
-        (self.pair_got, self.nb, self.late_sent, self.late_got, self.late_acc, self.pair_send,
+        (self.norm_tile, self.tile_sem, self.pair_got, self.nb, self.late_sent, self.late_got, self.late_acc, self.pair_send,
          self.pair_recv, self.line_send, self.line_recv, self.cross_send, self.cross_recv, self.norm_send,
          self.norm_recv, self.late_send, self.late_recv, self.factor_send, self.factor_recv, self.final_sem,
          self.pair_credit, self.left_credit, self.right_credit, self.cross_credit) = share
@@ -625,7 +625,7 @@
     def finish_norms(self, norm_out, norm3_out):
         nb = self.nb
         hand = self.norm_copy(7, 8, self.across)
-        norm_out[...] = nb[7, :, pl.ds(pl.multiple_of(self.dp * 128, 128), 128)]
+        self.norm_tile[0] = nb[7, :, pl.ds(pl.multiple_of(self.dp * 128, 128), 128)]
 
         @pl.when(self.encoder)
         def _():
@@ -633,11 +633,22 @@
 
         place = self.section * self.line * 2 + self.dp
         block = nb[8, :, pl.ds(pl.multiple_of(place // 2 * 128, 128), 128)]
-        norm3_out[...] = jnp.where(self.y == 0, block, pltpu.roll(block, 64, 1))
+        self.norm_tile[1] = jnp.where(self.y == 0, block, pltpu.roll(block, 64, 1))
+        for copy in self.norm_leaves(norm_out, norm3_out):
+            copy.start()
 
         @pl.when(self.decoder)
         def _():
             hand.wait_send()
+
+    def norm_leaves(self, *outs):
+        return [
+            pltpu.make_async_copy(self.norm_tile.at[e], out, self.tile_sem.at[e]) for e, out in enumerate(outs)
+        ]
+
+    def norms_left(self, *outs):
+        for copy in self.norm_leaves(*outs):
+            copy.wait()
 
     def run(self, sums, norm_out, norm3_out):
         self.start_norms(sums)
@@ -698,24 +709,31 @@
     inputs,
     targets,
     cotangent,
-    counts,
+    counts_hbm,
     qkv_hbm,
     out_hbm,
-    gain1,
-    bias1,
+    gain1_hbm,
+    bias1_hbm,
     up_hbm,
     down_hbm,
-    gain2,
-    bias2,
+    gain2_hbm,
+    bias2_hbm,
     cross_hbm,
     cross_out_hbm,
-    gain3,
-    bias3,
+    gain3_hbm,
+    bias3_hbm,
     seg_hbm,
     grad_hbm,
     norm_out,
     first_out,
     second_out,
+    gain1,
+    bias1,
+    gain2,
+    bias2,
+    gain3,
+    bias3,
+    counts,
     seg_out,
     in_grad,
     w_qkv,
@@ -813,6 +831,13 @@
                 (down_hbm.at[0], w_down),
                 (cross_hbm, w_cross),
                 (cross_out_hbm, w_cross_out),
+                (gain1_hbm, gain1),
+                (bias1_hbm, bias1),
+                (gain2_hbm, gain2),
+                (bias2_hbm, bias2),
+                (gain3_hbm, gain3),
+                (bias3_hbm, bias3),
+                (counts_hbm, counts),
             )
         )
     ]
@@ -1258,6 +1283,7 @@
     if ring:
         total.run(sums, norm_out, second_out)
         total.drain()
+        total.norms_left(norm_out, second_out)
         seg_leaves.wait()
         grad_leaves.wait()
         return
@@ -1279,7 +1305,8 @@
 
 def unpack_kernel(parts, seg, grads, norms, tiles, norm3, *outs):
     (seg_out, in_grad, qkv, proj_out, gain1, bias1, up, down, gain2, bias2, cross, cross_out, gain3, bias3,
-     rows16, rows32, come, go) = outs
+     rows16, rows32, small_in, *rest) = outs
+    small_out, (come, go) = rest[:6], rest[6:]
     rows = tiles.shape[1]
     small = rows // 2
     moves = [(seg.at[0], rows16.at[0], seg_out.at[0]), (grads.at[0], rows16.at[1], in_grad.at[0])]
@@ -1291,14 +1318,18 @@
     for q in range(4):
         n, half = 2 * parts + 4 + q // 2, pl.ds(q % 2 * small, small)
         moves.append((tiles.at[n, half], rows32.at[n, half], cross.at[q] if q < 3 else cross_out))
+    tiny = [pltpu.make_async_copy(src, small_in.at[i], come.at[len(moves) + i]) for i, src in enumerate((norms, norm3))]
     first = [pltpu.make_async_copy(src, mid, come.at[i]) for i, (src, mid, dst) in enumerate(moves)]
     second = [pltpu.make_async_copy(mid, dst, go.at[i]) for i, (src, mid, dst) in enumerate(moves)]
-    for copy in first:
+    for copy in tiny + first:
         copy.start()
-    for i, ref in enumerate((gain1, bias1, gain2, bias2)):
-        ref[...] = norms[i : i + 1]
-    gain3[...] = norm3[4:5, :small]
-    bias3[...] = norm3[5:6, :small]
+    for copy in tiny:
+        copy.wait()
+    values = [small_in[0, i : i + 1] for i in range(4)] + [small_in[1, i : i + 1, :small] for i in (4, 5)]
+    for i, (value, ref, dst) in enumerate(zip(values, small_out, (gain1, bias1, gain2, bias2, gain3, bias3))):
+        ref[...] = value
+        second.append(pltpu.make_async_copy(ref, dst, go.at[len(moves) + i]))
+        second[-1].start()
     for a, b in zip(first, second):
         a.wait()
         b.start()
@@ -1334,7 +1365,6 @@
     chunks = 2 * parts + 8
     hbm = pl.BlockSpec(memory_space=pl.ANY)
     vmem = pl.BlockSpec(memory_space=VM)
-    smem = pl.BlockSpec(memory_space=pltpu.SMEM)
     shape = jax.ShapeDtypeStruct
     if ring:
         results = (
@@ -1342,7 +1372,7 @@
             shape((chunks - 2, depth // ring, CHUNK), F32),
             shape((8, depth // ring), F32),
         )
-        places = (vmem, hbm, vmem)
+        places = (hbm, hbm, hbm)
     else:
         results = (
             shape((8, depth), F32),
@@ -1355,6 +1385,8 @@
     tile = (depth // ring, CHUNK) if ring else None
     share = (
         [
+            VM((2, 8, depth // ring), F32),
+            dma((2,)),
             VM((GradientShare.AHEAD * 4,) + tile, BF),
             VM((9, 8, depth), F32),
             VM((2,) + tile, BF),
@@ -1388,9 +1420,11 @@
             shape((1, micro, half, depth), BF),
         )
         + results,
-        in_specs=[hbm, hbm, hbm, smem, hbm, hbm, vmem, vmem, hbm, hbm, vmem, vmem, hbm, hbm, vmem, vmem],
+        in_specs=[hbm] * 16,
         out_specs=(hbm, hbm) + places,
-        scratch_shapes=[
+        scratch_shapes=[VM((1, depth), F32)] * 6
+        + [
+            pltpu.SMEM(slot_counts.shape, jnp.int32),
             VM((1, micro, half, depth), BF),
             VM((1, micro, half, depth), BF),
             VM((3, depth, heads), BF),
@@ -1419,7 +1453,7 @@
             VM((4, half, CHUNK), F32),
             VM((2 * half, depth), BF),
             VM((6, 8, depth), F32),
-            pltpu.SemaphoreType.DMA((6,)),
+            pltpu.SemaphoreType.DMA((13,)),
             pltpu.SemaphoreType.DMA((12,)),
             pltpu.SemaphoreType.DMA((5, micro)),
             pltpu.SemaphoreType.DMA((5, micro)),
@@ -1472,13 +1506,20 @@
                 small,
                 small,
             ),
-            in_specs=[hbm, hbm, vmem, hbm, vmem],
-            out_specs=(hbm, hbm, hbm, hbm, vmem, vmem, hbm, hbm, vmem, vmem, hbm, hbm, vmem, vmem),
+            in_specs=[hbm] * 5,
+            out_specs=(hbm,) * 14,
             scratch_shapes=[
                 VM((2, micro, half, depth), BF),
                 VM((chunks - 2, lanes, CHUNK), F32),
-                dma((2 * parts + 10,)),
-                dma((2 * parts + 10,)),
+                VM((2, 8, lanes), F32),
+                VM((1, lanes), F32),
+                VM((1, lanes), F32),
+                VM((1, lanes), F32),
+                VM((1, lanes), F32),
+                VM((1, lanes // 2), F32),
+                VM((1, lanes // 2), F32),
+                dma((2 * parts + 12,)),
+                dma((2 * parts + 16,)),
             ],
             name="unpack",
         )(seg_out, in_grad, norms, first, second)

time: 220 us -> 218 us (level)
  no operation moved by 1% of the time
where the time goes in v7:
time: 218 us
  Pallas kernels  217 us (100%)
    pallas_call x1, Pallas kernels, body(): pl.pallas_call(functools.partial(layer_kernel, sections, ring), out_shape...  212 us

profile of v7, /device:TPU:0, one launch (start us, length us, event | category | flops | bytes accessed | tf_op | source)
XLA Modules:
  0.0 217.5 jit_solution(18167459091739180732)
XLA Ops:
  0.7 212.4 %layers.1 = (bf16[1,2,128,1024]{3,2,1,0:T(8,128)(2,1)}, bf16[1,2,128,1024]{3,2,1,0:T(8,128)(2,1)}, f32[8,128]{1,0:T(8,128)}, f32[14,128,512]{2,1,0:T(8,128)}, f32[8,128]{1,0:T(8,128)}) custom-call(bf16[2,128,1024]{2,1,0:T(8,128)(2,1)} %inputs.1, bf16[2,128,1024]{2,1,0:T(8,128)(2,1)} %targets.1, bf16[2,128,1024]{2,1,0:T(8,128)(2,1)} %cotangent.1, ...), custom_call_target="tpu_custom_call" | custom-call | tf_op jit(solution)/shard_map/layers/pallas_call | solution.py:1416
  213.1 4.3 %unpack.1 = (bf16[1,2,128,1024]{3,2,1,0:T(8,128)(2,1)}, bf16[1,2,128,1024]{3,2,1,0:T(8,128)(2,1)}, f32[1,3,128,512]{3,2,1,0:T(8,128)}, f32[1,128,512]{2,1,0:T(8,...) custom-call(bf16[1,2,128,1024]{3,2,1,0:T(8,128)(2,1)} %get-tuple-ele, ...), custom_call_target="tpu_custom_call" | custom-call | tf_op jit(solution)/shard_map/unpack/pallas_call | solution.py:1491
